TPU v7x, 128 devices: a whole 4x4x4 slice. The times are simulated.
128 devices in a mesh: blk: 8 (over x_hi, z), dp: 16 (over x_lo, y, core).
Axes of the slice: x: 4 (x_hi: 2, x_lo: 2; x = x_hi * 2 + x_lo), y: 4, z: 4, core: 2. Of those that a mesh axis runs over, the one named last changes fastest.
Arguments:
- queries: bfloat16 [16384, 3072], P(('blk', 'dp')), may hold values from -10.5 to 10.5
- positives: bfloat16 [16384, 3072], P(('blk', 'dp')), may hold values from -7 to 7
- corpus: bfloat16 [65536, 3072], P(('blk', 'dp')), may hold values from -6 to 6
- hard_ids: int32 [128, 12], P(('blk', 'dp')), may hold values from 0 to 511, as said below
Outputs:
- grad_queries: float32 [16384, 3072], P(('blk', 'dp'))
- grad_positives: float32 [16384, 3072], P(('blk', 'dp'))
- grad_corpus: float32 [65536, 3072], P(('blk', 'dp'))
- losses: float32 [16384], P(('blk', 'dp'))
Inputs may be any that keep to these rules, and one draw needn't show every extreme that they name: `hard_ids`: the 12 ids of query block c name corpus blocks of 12 different device blocks that share the loop index of c: block h belongs to device block h // 4, whose loop index is h // 64.
All inputs are finite; a program needn't handle non-finite values.
Results may differ from a plain program's by a relative error of at most 0.0095.
Values may be sent and summed in bfloat16 or wider, within the bound.
No kernel may reach another device: no remote copies, remote signals or barrier semaphores. Data moves between devices by JAX's collectives and lax.ppermute only.
A program may use at most 192 MiB of HBM per device.

v0:
```python
import math

import jax
import jax.numpy as jnp
from jax import lax
from jax.experimental import pallas as pl
from jax.experimental.pallas import tpu as pltpu
from jax.sharding import PartitionSpec as P

BLOCK = 128
SCALE = 3.0
OUT_SCALE = 0.25
LOW = -1e30
CHUNK = 512
WIDE = 1024
AXES = ("blk", "dp")
F32 = jnp.float32
BF16 = jnp.bfloat16


def routes(move):
    pairs = []
    for i in range(128):
        b, d = i // 16, i % 16
        h, z, l, y, c = move(b // 4, b % 4, d // 8, (d // 2) % 4, d % 2)
        pairs.append((i, ((h % 2) * 4 + z % 4) * 16 + (l % 2) * 8 + (y % 4) * 2 + c % 2))
    return pairs


def way(c):
    return 1 - 2 * c


Y_FWD = routes(lambda h, z, l, y, c: (h, z, l, y + way(c), c))
Y_BWD = routes(lambda h, z, l, y, c: (h, z, l, y - way(c), c))
Z_FWD = routes(lambda h, z, l, y, c: (h, z + way(c), l, y, c))
Z_BWD = routes(lambda h, z, l, y, c: (h, z - way(c), l, y, c))
X_LO = routes(lambda h, z, l, y, c: (h, z, l + 1, y, c))
X_HI = routes(lambda h, z, l, y, c: (h + 1, z, l, y, c))
CORE = routes(lambda h, z, l, y, c: (h, z, l, y, c + 1))
Y_TWO = routes(lambda h, z, l, y, c: (h, z, l, y + 2, c))

SPOTS = [(dx, dr) for dx in range(2) for dr in range(4)]


def send(value, route):
    return lax.ppermute(value, AXES, route)


def after(value, *others):
    return lax.optimization_barrier((value, *others))[0]


def cat(*values):
    return jnp.concatenate(values, axis=0)


def rows_dot(left, right):
    return lax.dot_general(left, right, (((1,), (1,)), ((), ())), preferred_element_type=F32)


def mm(left, right):
    return jnp.dot(left, right, preferred_element_type=F32)


def near(value, *others):
    total = value.astype(F32)
    for other in others:
        total = total + other.astype(F32)
    return total


def column(array, chunk):
    if array.ndim == 2:
        return pl.BlockSpec((array.shape[0], chunk), lambda i, s: (0, i))
    return pl.BlockSpec((array.shape[0], array.shape[1], chunk), lambda i, s: (0, 0, i))


def kernel(body, slots, arrays, specs, out, out_spec, steps, scratch=()):
    return pl.pallas_call(
        body,
        grid_spec=pltpu.PrefetchScalarGridSpec(
            num_scalar_prefetch=1, grid=(steps,), in_specs=specs, out_specs=out_spec, scratch_shapes=scratch
        ),
        out_shape=out,
        compiler_params=pltpu.CompilerParams(vmem_limit_bytes=13 * 1024 * 1024),
        cost_estimate=pl.CostEstimate(flops=1024, bytes_accessed=1024, transcendentals=0),
    )(slots, *arrays)


def chosen(spot, w):
    return pl.BlockSpec((1, BLOCK, WIDE), lambda i, s: (jnp.maximum(s[2 * spot + w], 0), 0, i))


def whole(array):
    return pl.BlockSpec(array.shape, lambda i, s: (0,) * array.ndim)


def hard_scores(asked, tables, blocks, spots, mult):
    width = blocks[0].shape[1]
    count, steps = len(spots), width // WIDE

    def body(asked_ref, *refs):
        out, stats = refs[-2:]
        step = pl.program_id(0)

        @pl.when(step == 0)
        def _():
            out[...] = jnp.zeros_like(out)

        for n in range(count):
            query = refs[3 * n][...]
            for w in range(2):
                out[n, w] = out[n, w] + rows_dot(refs[3 * n + 1 + w][0], query)

        @pl.when(step == steps - 1)
        def _():
            for n, spot in enumerate(spots):
                scores = []
                for w in range(2):
                    score = jnp.where(asked_ref[2 * spot + w] >= 0, out[n, w] * mult, LOW)
                    out[n, w] = score
                    scores.append(score)
                peak = jnp.max(jnp.maximum(*scores), axis=0, keepdims=True)
                some = [jnp.where(score > 0.5 * LOW, jnp.exp(score - peak), 0.0) for score in scores]
                stats[n, 0:1] = peak
                stats[n, 1:2] = jnp.sum(some[0] + some[1], axis=0, keepdims=True)

    arrays, specs = [], []
    for block, spot in zip(blocks, spots):
        arrays += [block, *tables]
        specs += [column(block, WIDE), chosen(spot, 0), chosen(spot, 1)]
    outs = [jax.ShapeDtypeStruct((count, 2, BLOCK, BLOCK), F32), jax.ShapeDtypeStruct((count, 2, BLOCK), F32)]
    return kernel(body, asked, arrays, specs, outs, [whole(o) for o in outs], steps)


def hard_parts(asked, scores, norm, tables, plan, loop=()):
    width = tables[0].shape[2]
    count = len(plan)
    extra = [a for _, adds, _ in plan for a in adds]

    def body(asked_ref, norm_ref, *refs):
        mine, outs, held = refs[: 3 * count], refs[-count - 1 : -1], refs[-1]
        more = list(refs[3 * count : -count - 1])

        @pl.when(pl.program_id(0) == 0)
        def _():
            for n, (spot, _, _) in enumerate(plan):
                for w in range(2):
                    weight = jnp.exp(mine[3 * n][0, w] - norm_ref[spot : spot + 1, :])
                    held[n, :, w * BLOCK : (w + 1) * BLOCK] = weight.T.astype(BF16)

        for n, (_, adds, dtype) in enumerate(plan):
            keys = jnp.concatenate([mine[3 * n + 1][0], mine[3 * n + 2][0]], axis=0)
            total = mm(held[n], keys)
            for _ in adds:
                total = total + more.pop(0)[...].astype(F32)
            if n == 0 and loop:
                for m in range(len(loop) - 1):
                    total = total + mm(more[0][:, m * BLOCK : (m + 1) * BLOCK], more[m + 1][...])
            outs[n][...] = total.astype(dtype)

    arrays, specs = [], []
    for spot, _, _ in plan:
        array, n = scores[spot]
        arrays += [array, *tables]
        specs += [
            pl.BlockSpec((1, 2, BLOCK, BLOCK), lambda i, s, n=n: (n, 0, 0, 0)), chosen(spot, 0), chosen(spot, 1),
        ]
    arrays += extra + list(loop)
    specs += [column(a, WIDE) for a in extra] + [whole(a) for a in loop[:1]] + [column(a, WIDE) for a in loop[1:]]
    outs = [jax.ShapeDtypeStruct((BLOCK, width), dtype) for _, _, dtype in plan]
    return kernel(
        body, asked, (norm, *arrays), [whole(norm)] + specs, outs, [column(o, WIDE) for o in outs], width // WIDE,
        (pltpu.VMEM((count, BLOCK, 2 * BLOCK), BF16),),
    )


def corpus_part(asked, scores, norm, blocks, held, dtype, w, start=None):
    width = blocks[0].shape[1]
    count = len(blocks)
    arrays = []
    for array, _ in scores:
        if not any(array is a for a in arrays):
            arrays.append(array)
    place = [([array is a for a in arrays].index(True), n) for array, n in scores]

    def body(asked_ref, norm_ref, *refs):
        out, total, weights = refs[-3:]
        found, rest = refs[: len(arrays)], refs[len(arrays) :]

        @pl.when(pl.program_id(0) == 0)
        def _():
            for j, (k, n) in enumerate(place):
                weights[j] = jnp.exp(found[k][n, w] - norm_ref[j : j + 1, :]).astype(BF16)

        total[...] = jnp.zeros_like(total) if start is None else rest[count][...].astype(F32)
        for j in range(count):
            h = jnp.maximum(asked_ref[2 * j + w], 0)
            total[h] = total[h] + mm(weights[j], rest[j][...])
        out[...] = (total[...] * (1 if start is None else OUT_SCALE)).astype(dtype)

    more = () if start is None else (start,)
    out = jax.ShapeDtypeStruct((held, BLOCK, width), dtype)
    return kernel(
        body, asked, (norm, *arrays, *blocks, *more),
        [whole(a) for a in (norm, *arrays)] + [column(a, CHUNK) for a in (*blocks, *more)],
        out, column(out, CHUNK), width // CHUNK,
        (pltpu.VMEM((held, BLOCK, CHUNK), F32), pltpu.VMEM((count, BLOCK, BLOCK), BF16)),
    )


def local(queries, positives, corpus, hard_ids):
    rows, width = queries.shape
    held = corpus.shape[0] // BLOCK
    mult = SCALE / math.sqrt(width)
    me = lax.axis_index("dp")
    mx, my, mc = me // 8, (me // 2) % 4, me % 2
    turn = 1 - 2 * mc

    q, p = {(0, 0): queries}, {(0, 0): positives}
    other = send(corpus, CORE)
    q[1, 0] = send(queries, X_LO)
    q[0, 3], q[0, 1] = send(queries, Y_FWD), send(queries, Y_BWD)
    p[0, 3] = send(positives, Z_FWD)

    p[1, 0] = send(after(positives, q[1, 0], other), X_HI)
    q[1, 3] = send(after(q[1, 0], q[0, 3], other), Y_FWD)
    q[1, 1] = send(after(q[1, 0], q[0, 1], other), Y_BWD)
    p[0, 2] = send(after(p[0, 3], other), Z_FWD)
    p[0, 1] = send(after(positives, p[0, 3]), Z_BWD)

    q[0, 2] = send(after(q[0, 3], q[1, 3]), Y_FWD)
    q[1, 2] = send(q[1, 1], Y_BWD)
    p[1, 3], p[1, 1] = send(p[1, 0], Z_FWD), send(after(p[1, 0], p[0, 1]), Z_BWD)
    p[1, 2] = send(after(p[0, 2], p[1, 0]), X_HI)

    owner = hard_ids[0] // held % 16
    matches = owner[:, None] == jnp.arange(16, dtype=jnp.int32)[None, :]
    wanted = jnp.sum(jnp.where(matches, (hard_ids[0] % held)[:, None] + 1, 0), axis=0) - 1
    pairs = jnp.repeat(wanted.reshape(8, 1, 2), 2, axis=1).reshape(16, 2)
    asked = lax.all_to_all(after(pairs, q[1, 3]), "dp", split_axis=0, concat_axis=0, tiled=True)
    spot_place = jnp.stack([((mx + a) % 2) * 4 + (my + turn * b) % 4 for a, b in SPOTS])
    asked = jnp.take(asked.reshape(8, 2, 2), spot_place, axis=0)
    asked = lax.dynamic_index_in_dim(asked, mc, 1, keepdims=False)
    asked = jnp.where(mc == 0, asked, asked[:, ::-1])
    asked = after(jnp.clip(asked.reshape(16), -1, held - 1), p[1, 1])

    tables = (corpus.reshape(held, BLOCK, width), other.reshape(held, BLOCK, width))
    scores, stats = {}, {}
    for group in ([(0, 0), (1, 0), (0, 3), (0, 1), (1, 3), (1, 1)], [(0, 2), (1, 2)]):
        spots = [SPOTS.index(o) for o in group]
        out, stat = hard_scores(asked, tables, [q[o] for o in group], spots, mult)
        for n, j in enumerate(spots):
            scores[j], stats[j] = (out, n), stat[n]
    inner = cat(*[rows_dot(p[o], queries) for o in SPOTS]) * mult
    peak = jnp.max(inner, axis=0)
    total = jnp.sum(jnp.exp(inner - peak[None]), axis=0)
    row = lax.broadcasted_iota(jnp.int32, inner.shape, 0)
    col = lax.broadcasted_iota(jnp.int32, inner.shape, 1)
    diag = row == col
    own_score = jnp.sum(jnp.where(diag, inner, 0.0), axis=0)

    def merge(one, two):
        m = jnp.maximum(one[:, 0], two[:, 0])
        s = one[:, 1] * jnp.exp(one[:, 0] - m) + two[:, 1] * jnp.exp(two[:, 0] - m)
        return jnp.stack([m, s], axis=1)

    state = jnp.stack([stats[j] for j in range(8)])
    state = cat(merge(state[:1], jnp.stack([peak, total])[None]), state[1:])
    for route, turns in ((X_LO, (1, 0)), (Y_BWD, (0, 1)), (Y_TWO, (0, 2))):
        peer = send(state, route).reshape(2, 4, 2, BLOCK)
        state = merge(state, jnp.roll(peer, turns, axis=(0, 1)).reshape(8, 2, BLOCK))
    norm = state[:, 0] + jnp.log(state[:, 1])
    inner_w = (jnp.exp(inner - norm[:1]) - diag.astype(F32)).astype(BF16)
    losses = norm[0] - own_score

    def y_parts(wait, *plan, loop=()):
        return hard_parts(
            asked, scores, after(norm, *wait), tables, [(SPOTS.index(o), adds, dtype) for o, adds, dtype in plan], loop
        )

    def z_part(o, weights, *adds):
        j = SPOTS.index(o)
        return near(mm(weights[j * BLOCK : (j + 1) * BLOCK], queries), *adds).astype(BF16)

    y02, y12 = y_parts((), ((0, 2), (), BF16), ((1, 2), (), BF16))
    y02, y12 = send(y02, Y_FWD), send(y12, Y_BWD)
    z12 = send(z_part((1, 2), inner_w), X_HI)
    z11 = send(z_part((1, 1), inner_w), Z_FWD)
    z13 = send(z_part((1, 3), inner_w), Z_BWD)

    q_blocks = [q[o] for o in SPOTS]
    in_order = [scores[j] for j in range(8)]
    theirs = corpus_part(asked, in_order, norm, q_blocks, held, BF16, 1)
    inner_2 = after(inner_w, z12, z11, z13)
    y11, y13 = y_parts((y02, y12), ((1, 1), (), BF16), ((1, 3), (y12,), BF16))
    y11, y13 = send(y11, Y_FWD), send(y13, Y_BWD)
    z02 = send(z_part((0, 2), inner_2, z12), Z_FWD)
    z10 = send(z_part((1, 0), inner_2, z11, z13), X_HI)
    theirs = send(after(theirs, y02, y12, z12, z11, z13), CORE)

    inner_3 = after(inner_2, z02, z10)
    y10, y01, y03 = y_parts(
        (y11, y13, theirs), ((1, 0), (y11, y13), BF16), ((0, 1), (y02,), BF16), ((0, 3), (), BF16)
    )
    done = after(norm, y10)
    y10 = send(y10, X_LO)
    y01, y03 = send(y01, Y_FWD), send(y03, Y_BWD)
    z01 = send(z_part((0, 1), inner_3, z02), Z_FWD)
    z03 = send(z_part((0, 3), inner_3), Z_BWD)
    loop = (jnp.swapaxes(inner_3, 0, 1), *[p[o] for o in SPOTS])
    (mine,) = y_parts((done,), ((0, 0), (), F32), loop=loop)
    grad_corpus = corpus_part(asked, in_order, done, q_blocks, held, F32, 0, theirs)
    mine, first, grad_corpus = lax.optimization_barrier((mine, mm(inner_3[:BLOCK], queries), grad_corpus))
    grad_queries = OUT_SCALE * near(mine, y01, y03, y10)
    grad_positives = OUT_SCALE * near(first, z01, z03, z10)
    return grad_queries, grad_positives, grad_corpus.reshape(held * BLOCK, width), losses


def solution(mesh):
    spec = P(AXES, None)
    return jax.shard_map(
        local,
        mesh=mesh,
        in_specs=(spec,) * 4,
        out_specs=(spec, spec, spec, P(AXES)),
        check_vma=False,
    )
```

profile of v0, /device:TPU:1, one launch (start us, length us, event | category | flops | bytes accessed | tf_op | source)
XLA Modules:
  0.0 188.5 jit_solution(13601363654430165681)
XLA Ops:
  0.6 1.5 collective-permute-start.2
  2.1 3.8 %collective-permute-start.5 = (bf16[128,3072]{1,0:T(8,128)(2,1)}, bf16[128,3072]{1,0:T(8,128)(2,1)}, u32[]{:S(2)}, u32[]{:S(2)}) collective-permute-start(bf16[128,3072]{1,0:T(8,128)(2,1)} %refs_4_.1), channel_id=1, source_target_pairs={{0,16},{1,49},{2,18},{3,51},{4,20},{5,53},{6,22},{7,55},{8,24},{9,... | collective-permute-start | bytes 2359304 | tf_op jit(solution)/shard_map/ppermute | solution.py:47
  6.0 1.2 collective-permute-start
  7.2 2.7 %collective-permute-start.1 = (bf16[128,3072]{1,0:T(8,128)(2,1)}, bf16[128,3072]{1,0:T(8,128)(2,1)}, u32[]{:S(2)}, u32[]{:S(2)}) collective-permute-start(bf16[128,3072]{1,0:T(8,128)(2,1)} %refs_2_.3), channel_id=1, source_target_pairs={{0,2},{1,7},{2,4},{3,1},{4,6},{5,3},{6,0},{7,5},{8,10},{9,15},{10,... | collective-permute-start | bytes 2359304 | tf_op jit(solution)/shard_map/ppermute | solution.py:47
  10.0 0.7 and_select_fusion.1
  10.8 4.4 %collective-permute-done.5.refs_7_ = bf16[128,3072]{1,0:T(8,128)(2,1)} collective-permute-done((bf16[128,3072]{1,0:T(8,128)(2,1)}, bf16[128,3072]{1,0:T(8,128)(2,1)}, u32[]{:S(2)}, u32[]{:S(2)}) %collective-permute-start.5) | collective-permute-done | bytes 786464 | tf_op jit(solution)/shard_map/ppermute | solution.py:47
  15.5 9.1 %collective-permute-done.refs_3_.refs_6_ = bf16[128,3072]{1,0:T(8,128)(2,1)} collective-permute-done((bf16[128,3072]{1,0:T(8,128)(2,1)}, bf16[128,3072]{1,0:T(8,128)(2,1)}, u32[]{:S(2)}, u32[]{:S(2)}) %collective-permute-start) | collective-permute-done | bytes 786464 | tf_op jit(solution)/shard_map/ppermute | solution.py:47
  24.6 2.2 %collective-permute-done.1.refs_6_.refs_5_ = bf16[128,3072]{1,0:T(8,128)(2,1)} collective-permute-done((bf16[128,3072]{1,0:T(8,128)(2,1)}, bf16[128,3072]{1,0:T(8,128)(2,1)}, u32[]{:S(2)}, u32[]{:S(2)}) %collective-permute-start.1) | collective-permute-done | bytes 786464 | tf_op jit(solution)/shard_map/ppermute | solution.py:47
  26.8 3.1 %collective-permute-start.3 = (bf16[128,3072]{1,0:T(8,128)(2,1)}, bf16[128,3072]{1,0:T(8,128)(2,1)}, u32[]{:S(2)}, u32[]{:S(2)}) collective-permute-start(bf16[128,3072]{1,0:T(8,128)(2,1)} %collective-permute-done.refs_3_.refs_6_), channel_id=1, source_target_pairs={{0,2},{1,7},{2,4},{3,1},{4,6},{5,3},{6,0},{7,5},{8,10},{9,15},{10,... | collective-permute-start | bytes 2359304 | tf_op jit(solution)/shard_map/ppermute | solution.py:47
  29.9 2.5 %collective-permute-start.4 = (bf16[128,3072]{1,0:T(8,128)(2,1)}, bf16[128,3072]{1,0:T(8,128)(2,1)}, u32[]{:S(2)}, u32[]{:S(2)}) collective-permute-start(bf16[128,3072]{1,0:T(8,128)(2,1)} %refs_4_.1), channel_id=1, source_target_pairs={{0,64},{1,65},{2,66},{3,67},{4,68},{5,69},{6,70},{7,71},{8,72},{9,... | collective-permute-start | bytes 2359304 | tf_op jit(solution)/shard_map/ppermute | solution.py:47
  33.0 2.4 %convolution_dynamic-update-slice_fusion.7 = f32[1024,128]{0,1:T(8,128)} fusion(bf16[128,3072]{1,0:T(8,128)(2,1)} %refs_4_.1, bf16[128,3072]{1,0:T(8,128)(2,1)} %refs_2_.3), kind=kOutput, calls=%fused_computation.21 | convolution fusion | flops 100663296 | bytes 1638400 | tf_op jit(solution)/shard_map/dot_general | solution.py:59
  35.5 2.1 %convolution_dynamic-update-slice_fusion.6 = f32[1024,128]{0,1:T(8,128)} fusion(f32[1024,128]{0,1:T(8,128)} %convolution_dynamic-update-slice_fusion.7, bf16[128,3072]{1,0:T(8,128)(2,1)} %collective-permute-done.6.refs_5_, bf16[128,3072]{1,0:T(8,128)(2,1)S(1)} %copy-done.4), kind=kOutput, calls=%fused_computation.20 | convolution fusion | flops 100663296 | bytes 1638400 | tf_op jit(solution)/shard_map/dot_general | solution.py:59
  37.6 1.6 collective-permute-done.3.refs_12_.refs_9_
  39.2 0.7 copy.75
  39.9 5.1 %all-to-all-start = ((s32[16,1,2]{2,1,0:T(1,128)}), s32[16,1,2]{2,1,0:T(1,128)S(1)}, u32[]{:S(2)}, u32[]{:S(2)}) async-start(s32[16,1,2]{2,1,0:T(1,128)} %copy.75), calls=%async_computation | async-start | bytes 16384 | tf_op jit(solution)/shard_map/all_to_all | solution.py:242
  45.0 2.5 %collective-permute-done.4.refs_8_ = bf16[128,3072]{1,0:T(8,128)(2,1)} collective-permute-done((bf16[128,3072]{1,0:T(8,128)(2,1)}, bf16[128,3072]{1,0:T(8,128)(2,1)}, u32[]{:S(2)}, u32[]{:S(2)}) %collective-permute-start.4) | collective-permute-done | bytes 786464 | tf_op jit(solution)/shard_map/ppermute | solution.py:47
  47.4 3.0 %collective-permute-start.11 = (bf16[128,3072]{1,0:T(8,128)(2,1)}, bf16[128,3072]{1,0:T(8,128)(2,1)}, u32[]{:S(2)}, u32[]{:S(2)}) collective-permute-start(bf16[128,3072]{1,0:T(8,128)(2,1)} %collective-permute-done.10.refs_6_), channel_id=1, source_target_pairs={{0,64},{1,65},{2,66},{3,67},{4,68},{5,69},{6,70},{7,71},{8,72},{9,... | collective-permute-start | bytes 2359304 | tf_op jit(solution)/shard_map/ppermute | solution.py:47
  50.5 2.6 %collective-permute-start.13 = (bf16[128,3072]{1,0:T(8,128)(2,1)}, bf16[128,3072]{1,0:T(8,128)(2,1)}, u32[]{:S(2)}, u32[]{:S(2)}) collective-permute-start(bf16[128,3072]{1,0:T(8,128)(2,1)} %collective-permute-done.1.refs_6_.refs_5_), channel_id=1, source_target_pairs={{0,2},{1,7},{2,4},{3,1},{4,6},{5,3},{6,0},{7,5},{8,10},{9,15},{10,... | collective-permute-start | bytes 2359304 | tf_op jit(solution)/shard_map/ppermute | solution.py:47
  53.1 1.7 collective-permute-start.12
  54.8 2.4 %convolution_dynamic-update-slice_fusion.5 = f32[1024,128]{0,1:T(8,128)} fusion(f32[1024,128]{0,1:T(8,128)} %convolution_dynamic-update-slice_fusion.6, bf16[128,3072]{1,0:T(8,128)(2,1)} %collective-permute-done.10.refs_6_, bf16[128,3072]{1,0:T(8,128)(2,1)} %refs_2_.3), kind=kOutput, calls=%fused_computation.19 | convolution fusion | flops 100663296 | bytes 1638400 | tf_op jit(solution)/shard_map/dot_general | solution.py:59
  57.2 2.5 %convolution_dynamic-update-slice_fusion.4 = f32[1024,128]{0,1:T(8,128)} fusion(f32[1024,128]{0,1:T(8,128)} %convolution_dynamic-update-slice_fusion.5, bf16[128,3072]{1,0:T(8,128)(2,1)} %collective-permute-done.5.refs_7_, bf16[128,3072]{1,0:T(8,128)(2,1)} %refs_2_.3), kind=kOutput, calls=%fused_computation.18 | convolution fusion | flops 100663296 | bytes 1638400 | tf_op jit(solution)/shard_map/dot_general | solution.py:59
  59.7 2.1 %convolution_dynamic-update-slice_fusion.3 = f32[1024,128]{0,1:T(8,128)} fusion(f32[1024,128]{0,1:T(8,128)} %convolution_dynamic-update-slice_fusion.4, bf16[128,3072]{1,0:T(8,128)(2,1)} %collective-permute-done.4.refs_8_, bf16[128,3072]{1,0:T(8,128)(2,1)S(1)} %copy-done.5), kind=kOutput, calls=%fused_computation.17 | convolution fusion | flops 100663296 | bytes 1638400 | tf_op jit(solution)/shard_map/dot_general | solution.py:59
  61.9 0.6 gather_fusion
  62.9 1.9 copy-done.2
  64.8 1.1 copy-done.6
  65.9 5.8 %shard_map.75 = (f32[6,2,128,128]{3,2,1,0:T(8,128)S(1)}, f32[6,2,128]{2,1,0:T(2,128)S(1)}) custom-call(s32[16]{0:T(128)S(1)} %min.12.asked_ref, bf16[128,3072]{1,0:T(8,128)(2,1)S(1)} %copy-done.6, bf16[4,128,3072]{2,1,0:T(8,128)(2,1)S(1)} %bitcast.173, bf16[4,128,3072]{2,1,0:T(8,128)(2,1)S(1)} %bitcast.189, ...), custom_call_target="tpu_custom_call" | custom-call | flops 1024 | bytes 1024 | tf_op jit(solution)/shard_map/pallas_call | solution.py:80
  71.8 1.8 convolution_dynamic-update-slice_fusion.2
  73.6 1.5 convolution_dynamic-update-slice_fusion.1
  75.1 1.5 convolution_dynamic-update-slice_fusion
  77.0 3.7 %shard_map.76 = (f32[2,2,128,128]{3,2,1,0:T(8,128)S(1)}, f32[2,2,128]{2,1,0:T(2,128)S(1)}) custom-call(s32[16]{0:T(128)S(1)} %min.12.asked_ref, bf16[128,3072]{1,0:T(8,128)(2,1)} %collective-permute-done.13.refs_0_.refs_4_, bf16[4,128,3072]{2,1,0:T(8,128)(2,1)S(1)} %bitcast.179, bf16[4,128,3072]{2,1,0:T(8,128)(2,1)S(1)} %bitcast.195, ...), custom_call_target="tpu_custom_call" | custom-call | flops 1024 | bytes 1024 | tf_op jit(solution)/shard_map/pallas_call | solution.py:80
  80.8 0.6 collective-permute-start.15
  81.5 2.0 %collective-permute-done.15 = f32[8,2,128]{2,0,1:T(8,128)S(1)} collective-permute-done((f32[8,2,128]{2,0,1:T(8,128)S(1)}, f32[8,2,128]{2,0,1:T(8,128)S(1)}, u32[]{:S(2)}, u32[]{:S(2)}) %collective-permute-start.15) | collective-permute-done | bytes 8224 | tf_op jit(solution)/shard_map/ppermute | solution.py:47
  83.5 1.2 collective-permute-start.16
  84.7 2.6 %collective-permute-done.16 = f32[8,2,128]{2,0,1:T(8,128)S(1)} collective-permute-done((f32[8,2,128]{2,0,1:T(8,128)S(1)}, f32[8,2,128]{2,0,1:T(8,128)S(1)}, u32[]{:S(2)}, u32[]{:S(2)}) %collective-permute-start.16) | collective-permute-done | bytes 8224 | tf_op jit(solution)/shard_map/ppermute | solution.py:47
  87.3 1.7 collective-permute-start.17
  89.0 2.6 %collective-permute-done.17 = f32[8,2,128]{2,0,1:T(8,128)S(1)} collective-permute-done((f32[8,2,128]{2,0,1:T(8,128)S(1)}, f32[8,2,128]{2,0,1:T(8,128)S(1)}, u32[]{:S(2)}, u32[]{:S(2)}) %collective-permute-start.17) | collective-permute-done | bytes 8224 | tf_op jit(solution)/shard_map/ppermute | solution.py:47
  91.6 1.2 subtract_convert_fusion
  94.0 1.1 copy-done.3
  95.1 2.1 %shard_map.77 = (bf16[128,3072]{1,0:T(8,128)(2,1)S(1)}, bf16[128,3072]{1,0:T(8,128)(2,1)S(1)}) custom-call(s32[16]{0:T(128)S(1)} %min.12.asked_ref, f32[8,128]{1,0:T(8,128)S(1)} %fusion.16.norm_ref, f32[2,2,128,128]{3,2,1,0:T(8,128)S(1)} %get-tuple-element.47.refs_0_.refs_3_.refs_1_, bf16[4,128,3072]{2,1,0:T(8,128)(2,1)S(1)} %bitcast.181, ...), custom_call_target="tpu_custom_call" | custom-call | flops 1024 | bytes 1024 | tf_op jit(solution)/shard_map/pallas_call | solution.py:80
  97.2 1.5 collective-permute-start.18
  98.8 3.0 %collective-permute-start.22 = (bf16[128,3072]{1,0:T(8,128)(2,1)S(1)}, bf16[128,3072]{1,0:T(8,128)(2,1)S(1)}, u32[]{:S(2)}, u32[]{:S(2)}) collective-permute-start(bf16[128,3072]{1,0:T(8,128)(2,1)S(1)} %convolution_convert_fusion.3), channel_id=1, source_target_pairs={{0,64},{1,65},{2,66},{3,67},{4,68},{5,69},{6,70},{7,71},{8,72},{9,... | collective-permute-start | bytes 2359304 | tf_op jit(solution)/shard_map/ppermute | solution.py:47
  101.7 6.5 %collective-permute-start.23 = (bf16[128,3072]{1,0:T(8,128)(2,1)S(1)}, bf16[128,3072]{1,0:T(8,128)(2,1)S(1)}, u32[]{:S(2)}, u32[]{:S(2)}) collective-permute-start(bf16[128,3072]{1,0:T(8,128)(2,1)S(1)} %convolution_convert_fusion.2), channel_id=1, source_target_pairs={{0,16},{1,49},{2,18},{3,51},{4,20},{5,53},{6,22},{7,55},{8,24},{9,... | collective-permute-start | bytes 2359304 | tf_op jit(solution)/shard_map/ppermute | solution.py:47
  108.5 6.6 %shard_map.79 = bf16[4,128,3072]{2,1,0:T(8,128)(2,1)S(1)} custom-call(s32[16]{0:T(128)S(1)} %min.12.asked_ref, f32[8,128]{1,0:T(8,128)S(1)} %fusion.16.norm_ref, f32[6,2,128,128]{3,2,1,0:T(8,128)S(1)} %copy-done.9, f32[2,2,128,128]{3,2,1,0:T(8,128)S(1)} %get-tuple-element.47.refs_0_.refs_3_.refs_1_, bf16[128,3072]{1,0:T(8,128)(2,1)S(1)} %copy-done.7, ...), custom_call_target="tpu_custom_call" | custom-call | flops 1024 | bytes 1024 | tf_op jit(solution)/shard_map/pallas_call | solution.py:80
  115.1 3.0 %collective-permute-done.23 = bf16[128,3072]{1,0:T(8,128)(2,1)S(1)} collective-permute-done((bf16[128,3072]{1,0:T(8,128)(2,1)S(1)}, bf16[128,3072]{1,0:T(8,128)(2,1)S(1)}, u32[]{:S(2)}, u32[]{:S(2)}) %collective-permute-start.23) | collective-permute-done | bytes 786464 | tf_op jit(solution)/shard_map/ppermute | solution.py:47
  118.1 5.5 %collective-permute-done.24 = bf16[128,3072]{1,0:T(8,128)(2,1)S(1)} collective-permute-done((bf16[128,3072]{1,0:T(8,128)(2,1)S(1)}, bf16[128,3072]{1,0:T(8,128)(2,1)S(1)}, u32[]{:S(2)}, u32[]{:S(2)}) %collective-permute-start.24) | collective-permute-done | bytes 786464 | tf_op jit(solution)/shard_map/ppermute | solution.py:47
  123.7 6.1 %collective-permute-start.25 = (bf16[4,128,3072]{2,1,0:T(8,128)(2,1)S(1)}, bf16[4,128,3072]{2,1,0:T(8,128)(2,1)S(1)}, u32[]{:S(2)}, u32[]{:S(2)}) collective-permute-start(bf16[4,128,3072]{2,1,0:T(8,128)(2,1)S(1)} %shard_map.79), channel_id=1, source_target_pairs={{0,1},{1,0},{2,3},{3,2},{4,5},{5,4},{6,7},{7,6},{8,9},{9,8},{10,11... | collective-permute-start | bytes 9437192 | tf_op jit(solution)/shard_map/ppermute | solution.py:47
  130.2 1.5 collective-permute-start.26
  131.7 0.5 fusion.2
  132.3 2.2 %shard_map.78 = (bf16[128,3072]{1,0:T(8,128)(2,1)S(1)}, bf16[128,3072]{1,0:T(8,128)(2,1)S(1)}) custom-call(s32[16]{0:T(128)S(1)} %min.12.asked_ref, f32[8,128]{1,0:T(8,128)S(1)} %fusion.16.norm_ref, f32[6,2,128,128]{3,2,1,0:T(8,128)S(1)} %copy-done.9, bf16[4,128,3072]{2,1,0:T(8,128)(2,1)S(1)} %bitcast.183, bf16[4,128,3072]{2,1,0:T(8,128)(2,1)S(1)} %bitcast.199, ...), custom_call_target="tpu_custom_call" | custom-call | flops 1024 | bytes 1024 | tf_op jit(solution)/shard_map/pallas_call | solution.py:80
  134.5 2.7 %collective-permute-start.20 = (bf16[128,3072]{1,0:T(8,128)(2,1)S(1)}, bf16[128,3072]{1,0:T(8,128)(2,1)S(1)}, u32[]{:S(2)}, u32[]{:S(2)}) collective-permute-start(bf16[128,3072]{1,0:T(8,128)(2,1)S(1)} %get-tuple-element.52), channel_id=1, source_target_pairs={{0,2},{1,7},{2,4},{3,1},{4,6},{5,3},{6,0},{7,5},{8,10},{9,15},{10,... | collective-permute-start | bytes 2359304 | tf_op jit(solution)/shard_map/ppermute | solution.py:47
  137.3 4.1 %collective-permute-done.26 = bf16[128,3072]{1,0:T(8,128)(2,1)S(1)} collective-permute-done((bf16[128,3072]{1,0:T(8,128)(2,1)S(1)}, bf16[128,3072]{1,0:T(8,128)(2,1)S(1)}, u32[]{:S(2)}, u32[]{:S(2)}) %collective-permute-start.26) | collective-permute-done | bytes 786464 | tf_op jit(solution)/shard_map/ppermute | solution.py:47
  141.4 11.9 %collective-permute-done.27 = bf16[128,3072]{1,0:T(8,128)(2,1)S(1)} collective-permute-done((bf16[128,3072]{1,0:T(8,128)(2,1)S(1)}, bf16[128,3072]{1,0:T(8,128)(2,1)S(1)}, u32[]{:S(2)}, u32[]{:S(2)}) %collective-permute-start.27) | collective-permute-done | bytes 786464 | tf_op jit(solution)/shard_map/ppermute | solution.py:47
  153.3 0.4 convolution_convert_fusion
  153.7 0.4 fusion.3
  154.2 2.7 %collective-permute-start.31 = (bf16[128,3072]{1,0:T(8,128)(2,1)S(1)}, bf16[128,3072]{1,0:T(8,128)(2,1)S(1)}, u32[]{:S(2)}, u32[]{:S(2)}) collective-permute-start(bf16[128,3072]{1,0:T(8,128)(2,1)S(1)} %fusion.3), channel_id=1, source_target_pairs={{0,16},{1,49},{2,18},{3,51},{4,20},{5,53},{6,22},{7,55},{8,24},{9,... | collective-permute-start | bytes 2359304 | tf_op jit(solution)/shard_map/ppermute | solution.py:47
  156.9 0.5 fusion.31
  157.8 3.0 %shard_map.80 = (bf16[128,3072]{1,0:T(8,128)(2,1)S(1)}, bf16[128,3072]{1,0:T(8,128)(2,1)S(1)}, bf16[128,3072]{1,0:T(8,128)(2,1)S(1)}) custom-call(s32[16]{0:T(128)S(1)} %min.12.asked_ref, f32[8,128]{1,0:T(8,128)S(1)} %fusion.16.norm_ref, f32[6,2,128,128]{3,2,1,0:T(8,128)S(1)} %copy-done.9, bf16[4,128,3072]{2,1,0:T(8,128)(2,1)S(1)} %bitcast.185, ...), custom_call_target="tpu_custom_call" | custom-call | flops 1024 | bytes 1024 | tf_op jit(solution)/shard_map/pallas_call | solution.py:80
  161.0 9.0 %shard_map.82 = f32[4,128,3072]{2,1,0:T(8,128)} custom-call(s32[16]{0:T(128)S(1)} %min.12.asked_ref, f32[8,128]{1,0:T(8,128)S(1)} %fusion.16.norm_ref, f32[6,2,128,128]{3,2,1,0:T(8,128)S(1)} %copy-done.9, f32[2,2,128,128]{3,2,1,0:T(8,128)S(1)} %get-tuple-element.47.refs_0_.refs_3_.refs_1_, bf16[128,3072]{1,0:T(8,128)(2,1)S(1)} %copy-done.7, ...), custom_call_target="tpu_custom_call" | custom-call | flops 1024 | bytes 1024 | tf_op jit(solution)/shard_map/pallas_call | solution.py:80
  169.9 5.3 %shard_map.81 = f32[128,3072]{1,0:T(8,128)S(1)} custom-call(s32[16]{0:T(128)S(1)} %min.12.asked_ref, f32[8,128]{1,0:T(8,128)S(1)} %fusion.16.norm_ref, f32[6,2,128,128]{3,2,1,0:T(8,128)S(1)} %copy-done.9, bf16[4,128,3072]{2,1,0:T(8,128)(2,1)S(1)} %bitcast.188, bf16[4,128,3072]{2,1,0:T(8,128)(2,1)S(1)} %bitcast.204, bf16[128,1024]{1,0:T(8,128)(2,1)S(1)} %bitcast.205, ...), custom_call_target="tpu_custom_call" | custom-call | flops 1024 | bytes 1024 | tf_op jit(solution)/shard_map/pallas_call | solution.py:80
  175.3 2.8 %collective-permute-start.28 = (bf16[128,3072]{1,0:T(8,128)(2,1)S(1)}, bf16[128,3072]{1,0:T(8,128)(2,1)S(1)}, u32[]{:S(2)}, u32[]{:S(2)}) collective-permute-start(bf16[128,3072]{1,0:T(8,128)(2,1)S(1)} %get-tuple-element.62), channel_id=1, source_target_pairs={{0,2},{1,7},{2,4},{3,1},{4,6},{5,3},{6,0},{7,5},{8,10},{9,15},{10,... | collective-permute-start | bytes 2359304 | tf_op jit(solution)/shard_map/ppermute | solution.py:47
  178.0 1.6 add_multiply_fusion
  179.6 0.5 collective-permute-done.30
  180.1 6.8 %collective-permute-done.28 = bf16[128,3072]{1,0:T(8,128)(2,1)S(1)} collective-permute-done((bf16[128,3072]{1,0:T(8,128)(2,1)S(1)}, bf16[128,3072]{1,0:T(8,128)(2,1)S(1)}, u32[]{:S(2)}, u32[]{:S(2)}) %collective-permute-start.28) | collective-permute-done | bytes 786464 | tf_op jit(solution)/shard_map/ppermute | solution.py:47
  186.9 1.6 add_multiply_fusion.1
  (100 shorter events, 4.7 us)
Async XLA Ops:
  0.6 26.2 %collective-permute-start.2 = (bf16[512,3072]{1,0:T(8,128)(2,1)}, bf16[512,3072]{1,0:T(8,128)(2,1)S(1)}, u32[]{:S(2)}, u32[]{:S(2)}) collective-permute-start(bf16[512,3072]{1,0:T(8,128)(2,1)} %param.6), channel_id=1, source_target_pairs={{0,1},{1,0},{2,3},{3,2},{4,5},{5,4},{6,7},{7,6},{8,9},{9,8},{10,11... | collective-permute-start | bytes 9437192 | tf_op jit(solution)/shard_map/ppermute | solution.py:47
  2.1 13.1 %collective-permute-start.5 = (bf16[128,3072]{1,0:T(8,128)(2,1)}, bf16[128,3072]{1,0:T(8,128)(2,1)}, u32[]{:S(2)}, u32[]{:S(2)}) collective-permute-start(bf16[128,3072]{1,0:T(8,128)(2,1)} %refs_4_.1), channel_id=1, source_target_pairs={{0,16},{1,49},{2,18},{3,51},{4,20},{5,53},{6,22},{7,55},{8,24},{9,... | collective-permute-start | bytes 2359304 | tf_op jit(solution)/shard_map/ppermute | solution.py:47
  6.0 18.6 %collective-permute-start = (bf16[128,3072]{1,0:T(8,128)(2,1)}, bf16[128,3072]{1,0:T(8,128)(2,1)}, u32[]{:S(2)}, u32[]{:S(2)}) collective-permute-start(bf16[128,3072]{1,0:T(8,128)(2,1)} %refs_2_.3), channel_id=1, source_target_pairs={{0,8},{1,9},{2,10},{3,11},{4,12},{5,13},{6,14},{7,15},{8,0},{9,1},... | collective-permute-start | bytes 2359304 | tf_op jit(solution)/shard_map/ppermute | solution.py:47
  7.2 19.6 %collective-permute-start.1 = (bf16[128,3072]{1,0:T(8,128)(2,1)}, bf16[128,3072]{1,0:T(8,128)(2,1)}, u32[]{:S(2)}, u32[]{:S(2)}) collective-permute-start(bf16[128,3072]{1,0:T(8,128)(2,1)} %refs_2_.3), channel_id=1, source_target_pairs={{0,2},{1,7},{2,4},{3,1},{4,6},{5,3},{6,0},{7,5},{8,10},{9,15},{10,... | collective-permute-start | bytes 2359304 | tf_op jit(solution)/shard_map/ppermute | solution.py:47
  9.9 27.7 %collective-permute-start.8 = (bf16[128,3072]{1,0:T(8,128)(2,1)}, bf16[128,3072]{1,0:T(8,128)(2,1)}, u32[]{:S(2)}, u32[]{:S(2)}) collective-permute-start(bf16[128,3072]{1,0:T(8,128)(2,1)} %refs_2_.3), channel_id=1, source_target_pairs={{0,6},{1,3},{2,0},{3,5},{4,2},{5,7},{6,4},{7,1},{8,14},{9,11},{10,... | collective-permute-start | bytes 2359304 | tf_op jit(solution)/shard_map/ppermute | solution.py:47
  15.2 20.2 %collective-permute-start.6 = (bf16[128,3072]{1,0:T(8,128)(2,1)}, bf16[128,3072]{1,0:T(8,128)(2,1)}, u32[]{:S(2)}, u32[]{:S(2)}) collective-permute-start(bf16[128,3072]{1,0:T(8,128)(2,1)} %refs_4_.1), channel_id=1, source_target_pairs={{0,48},{1,17},{2,50},{3,19},{4,52},{5,21},{6,54},{7,23},{8,56},{9,... | collective-permute-start | bytes 2359304 | tf_op jit(solution)/shard_map/ppermute | solution.py:47
  26.8 10.8 %copy-start.1 = (bf16[512,3072]{1,0:T(8,128)(2,1)}, bf16[512,3072]{1,0:T(8,128)(2,1)S(1)}, u32[]{:S(2)}) copy-start(bf16[512,3072]{1,0:T(8,128)(2,1)S(1)} %collective-permute-done.2) | copy-start | bytes 9437188
  26.8 12.4 %collective-permute-start.3 = (bf16[128,3072]{1,0:T(8,128)(2,1)}, bf16[128,3072]{1,0:T(8,128)(2,1)}, u32[]{:S(2)}, u32[]{:S(2)}) collective-permute-start(bf16[128,3072]{1,0:T(8,128)(2,1)} %collective-permute-done.refs_3_.refs_6_), channel_id=1, source_target_pairs={{0,2},{1,7},{2,4},{3,1},{4,6},{5,3},{6,0},{7,5},{8,10},{9,15},{10,... | collective-permute-start | bytes 2359304 | tf_op jit(solution)/shard_map/ppermute | solution.py:47
  29.9 17.5 %collective-permute-start.4 = (bf16[128,3072]{1,0:T(8,128)(2,1)}, bf16[128,3072]{1,0:T(8,128)(2,1)}, u32[]{:S(2)}, u32[]{:S(2)}) collective-permute-start(bf16[128,3072]{1,0:T(8,128)(2,1)} %refs_4_.1), channel_id=1, source_target_pairs={{0,64},{1,65},{2,66},{3,67},{4,68},{5,69},{6,70},{7,71},{8,72},{9,... | collective-permute-start | bytes 2359304 | tf_op jit(solution)/shard_map/ppermute | solution.py:47
  32.4 15.1 %collective-permute-start.10 = (bf16[128,3072]{1,0:T(8,128)(2,1)}, bf16[128,3072]{1,0:T(8,128)(2,1)}, u32[]{:S(2)}, u32[]{:S(2)}) collective-permute-start(bf16[128,3072]{1,0:T(8,128)(2,1)} %collective-permute-done.5.refs_7_), channel_id=1, source_target_pairs={{0,16},{1,49},{2,18},{3,51},{4,20},{5,53},{6,22},{7,55},{8,24},{9,... | collective-permute-start | bytes 2359304 | tf_op jit(solution)/shard_map/ppermute | solution.py:47
  33.0 2.5 %copy-start.4 = (bf16[128,3072]{1,0:T(8,128)(2,1)S(1)}, bf16[128,3072]{1,0:T(8,128)(2,1)}, u32[]{:S(2)}) copy-start(bf16[128,3072]{1,0:T(8,128)(2,1)} %refs_2_.3) | copy-start | bytes 2359300
  37.6 24.3 %collective-permute-start.9 = (bf16[128,3072]{1,0:T(8,128)(2,1)}, bf16[128,3072]{1,0:T(8,128)(2,1)}, u32[]{:S(2)}, u32[]{:S(2)}) collective-permute-start(bf16[128,3072]{1,0:T(8,128)(2,1)} %collective-permute-done.refs_3_.refs_6_), channel_id=1, source_target_pairs={{0,6},{1,3},{2,0},{3,5},{4,2},{5,7},{6,4},{7,1},{8,14},{9,11},{10,... | collective-permute-start | bytes 2359304 | tf_op jit(solution)/shard_map/ppermute | solution.py:47
  39.9 22.0 %all-to-all-start = ((s32[16,1,2]{2,1,0:T(1,128)}), s32[16,1,2]{2,1,0:T(1,128)S(1)}, u32[]{:S(2)}, u32[]{:S(2)}) async-start(s32[16,1,2]{2,1,0:T(1,128)} %copy.75), calls=%async_computation | async-start | bytes 16384 | tf_op jit(solution)/shard_map/all_to_all | solution.py:242
  45.0 14.8 %copy-start.5 = (bf16[128,3072]{1,0:T(8,128)(2,1)S(1)}, bf16[128,3072]{1,0:T(8,128)(2,1)}, u32[]{:S(2)}) copy-start(bf16[128,3072]{1,0:T(8,128)(2,1)} %refs_2_.3) | copy-start | bytes 2359300
  47.4 15.4 %collective-permute-start.7 = (bf16[128,3072]{1,0:T(8,128)(2,1)}, bf16[128,3072]{1,0:T(8,128)(2,1)}, u32[]{:S(2)}, u32[]{:S(2)}) collective-permute-start(bf16[128,3072]{1,0:T(8,128)(2,1)} %collective-permute-done.4.refs_8_), channel_id=1, source_target_pairs={{0,48},{1,17},{2,50},{3,19},{4,52},{5,21},{6,54},{7,23},{8,56},{9,... | collective-permute-start | bytes 2359304 | tf_op jit(solution)/shard_map/ppermute | solution.py:47
  47.4 26.1 %collective-permute-start.11 = (bf16[128,3072]{1,0:T(8,128)(2,1)}, bf16[128,3072]{1,0:T(8,128)(2,1)}, u32[]{:S(2)}, u32[]{:S(2)}) collective-permute-start(bf16[128,3072]{1,0:T(8,128)(2,1)} %collective-permute-done.10.refs_6_), channel_id=1, source_target_pairs={{0,64},{1,65},{2,66},{3,67},{4,68},{5,69},{6,70},{7,71},{8,72},{9,... | collective-permute-start | bytes 2359304 | tf_op jit(solution)/shard_map/ppermute | solution.py:47
  50.5 26.5 %collective-permute-start.13 = (bf16[128,3072]{1,0:T(8,128)(2,1)}, bf16[128,3072]{1,0:T(8,128)(2,1)}, u32[]{:S(2)}, u32[]{:S(2)}) collective-permute-start(bf16[128,3072]{1,0:T(8,128)(2,1)} %collective-permute-done.1.refs_6_.refs_5_), channel_id=1, source_target_pairs={{0,2},{1,7},{2,4},{3,1},{4,6},{5,3},{6,0},{7,5},{8,10},{9,15},{10,... | collective-permute-start | bytes 2359304 | tf_op jit(solution)/shard_map/ppermute | solution.py:47
  53.1 22.0 %collective-permute-start.12 = (bf16[128,3072]{1,0:T(8,128)(2,1)}, bf16[128,3072]{1,0:T(8,128)(2,1)}, u32[]{:S(2)}, u32[]{:S(2)}) collective-permute-start(bf16[128,3072]{1,0:T(8,128)(2,1)} %collective-permute-done.4.refs_8_), channel_id=1, source_target_pairs={{0,16},{1,49},{2,18},{3,51},{4,20},{5,53},{6,22},{7,55},{8,24},{9,... | collective-permute-start | bytes 2359304 | tf_op jit(solution)/shard_map/ppermute | solution.py:47
  57.2 5.7 %copy-start = (bf16[512,3072]{1,0:T(8,128)(2,1)S(1)}, bf16[512,3072]{1,0:T(8,128)(2,1)}, u32[]{:S(2)}) copy-start(bf16[512,3072]{1,0:T(8,128)(2,1)} %param.6) | copy-start | bytes 9437188
  61.9 15.1 %collective-permute-start.14 = (bf16[128,3072]{1,0:T(8,128)(2,1)}, bf16[128,3072]{1,0:T(8,128)(2,1)}, u32[]{:S(2)}, u32[]{:S(2)}) collective-permute-start(bf16[128,3072]{1,0:T(8,128)(2,1)} %collective-permute-done.9.refs_15_.refs_7_), channel_id=1, source_target_pairs={{0,6},{1,3},{2,0},{3,5},{4,2},{5,7},{6,4},{7,1},{8,14},{9,11},{10,... | collective-permute-start | bytes 2359304 | tf_op jit(solution)/shard_map/ppermute | solution.py:47
  62.9 1.9 %copy-start.2 = (bf16[512,3072]{1,0:T(8,128)(2,1)S(1)}, bf16[512,3072]{1,0:T(8,128)(2,1)}, u32[]{:S(2)}) copy-start(bf16[512,3072]{1,0:T(8,128)(2,1)} %copy-done.1) | copy-start | bytes 9437188
  64.8 1.1 copy-start.6
  65.9 5.9 %copy-start.11 = (f32[1024,128]{0,1:T(8,128)S(1)}, f32[1024,128]{0,1:T(8,128)}, u32[]{:S(2)}) copy-start(f32[1024,128]{0,1:T(8,128)} %convolution_dynamic-update-slice_fusion.3) | copy-start | bytes 1572868
  71.7 3.3 %copy-start.8 = (f32[6,2,128,128]{3,2,1,0:T(8,128)}, f32[6,2,128,128]{3,2,1,0:T(8,128)S(1)}, u32[]{:S(2)}) copy-start(f32[6,2,128,128]{3,2,1,0:T(8,128)S(1)} %get-tuple-element.51.refs_0_.refs_3_.refs_6_) | copy-start | bytes 2359300
  76.6 4.1 %copy-start.12 = (f32[1024,128]{0,1:T(8,128)}, f32[1024,128]{0,1:T(8,128)S(1)}, u32[]{:S(2)}) copy-start(f32[1024,128]{0,1:T(8,128)S(1)} %convolution_dynamic-update-slice_fusion) | copy-start | bytes 1572868
  80.8 12.0 %copy-start.7 = (bf16[128,3072]{1,0:T(8,128)(2,1)S(1)}, bf16[128,3072]{1,0:T(8,128)(2,1)}, u32[]{:S(2)}) copy-start(bf16[128,3072]{1,0:T(8,128)(2,1)} %refs_2_.3) | copy-start | bytes 2359300
  80.8 2.6 %collective-permute-start.15 = (f32[8,2,128]{2,0,1:T(8,128)S(1)}, f32[8,2,128]{2,0,1:T(8,128)S(1)}, u32[]{:S(2)}, u32[]{:S(2)}) collective-permute-start(f32[8,2,128]{2,0,1:T(8,128)S(1)} %concatenate.40), channel_id=1, source_target_pairs={{0,8},{1,9},{2,10},{3,11},{4,12},{5,13},{6,14},{7,15},{8,0},{9,1},... | collective-permute-start | bytes 24584 | tf_op jit(solution)/shard_map/ppermute | solution.py:47
  83.5 3.8 %collective-permute-start.16 = (f32[8,2,128]{2,0,1:T(8,128)S(1)}, f32[8,2,128]{2,0,1:T(8,128)S(1)}, u32[]{:S(2)}, u32[]{:S(2)}) collective-permute-start(f32[8,2,128]{2,0,1:T(8,128)S(1)} %pad_maximum_fusion.1), channel_id=1, source_target_pairs={{0,6},{1,3},{2,0},{3,5},{4,2},{5,7},{6,4},{7,1},{8,14},{9,11},{10,... | collective-permute-start | bytes 24584 | tf_op jit(solution)/shard_map/ppermute | solution.py:47
  87.3 4.3 %collective-permute-start.17 = (f32[8,2,128]{2,0,1:T(8,128)S(1)}, f32[8,2,128]{2,0,1:T(8,128)S(1)}, u32[]{:S(2)}, u32[]{:S(2)}) collective-permute-start(f32[8,2,128]{2,0,1:T(8,128)S(1)} %pad_maximum_fusion.3), channel_id=1, source_target_pairs={{0,4},{1,5},{2,6},{3,7},{4,0},{5,1},{6,2},{7,3},{8,12},{9,13},{10,... | collective-permute-start | bytes 24584 | tf_op jit(solution)/shard_map/ppermute | solution.py:47
  93.2 1.9 %copy-start.3 = (bf16[512,3072]{1,0:T(8,128)(2,1)S(1)}, bf16[512,3072]{1,0:T(8,128)(2,1)}, u32[]{:S(2)}) copy-start(bf16[512,3072]{1,0:T(8,128)(2,1)} %copy-done.1) | copy-start | bytes 9437188
  95.1 13.3 %copy-start.9 = (f32[6,2,128,128]{3,2,1,0:T(8,128)S(1)}, f32[6,2,128,128]{3,2,1,0:T(8,128)}, u32[]{:S(2)}) copy-start(f32[6,2,128,128]{3,2,1,0:T(8,128)} %copy-done.8) | copy-start | bytes 2359300
  97.2 17.8 %collective-permute-start.18 = (bf16[128,3072]{1,0:T(8,128)(2,1)S(1)}, bf16[128,3072]{1,0:T(8,128)(2,1)S(1)}, u32[]{:S(2)}, u32[]{:S(2)}) collective-permute-start(bf16[128,3072]{1,0:T(8,128)(2,1)S(1)} %get-tuple-element.48), channel_id=1, source_target_pairs={{0,2},{1,7},{2,4},{3,1},{4,6},{5,3},{6,0},{7,5},{8,10},{9,15},{10,... | collective-permute-start | bytes 2359304 | tf_op jit(solution)/shard_map/ppermute | solution.py:47
  98.7 16.4 %collective-permute-start.19 = (bf16[128,3072]{1,0:T(8,128)(2,1)S(1)}, bf16[128,3072]{1,0:T(8,128)(2,1)S(1)}, u32[]{:S(2)}, u32[]{:S(2)}) collective-permute-start(bf16[128,3072]{1,0:T(8,128)(2,1)S(1)} %get-tuple-element.49), channel_id=1, source_target_pairs={{0,6},{1,3},{2,0},{3,5},{4,2},{5,7},{6,4},{7,1},{8,14},{9,11},{10,... | collective-permute-start | bytes 2359304 | tf_op jit(solution)/shard_map/ppermute | solution.py:47
  98.8 16.3 %collective-permute-start.22 = (bf16[128,3072]{1,0:T(8,128)(2,1)S(1)}, bf16[128,3072]{1,0:T(8,128)(2,1)S(1)}, u32[]{:S(2)}, u32[]{:S(2)}) collective-permute-start(bf16[128,3072]{1,0:T(8,128)(2,1)S(1)} %convolution_convert_fusion.3), channel_id=1, source_target_pairs={{0,64},{1,65},{2,66},{3,67},{4,68},{5,69},{6,70},{7,71},{8,72},{9,... | collective-permute-start | bytes 2359304 | tf_op jit(solution)/shard_map/ppermute | solution.py:47
  101.7 16.4 %collective-permute-start.23 = (bf16[128,3072]{1,0:T(8,128)(2,1)S(1)}, bf16[128,3072]{1,0:T(8,128)(2,1)S(1)}, u32[]{:S(2)}, u32[]{:S(2)}) collective-permute-start(bf16[128,3072]{1,0:T(8,128)(2,1)S(1)} %convolution_convert_fusion.2), channel_id=1, source_target_pairs={{0,16},{1,49},{2,18},{3,51},{4,20},{5,53},{6,22},{7,55},{8,24},{9,... | collective-permute-start | bytes 2359304 | tf_op jit(solution)/shard_map/ppermute | solution.py:47
  108.2 15.5 %collective-permute-start.24 = (bf16[128,3072]{1,0:T(8,128)(2,1)S(1)}, bf16[128,3072]{1,0:T(8,128)(2,1)S(1)}, u32[]{:S(2)}, u32[]{:S(2)}) collective-permute-start(bf16[128,3072]{1,0:T(8,128)(2,1)S(1)} %convolution_convert_fusion.1), channel_id=1, source_target_pairs={{0,48},{1,17},{2,50},{3,19},{4,52},{5,21},{6,54},{7,23},{8,56},{9,... | collective-permute-start | bytes 2359304 | tf_op jit(solution)/shard_map/ppermute | solution.py:47
  123.7 34.1 %collective-permute-start.25 = (bf16[4,128,3072]{2,1,0:T(8,128)(2,1)S(1)}, bf16[4,128,3072]{2,1,0:T(8,128)(2,1)S(1)}, u32[]{:S(2)}, u32[]{:S(2)}) collective-permute-start(bf16[4,128,3072]{2,1,0:T(8,128)(2,1)S(1)} %shard_map.79), channel_id=1, source_target_pairs={{0,1},{1,0},{2,3},{3,2},{4,5},{5,4},{6,7},{7,6},{8,9},{9,8},{10,11... | collective-permute-start | bytes 9437192 | tf_op jit(solution)/shard_map/ppermute | solution.py:47
  130.2 11.2 %collective-permute-start.26 = (bf16[128,3072]{1,0:T(8,128)(2,1)S(1)}, bf16[128,3072]{1,0:T(8,128)(2,1)S(1)}, u32[]{:S(2)}, u32[]{:S(2)}) collective-permute-start(bf16[128,3072]{1,0:T(8,128)(2,1)S(1)} %fusion.1), channel_id=1, source_target_pairs={{0,16},{1,49},{2,18},{3,51},{4,20},{5,53},{6,22},{7,55},{8,24},{9,... | collective-permute-start | bytes 2359304 | tf_op jit(solution)/shard_map/ppermute | solution.py:47
  132.2 21.0 %collective-permute-start.27 = (bf16[128,3072]{1,0:T(8,128)(2,1)S(1)}, bf16[128,3072]{1,0:T(8,128)(2,1)S(1)}, u32[]{:S(2)}, u32[]{:S(2)}) collective-permute-start(bf16[128,3072]{1,0:T(8,128)(2,1)S(1)} %fusion.2), channel_id=1, source_target_pairs={{0,64},{1,65},{2,66},{3,67},{4,68},{5,69},{6,70},{7,71},{8,72},{9,... | collective-permute-start | bytes 2359304 | tf_op jit(solution)/shard_map/ppermute | solution.py:47
  134.5 23.3 %collective-permute-start.20 = (bf16[128,3072]{1,0:T(8,128)(2,1)S(1)}, bf16[128,3072]{1,0:T(8,128)(2,1)S(1)}, u32[]{:S(2)}, u32[]{:S(2)}) collective-permute-start(bf16[128,3072]{1,0:T(8,128)(2,1)S(1)} %get-tuple-element.52), channel_id=1, source_target_pairs={{0,2},{1,7},{2,4},{3,1},{4,6},{5,3},{6,0},{7,5},{8,10},{9,15},{10,... | collective-permute-start | bytes 2359304 | tf_op jit(solution)/shard_map/ppermute | solution.py:47
  137.3 20.5 %collective-permute-start.21 = (bf16[128,3072]{1,0:T(8,128)(2,1)S(1)}, bf16[128,3072]{1,0:T(8,128)(2,1)S(1)}, u32[]{:S(2)}, u32[]{:S(2)}) collective-permute-start(bf16[128,3072]{1,0:T(8,128)(2,1)S(1)} %get-tuple-element.53), channel_id=1, source_target_pairs={{0,6},{1,3},{2,0},{3,5},{4,2},{5,7},{6,4},{7,1},{8,14},{9,11},{10,... | collective-permute-start | bytes 2359304 | tf_op jit(solution)/shard_map/ppermute | solution.py:47
  153.7 24.3 %collective-permute-start.32 = (bf16[128,3072]{1,0:T(8,128)(2,1)S(1)}, bf16[128,3072]{1,0:T(8,128)(2,1)S(1)}, u32[]{:S(2)}, u32[]{:S(2)}) collective-permute-start(bf16[128,3072]{1,0:T(8,128)(2,1)S(1)} %convolution_convert_fusion), channel_id=1, source_target_pairs={{0,48},{1,17},{2,50},{3,19},{4,52},{5,21},{6,54},{7,23},{8,56},{9,... | collective-permute-start | bytes 2359304 | tf_op jit(solution)/shard_map/ppermute | solution.py:47
  154.2 23.9 %collective-permute-start.31 = (bf16[128,3072]{1,0:T(8,128)(2,1)S(1)}, bf16[128,3072]{1,0:T(8,128)(2,1)S(1)}, u32[]{:S(2)}, u32[]{:S(2)}) collective-permute-start(bf16[128,3072]{1,0:T(8,128)(2,1)S(1)} %fusion.3), channel_id=1, source_target_pairs={{0,16},{1,49},{2,18},{3,51},{4,20},{5,53},{6,22},{7,55},{8,24},{9,... | collective-permute-start | bytes 2359304 | tf_op jit(solution)/shard_map/ppermute | solution.py:47
  160.8 19.3 %collective-permute-start.30 = (bf16[128,3072]{1,0:T(8,128)(2,1)S(1)}, bf16[128,3072]{1,0:T(8,128)(2,1)S(1)}, u32[]{:S(2)}, u32[]{:S(2)}) collective-permute-start(bf16[128,3072]{1,0:T(8,128)(2,1)S(1)} %get-tuple-element.56), channel_id=1, source_target_pairs={{0,8},{1,9},{2,10},{3,11},{4,12},{5,13},{6,14},{7,15},{8,0},{9,1},... | collective-permute-start | bytes 2359304 | tf_op jit(solution)/shard_map/ppermute | solution.py:47
  160.9 9.1 %copy-start.10 = (bf16[128,3072]{1,0:T(8,128)(2,1)S(1)}, bf16[128,3072]{1,0:T(8,128)(2,1)}, u32[]{:S(2)}) copy-start(bf16[128,3072]{1,0:T(8,128)(2,1)} %refs_4_.1) | copy-start | bytes 2359300
  160.9 19.2 %collective-permute-start.29 = (bf16[128,3072]{1,0:T(8,128)(2,1)S(1)}, bf16[128,3072]{1,0:T(8,128)(2,1)S(1)}, u32[]{:S(2)}, u32[]{:S(2)}) collective-permute-start(bf16[128,3072]{1,0:T(8,128)(2,1)S(1)} %get-tuple-element.63), channel_id=1, source_target_pairs={{0,6},{1,3},{2,0},{3,5},{4,2},{5,7},{6,4},{7,1},{8,14},{9,11},{10,... | collective-permute-start | bytes 2359304 | tf_op jit(solution)/shard_map/ppermute | solution.py:47
  175.3 11.7 %collective-permute-start.28 = (bf16[128,3072]{1,0:T(8,128)(2,1)S(1)}, bf16[128,3072]{1,0:T(8,128)(2,1)S(1)}, u32[]{:S(2)}, u32[]{:S(2)}) collective-permute-start(bf16[128,3072]{1,0:T(8,128)(2,1)S(1)} %get-tuple-element.62), channel_id=1, source_target_pairs={{0,2},{1,7},{2,4},{3,1},{4,6},{5,3},{6,0},{7,5},{8,10},{9,15},{10,... | collective-permute-start | bytes 2359304 | tf_op jit(solution)/shard_map/ppermute | solution.py:47
where the time goes:
time: 192 us; the launch traced here: 189 us
  waiting for transfers between devices  58.9 us (31%)
  starting transfers between devices  58.7 us (31%)
  Pallas kernels  37.7 us (20%)
  matrix products  19.7 us (10%)
  local copies, waits for them, and re-layouts  6.25 us (3%)
  other arithmetic  6.17 us (3%)
    ppermute x33, waiting for transfers between devices, send(): return lax.ppermute(value, AXES, route)  58.9 us
    ppermute x33, starting transfers between devices, send(): return lax.ppermute(value, AXES, route)  53.6 us
    pallas_call x8, Pallas kernels, kernel(): pl.pallas_call(body, grid_spec=pltpu.PrefetchScalarGridSpec(num_scalar_pr...  37.7 us
    dot_general x8, matrix products, rows_dot(): lax.dot_general(left, right, (((1,), (1,)), ((), ())), preferred_element_...  16.4 us
    all_to_all x1, starting transfers between devices, local(): lax.all_to_all(after(pairs, q[1, 3]), 'dp', split_axis=0, concat_axis=0,...  5.09 us
    unnamed x26, local copies, waits for them, and re-layouts  4.15 us
  transfers between devices with their start and end apart: 34, of which 14 were waited for; matrix products, arithmetic and copies ran while one was open for 13% of the time, Pallas kernels for 17%

commit v1 on v0

--- a/solution.py
+++ b/solution.py
@@ -134,30 +134,38 @@
     return kernel(body, asked, arrays, specs, outs, [whole(o) for o in outs], steps)
 
 
-def hard_parts(asked, scores, norm, tables, plan, loop=()):
+def hard_parts(asked, scores, norm, tables, plan, peers=None, loop=()):
     width = tables[0].shape[2]
     count = len(plan)
-    extra = [a for _, adds, _ in plan for a in adds]
+    extra = [a for _, adds, _ in plan for a, _ in adds]
+    tail = (() if peers is None else (peers,)) + tuple(loop)
 
     def body(asked_ref, norm_ref, *refs):
         mine, outs, held = refs[: 3 * count], refs[-count - 1 : -1], refs[-1]
-        more = list(refs[3 * count : -count - 1])
+        more = list(refs[3 * count : 3 * count + len(extra)])
+        rest = list(refs[3 * count + len(extra) : -count - 1])
+        peers_ref = None if peers is None else rest.pop(0)
 
         @pl.when(pl.program_id(0) == 0)
         def _():
             for n, (spot, _, _) in enumerate(plan):
                 for w in range(2):
-                    weight = jnp.exp(mine[3 * n][0, w] - norm_ref[spot : spot + 1, :])
+                    score = mine[3 * n][0, w]
+                    weight = jnp.where(score > 0.5 * LOW, jnp.exp(score - norm_ref[spot : spot + 1, :]), 0.0)
                     held[n, :, w * BLOCK : (w + 1) * BLOCK] = weight.T.astype(BF16)
 
-        for n, (_, adds, dtype) in enumerate(plan):
+        for n, (spot, adds, dtype) in enumerate(plan):
             keys = jnp.concatenate([mine[3 * n + 1][0], mine[3 * n + 2][0]], axis=0)
             total = mm(held[n], keys)
-            for _ in adds:
-                total = total + more.pop(0)[...].astype(F32)
+            for _, peer in adds:
+                piece = more.pop(0)[...].astype(F32)
+                if peer is not None:
+                    scale = jnp.exp(peers_ref[peer : peer + 1, :] - norm_ref[spot : spot + 1, :])
+                    piece = piece * jnp.broadcast_to(scale, (BLOCK, BLOCK)).T[:, :1]
+                total = total + piece
             if n == 0 and loop:
                 for m in range(len(loop) - 1):
-                    total = total + mm(more[0][:, m * BLOCK : (m + 1) * BLOCK], more[m + 1][...])
+                    total = total + mm(rest[0][:, m * BLOCK : (m + 1) * BLOCK], rest[m + 1][...])
             outs[n][...] = total.astype(dtype)
 
     arrays, specs = [], []
@@ -167,8 +175,9 @@
         specs += [
             pl.BlockSpec((1, 2, BLOCK, BLOCK), lambda i, s, n=n: (n, 0, 0, 0)), chosen(spot, 0), chosen(spot, 1),
         ]
-    arrays += extra + list(loop)
-    specs += [column(a, WIDE) for a in extra] + [whole(a) for a in loop[:1]] + [column(a, WIDE) for a in loop[1:]]
+    arrays += extra + list(tail)
+    specs += [column(a, WIDE) for a in extra] + [whole(a) for a in tail[: len(tail) - max(len(loop) - 1, 0)]]
+    specs += [column(a, WIDE) for a in loop[1:]]
     outs = [jax.ShapeDtypeStruct((BLOCK, width), dtype) for _, _, dtype in plan]
     return kernel(
         body, asked, (norm, *arrays), [whole(norm)] + specs, outs, [column(o, WIDE) for o in outs], width // WIDE,
@@ -192,7 +201,9 @@
         @pl.when(pl.program_id(0) == 0)
         def _():
             for j, (k, n) in enumerate(place):
-                weights[j] = jnp.exp(found[k][n, w] - norm_ref[j : j + 1, :]).astype(BF16)
+                score = found[k][n, w]
+                weight = jnp.where(score > 0.5 * LOW, jnp.exp(score - norm_ref[j : j + 1, :]), 0.0)
+                weights[j] = weight.astype(BF16)
 
         total[...] = jnp.zeros_like(total) if start is None else rest[count][...].astype(F32)
         for j in range(count):
@@ -218,33 +229,34 @@
     mx, my, mc = me // 8, (me // 2) % 4, me % 2
     turn = 1 - 2 * mc
 
+    owner = hard_ids[0] // held % 16
+    matches = owner[:, None] == jnp.arange(16, dtype=jnp.int32)[None, :]
+    wanted = jnp.sum(jnp.where(matches, (hard_ids[0] % held)[:, None] + 1, 0), axis=0) - 1
+    pairs = jnp.repeat(wanted.reshape(8, 1, 2), 2, axis=1).reshape(16, 2)
+    asked = lax.all_to_all(pairs, "dp", split_axis=0, concat_axis=0, tiled=True)
+    spot_place = jnp.stack([((mx + a) % 2) * 4 + (my + turn * b) % 4 for a, b in SPOTS])
+    asked = jnp.take(asked.reshape(8, 2, 2), spot_place, axis=0)
+    asked = lax.dynamic_index_in_dim(asked, mc, 1, keepdims=False)
+    asked = jnp.where(mc == 0, asked, asked[:, ::-1])
+    asked = jnp.clip(asked.reshape(16), -1, held - 1)
+
     q, p = {(0, 0): queries}, {(0, 0): positives}
     other = send(corpus, CORE)
     q[1, 0] = send(queries, X_LO)
     q[0, 3], q[0, 1] = send(queries, Y_FWD), send(queries, Y_BWD)
-    p[0, 3] = send(positives, Z_FWD)
+    p[0, 3] = send(after(positives, asked), Z_FWD)
 
     p[1, 0] = send(after(positives, q[1, 0], other), X_HI)
-    q[1, 3] = send(after(q[1, 0], q[0, 3], other), Y_FWD)
-    q[1, 1] = send(after(q[1, 0], q[0, 1], other), Y_BWD)
+    q[1, 3] = send(after(q[1, 0], other), Y_FWD)
+    q[1, 1] = send(after(q[1, 0], other), Y_BWD)
     p[0, 2] = send(after(p[0, 3], other), Z_FWD)
-    p[0, 1] = send(after(positives, p[0, 3]), Z_BWD)
+    p[0, 1] = send(after(positives, q[0, 1], q[0, 3], other), Z_BWD)
 
     q[0, 2] = send(after(q[0, 3], q[1, 3]), Y_FWD)
     q[1, 2] = send(q[1, 1], Y_BWD)
     p[1, 3], p[1, 1] = send(p[1, 0], Z_FWD), send(after(p[1, 0], p[0, 1]), Z_BWD)
     p[1, 2] = send(after(p[0, 2], p[1, 0]), X_HI)
 
-    owner = hard_ids[0] // held % 16
-    matches = owner[:, None] == jnp.arange(16, dtype=jnp.int32)[None, :]
-    wanted = jnp.sum(jnp.where(matches, (hard_ids[0] % held)[:, None] + 1, 0), axis=0) - 1
-    pairs = jnp.repeat(wanted.reshape(8, 1, 2), 2, axis=1).reshape(16, 2)
-    asked = lax.all_to_all(after(pairs, q[1, 3]), "dp", split_axis=0, concat_axis=0, tiled=True)
-    spot_place = jnp.stack([((mx + a) % 2) * 4 + (my + turn * b) % 4 for a, b in SPOTS])
-    asked = jnp.take(asked.reshape(8, 2, 2), spot_place, axis=0)
-    asked = lax.dynamic_index_in_dim(asked, mc, 1, keepdims=False)
-    asked = jnp.where(mc == 0, asked, asked[:, ::-1])
-    asked = after(jnp.clip(asked.reshape(16), -1, held - 1), p[1, 1])
 
     tables = (corpus.reshape(held, BLOCK, width), other.reshape(held, BLOCK, width))
     scores, stats = {}, {}
@@ -267,25 +279,35 @@
         return jnp.stack([m, s], axis=1)
 
     state = jnp.stack([stats[j] for j in range(8)])
+    peaks = state[:, 0]
+    near_spot, far_spot = SPOTS.index((0, 2)), SPOTS.index((1, 2))
     state = cat(merge(state[:1], jnp.stack([peak, total])[None]), state[1:])
-    for route, turns in ((X_LO, (1, 0)), (Y_BWD, (0, 1)), (Y_TWO, (0, 2))):
-        peer = send(state, route).reshape(2, 4, 2, BLOCK)
-        state = merge(state, jnp.roll(peer, turns, axis=(0, 1)).reshape(8, 2, BLOCK))
+
+    def turned(peer, turns):
+        return jnp.roll(peer.reshape(2, 4, 2, BLOCK), turns, axis=(0, 1)).reshape(8, 2, BLOCK)
+
+    state = merge(state, turned(send(state, X_LO), (1, 0)))
+    behind = send(cat(state, stats[near_spot][None]), Y_FWD)
+    ahead = send(cat(state, stats[far_spot][None]), Y_BWD)
+    across = send(state, Y_TWO)
+    peers = cat(behind[8:, 0], ahead[8:, 0])
+    state = merge(merge(state, turned(ahead[:8], (0, 1))), merge(turned(behind[:8], (0, 3)), turned(across, (0, 2))))
     norm = state[:, 0] + jnp.log(state[:, 1])
     inner_w = (jnp.exp(inner - norm[:1]) - diag.astype(F32)).astype(BF16)
     losses = norm[0] - own_score
 
-    def y_parts(wait, *plan, loop=()):
+    def y_parts(reference, wait, *plan, **more):
         return hard_parts(
-            asked, scores, after(norm, *wait), tables, [(SPOTS.index(o), adds, dtype) for o, adds, dtype in plan], loop
+            asked, scores, after(reference, *wait), tables,
+            [(SPOTS.index(o), adds, dtype) for o, adds, dtype in plan], **more
         )
 
     def z_part(o, weights, *adds):
         j = SPOTS.index(o)
         return near(mm(weights[j * BLOCK : (j + 1) * BLOCK], queries), *adds).astype(BF16)
 
-    y02, y12 = y_parts((), ((0, 2), (), BF16), ((1, 2), (), BF16))
-    y02, y12 = send(y02, Y_FWD), send(y12, Y_BWD)
+    y02, y12 = y_parts(peaks, (), ((0, 2), (), BF16), ((1, 2), (), BF16))
+    y02, y12 = send(after(y02, across), Y_FWD), send(after(y12, across), Y_BWD)
     z12 = send(z_part((1, 2), inner_w), X_HI)
     z11 = send(z_part((1, 1), inner_w), Z_FWD)
     z13 = send(z_part((1, 3), inner_w), Z_BWD)
@@ -293,25 +315,25 @@
     q_blocks = [q[o] for o in SPOTS]
     in_order = [scores[j] for j in range(8)]
     theirs = corpus_part(asked, in_order, norm, q_blocks, held, BF16, 1)
-    inner_2 = after(inner_w, z12, z11, z13)
-    y11, y13 = y_parts((y02, y12), ((1, 1), (), BF16), ((1, 3), (y12,), BF16))
+    y11, y13 = y_parts(norm, (y02, y12), ((1, 1), (), BF16), ((1, 3), ((y12, 1),), BF16), peers=peers)
+    inner_2 = after(inner_w, y11)
     y11, y13 = send(y11, Y_FWD), send(y13, Y_BWD)
     z02 = send(z_part((0, 2), inner_2, z12), Z_FWD)
     z10 = send(z_part((1, 0), inner_2, z11, z13), X_HI)
-    theirs = send(after(theirs, y02, y12, z12, z11, z13), CORE)
-
-    inner_3 = after(inner_2, z02, z10)
-    y10, y01, y03 = y_parts(
-        (y11, y13, theirs), ((1, 0), (y11, y13), BF16), ((0, 1), (y02,), BF16), ((0, 3), (), BF16)
-    )
-    done = after(norm, y10)
-    y10 = send(y10, X_LO)
-    y01, y03 = send(y01, Y_FWD), send(y03, Y_BWD)
+    theirs = send(after(theirs, inner_2, z12, z11, z13), CORE)
+
+    inner_3 = after(inner_2, z02, theirs)
     z01 = send(z_part((0, 1), inner_3, z02), Z_FWD)
     z03 = send(z_part((0, 3), inner_3), Z_BWD)
     loop = (jnp.swapaxes(inner_3, 0, 1), *[p[o] for o in SPOTS])
-    (mine,) = y_parts((done,), ((0, 0), (), F32), loop=loop)
-    grad_corpus = corpus_part(asked, in_order, done, q_blocks, held, F32, 0, theirs)
+    (mine,) = y_parts(norm, (z02, theirs), ((0, 0), (), F32), loop=loop)
+    y10, y01, y03 = y_parts(
+        norm, (y11, y13, mine), ((1, 0), ((y11, None), (y13, None)), BF16), ((0, 1), ((y02, 0),), BF16),
+        ((0, 3), (), BF16), peers=peers
+    )
+    y10 = send(after(y10, z10), X_LO)
+    y01, y03 = send(y01, Y_FWD), send(y03, Y_BWD)
+    grad_corpus = corpus_part(asked, in_order, after(norm, z03), q_blocks, held, F32, 0, theirs)
     mine, first, grad_corpus = lax.optimization_barrier((mine, mm(inner_3[:BLOCK], queries), grad_corpus))
     grad_queries = OUT_SCALE * near(mine, y01, y03, y10)
     grad_positives = OUT_SCALE * near(first, z01, z03, z10)

time: 192 us -> 165 us (0.86); the launches traced: 189 us -> 164 us
  matrix products: 19.7 us -> 7.95 us
  starting transfers between devices: 58.7 us -> 48 us
  Pallas kernels: 37.7 us -> 32.6 us
  local copies, waits for them, and re-layouts: 6.25 us -> 9.45 us
    dot_general x8, matrix products: 16.4 us -> 4.73 us  [rows_dot(): lax.dot_general(left, right, (((1,), (1,)), ((), ())), preferred_element_...]
    ppermute x33 -> x34, starting transfers between devices: 53.6 us -> 42.4 us  [send(): return lax.ppermute(value, AXES, route)]
    pallas_call x8, Pallas kernels: 37.7 us -> 32.6 us  [kernel(): pl.pallas_call(body, grid_spec=pltpu.PrefetchScalarGridSpec(num_scalar_pr...]
    all_to_all x1, waiting for transfers between devices: 0.01 us -> 3.81 us  [local(): asked = lax.all_to_all(pairs, 'dp', split_axis=0, concat_axis=0, tiled=True)]
    unnamed x26 -> x76, local copies, waits for them, and re-layouts: 4.15 us -> 7.61 us
    ppermute x33 -> x34, waiting for transfers between devices: 58.9 us -> 55.8 us  [send(): return lax.ppermute(value, AXES, route)]
  transfers between devices with their start and end apart: 34 -> 35, of which waited for: 14 -> 17; matrix products, arithmetic and copies ran while one was open for 13% -> 8% of each run, Pallas kernels for 17% -> 20%
where the time goes in v1:
time: 165 us; the launch traced here: 164 us
  waiting for transfers between devices  59.6 us (36%)
  starting transfers between devices  48 us (29%)
  Pallas kernels  32.6 us (20%)
  local copies, waits for them, and re-layouts  9.45 us (6%)
  matrix products  7.95 us (5%)
  other arithmetic  5.16 us (3%)
    ppermute x34, waiting for transfers between devices, send(): return lax.ppermute(value, AXES, route)  55.8 us
    ppermute x34, starting transfers between devices, send(): return lax.ppermute(value, AXES, route)  42.4 us
    pallas_call x8, Pallas kernels, kernel(): pl.pallas_call(body, grid_spec=pltpu.PrefetchScalarGridSpec(num_scalar_pr...  32.6 us
    unnamed x76, local copies, waits for them, and re-layouts  7.61 us
    all_to_all x1, starting transfers between devices, local(): asked = lax.all_to_all(pairs, 'dp', split_axis=0, concat_axis=0, tiled=True)  5.61 us
    dot_general x8, matrix products, rows_dot(): lax.dot_general(left, right, (((1,), (1,)), ((), ())), preferred_element_...  4.73 us
    all_to_all x1, waiting for transfers between devices, local(): asked = lax.all_to_all(pairs, 'dp', split_axis=0, concat_axis=0, tiled=True)  3.81 us
  transfers between devices with their start and end apart: 35, of which 17 were waited for; matrix products, arithmetic and copies ran while one was open for 8% of the time, Pallas kernels for 20%

profile of v1, /device:TPU:1, one launch (start us, length us, event | category | flops | bytes accessed | tf_op | source)
XLA Modules:
  0.0 164.0 jit_solution(12363295417664831638)
XLA Ops:
  0.6 1.5 collective-permute-start
  2.1 0.7 and_select_fusion.1
  3.0 0.6 broadcast_in_dim.39.clone
  3.6 5.6 %all-to-all-start = ((s32[16,1,2]{2,1,0:T(1,128)}), s32[16,1,2]{2,1,0:T(1,128)S(1)}, u32[]{:S(2)}, u32[]{:S(2)}) async-start(s32[16,1,2]{2,1,0:T(1,128)} %bitcast.9), calls=%async_computation | async-start | bytes 16384 | tf_op jit(solution)/shard_map/all_to_all | solution.py:236
  9.2 1.4 collective-permute-start.1
  10.8 3.8 %all-to-all-done = s32[16,1,2]{2,1,0:T(1,128)S(1)} async-done(((s32[16,1,2]{2,1,0:T(1,128)}), s32[16,1,2]{2,1,0:T(1,128)S(1)}, u32[]{:S(2)}, u32[]{:S(2)}) %all-to-all-start) | async-done | bytes 160 | tf_op jit(solution)/shard_map/all_to_all | solution.py:236
  14.6 0.6 gather_fusion
  15.6 3.8 %collective-permute-start.7 = (bf16[128,3072]{1,0:T(8,128)(2,1)}, bf16[128,3072]{1,0:T(8,128)(2,1)S(1)}, u32[]{:S(2)}, u32[]{:S(2)}) collective-permute-start(bf16[128,3072]{1,0:T(8,128)(2,1)} %refs_4_.1), channel_id=1, source_target_pairs={{0,16},{1,49},{2,18},{3,51},{4,20},{5,53},{6,22},{7,55},{8,24},{9,... | collective-permute-start | bytes 2359304 | tf_op jit(solution)/shard_map/ppermute | solution.py:47
  19.7 2.4 %collective-permute-start.2 = (bf16[128,3072]{1,0:T(8,128)(2,1)}, bf16[128,3072]{1,0:T(8,128)(2,1)S(1)}, u32[]{:S(2)}, u32[]{:S(2)}) collective-permute-start(bf16[128,3072]{1,0:T(8,128)(2,1)} %refs_2_.3), channel_id=1, source_target_pairs={{0,2},{1,7},{2,4},{3,1},{4,6},{5,3},{6,0},{7,5},{8,10},{9,15},{10,... | collective-permute-start | bytes 2359304 | tf_op jit(solution)/shard_map/ppermute | solution.py:47
  22.1 6.5 %collective-permute-done.1.refs_3_.refs_6_ = bf16[128,3072]{1,0:T(8,128)(2,1)} collective-permute-done((bf16[128,3072]{1,0:T(8,128)(2,1)}, bf16[128,3072]{1,0:T(8,128)(2,1)}, u32[]{:S(2)}, u32[]{:S(2)}) %collective-permute-start.1) | collective-permute-done | bytes 786464 | tf_op jit(solution)/shard_map/ppermute | solution.py:47
  28.6 2.4 %collective-permute-start.4 = (bf16[128,3072]{1,0:T(8,128)(2,1)}, bf16[128,3072]{1,0:T(8,128)(2,1)S(1)}, u32[]{:S(2)}, u32[]{:S(2)}) collective-permute-start(bf16[128,3072]{1,0:T(8,128)(2,1)} %collective-permute-done.1.refs_3_.refs_6_), channel_id=1, source_target_pairs={{0,2},{1,7},{2,4},{3,1},{4,6},{5,3},{6,0},{7,5},{8,10},{9,15},{10,... | collective-permute-start | bytes 2359304 | tf_op jit(solution)/shard_map/ppermute | solution.py:47
  31.1 3.8 %collective-permute-start.8 = (bf16[128,3072]{1,0:T(8,128)(2,1)S(1)}, bf16[128,3072]{1,0:T(8,128)(2,1)S(1)}, u32[]{:S(2)}, u32[]{:S(2)}) collective-permute-start(bf16[128,3072]{1,0:T(8,128)(2,1)S(1)} %collective-permute-done.7.refs_7_), channel_id=1, source_target_pairs={{0,16},{1,49},{2,18},{3,51},{4,20},{5,53},{6,22},{7,55},{8,24},{9,... | collective-permute-start | bytes 2359304 | tf_op jit(solution)/shard_map/ppermute | solution.py:47
  34.8 2.5 %collective-permute-start.9 = (bf16[128,3072]{1,0:T(8,128)(2,1)}, bf16[128,3072]{1,0:T(8,128)(2,1)S(1)}, u32[]{:S(2)}, u32[]{:S(2)}) collective-permute-start(bf16[128,3072]{1,0:T(8,128)(2,1)} %refs_4_.1), channel_id=1, source_target_pairs={{0,64},{1,65},{2,66},{3,67},{4,68},{5,69},{6,70},{7,71},{8,72},{9,... | collective-permute-start | bytes 2359304 | tf_op jit(solution)/shard_map/ppermute | solution.py:47
  37.3 2.7 %collective-permute-done.3.refs_9_.refs_3_ = bf16[128,3072]{1,0:T(8,128)(2,1)S(1)} collective-permute-done((bf16[128,3072]{1,0:T(8,128)(2,1)}, bf16[128,3072]{1,0:T(8,128)(2,1)S(1)}, u32[]{:S(2)}, u32[]{:S(2)}) %collective-permute-start.3) | collective-permute-done | bytes 786464 | tf_op jit(solution)/shard_map/ppermute | solution.py:47
  40.1 2.1 %convolution_dynamic-update-slice_fusion.7 = f32[1024,128]{0,1:T(8,128)S(1)} fusion(bf16[128,3072]{1,0:T(8,128)(2,1)} %refs_4_.1, bf16[128,3072]{1,0:T(8,128)(2,1)} %refs_2_.3), kind=kOutput, calls=%fused_computation.18 | convolution fusion | flops 100663296 | bytes 1638400 | tf_op jit(solution)/shard_map/dot_general | solution.py:59
  42.3 6.8 %collective-permute-done.4.refs_12_.refs_9_ = bf16[128,3072]{1,0:T(8,128)(2,1)S(1)} collective-permute-done((bf16[128,3072]{1,0:T(8,128)(2,1)}, bf16[128,3072]{1,0:T(8,128)(2,1)S(1)}, u32[]{:S(2)}, u32[]{:S(2)}) %collective-permute-start.4) | collective-permute-done | bytes 786464 | tf_op jit(solution)/shard_map/ppermute | solution.py:47
  49.1 1.6 %collective-permute-start.13 = (bf16[128,3072]{1,0:T(8,128)(2,1)S(1)}, bf16[128,3072]{1,0:T(8,128)(2,1)S(1)}, u32[]{:S(2)}, u32[]{:S(2)}) collective-permute-start(bf16[128,3072]{1,0:T(8,128)(2,1)S(1)} %collective-permute-done.2.refs_6_.refs_5_), channel_id=1, source_target_pairs={{0,2},{1,7},{2,4},{3,1},{4,6},{5,3},{6,0},{7,5},{8,10},{9,15},{10,... | collective-permute-start | bytes 2359304 | tf_op jit(solution)/shard_map/ppermute | solution.py:47
  50.7 3.9 %collective-permute-done.9.refs_8_ = bf16[128,3072]{1,0:T(8,128)(2,1)S(1)} collective-permute-done((bf16[128,3072]{1,0:T(8,128)(2,1)}, bf16[128,3072]{1,0:T(8,128)(2,1)S(1)}, u32[]{:S(2)}, u32[]{:S(2)}) %collective-permute-start.9) | collective-permute-done | bytes 786464 | tf_op jit(solution)/shard_map/ppermute | solution.py:47
  54.6 2.5 %collective-permute-start.11 = (bf16[128,3072]{1,0:T(8,128)(2,1)S(1)}, bf16[128,3072]{1,0:T(8,128)(2,1)S(1)}, u32[]{:S(2)}, u32[]{:S(2)}) collective-permute-start(bf16[128,3072]{1,0:T(8,128)(2,1)S(1)} %collective-permute-done.8.refs_6_), channel_id=1, source_target_pairs={{0,64},{1,65},{2,66},{3,67},{4,68},{5,69},{6,70},{7,71},{8,72},{9,... | collective-permute-start | bytes 2359304 | tf_op jit(solution)/shard_map/ppermute | solution.py:47
  57.1 2.7 %collective-permute-start.12 = (bf16[128,3072]{1,0:T(8,128)(2,1)S(1)}, bf16[128,3072]{1,0:T(8,128)(2,1)S(1)}, u32[]{:S(2)}, u32[]{:S(2)}) collective-permute-start(bf16[128,3072]{1,0:T(8,128)(2,1)S(1)} %collective-permute-done.9.refs_8_), channel_id=1, source_target_pairs={{0,16},{1,49},{2,18},{3,51},{4,20},{5,53},{6,22},{7,55},{8,24},{9,... | collective-permute-start | bytes 2359304 | tf_op jit(solution)/shard_map/ppermute | solution.py:47
  60.2 0.9 copy-done.28
  61.5 0.9 copy-done.24
  63.1 0.9 copy-done.26
  64.0 0.5 copy-done
  64.5 1.9 %copy-done.2 = bf16[512,3072]{1,0:T(8,128)(2,1)S(1)} copy-done((bf16[512,3072]{1,0:T(8,128)(2,1)S(1)}, bf16[512,3072]{1,0:T(8,128)(2,1)}, u32[]{:S(2)}) %copy-start.2) | copy-done | bytes 3145752
  66.4 5.5 %shard_map.75 = (f32[6,2,128,128]{3,2,1,0:T(8,128)S(1)}, f32[6,2,128]{2,1,0:T(2,128)S(1)}) custom-call(s32[16]{0:T(128)S(1)} %min.12.asked_ref, bf16[128,3072]{1,0:T(8,128)(2,1)S(1)} %copy-done.5, bf16[4,128,3072]{2,1,0:T(8,128)(2,1)S(1)} %bitcast.176, bf16[4,128,3072]{2,1,0:T(8,128)(2,1)S(1)} %bitcast.192, ...), custom_call_target="tpu_custom_call" | custom-call | flops 1024 | bytes 1024 | tf_op jit(solution)/shard_map/pallas_call | solution.py:80
  72.0 2.9 %collective-permute-done.14.refs_3_.refs_8_ = bf16[128,3072]{1,0:T(8,128)(2,1)S(1)} collective-permute-done((bf16[128,3072]{1,0:T(8,128)(2,1)S(1)}, bf16[128,3072]{1,0:T(8,128)(2,1)S(1)}, u32[]{:S(2)}, u32[]{:S(2)}) %collective-permute-start.14) | collective-permute-done | bytes 786464 | tf_op jit(solution)/shard_map/ppermute | solution.py:47
  74.9 2.5 %shard_map.76 = (f32[2,2,128,128]{3,2,1,0:T(8,128)S(1)}, f32[2,2,128]{2,1,0:T(2,128)S(1)}) custom-call(s32[16]{0:T(128)S(1)} %min.12.asked_ref, bf16[128,3072]{1,0:T(8,128)(2,1)S(1)} %collective-permute-done.13.refs_0_.refs_4_, bf16[4,128,3072]{2,1,0:T(8,128)(2,1)S(1)} %bitcast.182, bf16[4,128,3072]{2,1,0:T(8,128)(2,1)S(1)} %bitcast.198, ...), custom_call_target="tpu_custom_call" | custom-call | flops 1024 | bytes 1024 | tf_op jit(solution)/shard_map/pallas_call | solution.py:80
  78.9 0.4 copy-done.34
  80.0 1.9 %copy-done.3 = bf16[512,3072]{1,0:T(8,128)(2,1)S(1)} copy-done((bf16[512,3072]{1,0:T(8,128)(2,1)S(1)}, bf16[512,3072]{1,0:T(8,128)(2,1)}, u32[]{:S(2)}) %copy-start.3) | copy-done | bytes 3145752
  81.9 2.1 %shard_map.77 = (bf16[128,3072]{1,0:T(8,128)(2,1)S(1)}, bf16[128,3072]{1,0:T(8,128)(2,1)S(1)}) custom-call(s32[16]{0:T(128)S(1)} %min.12.asked_ref, f32[8,128]{1,0:T(8,128)S(1)} %slice_bitcast_fusion.norm_ref, f32[2,2,128,128]{3,2,1,0:T(8,128)S(1)} %get-tuple-element.46.refs_0_.refs_3_.refs_1_, bf16[4,128,3072]{2,1,0:T(8,128)(2,1)S(1)} %bitcast.184, ...), custom_call_target="tpu_custom_call" | custom-call | flops 1024 | bytes 1024 | tf_op jit(solution)/shard_map/pallas_call | solution.py:80
  84.1 0.4 collective-permute-start.18
  84.5 0.5 collective-permute-start.16
  85.0 2.2 %collective-permute-start.17 = (f32[9,2,128]{2,0,1:T(8,128)S(1)}, f32[9,2,128]{2,0,1:T(8,128)S(1)}, u32[]{:S(2)}, u32[]{:S(2)}) collective-permute-start(f32[9,2,128]{2,0,1:T(8,128)S(1)} %get-tuple-element.81), channel_id=1, source_target_pairs={{0,2},{1,7},{2,4},{3,1},{4,6},{5,3},{6,0},{7,5},{8,10},{9,15},{10,... | collective-permute-start | bytes 27656 | tf_op jit(solution)/shard_map/ppermute | solution.py:47
  87.2 1.5 collective-permute-done.18
  88.8 2.7 %collective-permute-start.19 = (bf16[128,3072]{1,0:T(8,128)(2,1)S(1)}, bf16[128,3072]{1,0:T(8,128)(2,1)S(1)}, u32[]{:S(2)}, u32[]{:S(2)}) collective-permute-start(bf16[128,3072]{1,0:T(8,128)(2,1)S(1)} %get-tuple-element.48), channel_id=1, source_target_pairs={{0,2},{1,7},{2,4},{3,1},{4,6},{5,3},{6,0},{7,5},{8,10},{9,15},{10,... | collective-permute-start | bytes 2359304 | tf_op jit(solution)/shard_map/ppermute | solution.py:47
  91.8 0.4 convolution_convert_fusion.1
  92.2 0.4 convolution_convert_fusion.2
  93.0 2.3 %collective-permute-start.21 = (bf16[128,3072]{1,0:T(8,128)(2,1)S(1)}, bf16[128,3072]{1,0:T(8,128)(2,1)S(1)}, u32[]{:S(2)}, u32[]{:S(2)}) collective-permute-start(bf16[128,3072]{1,0:T(8,128)(2,1)S(1)} %convolution_convert_fusion.3), channel_id=1, source_target_pairs={{0,64},{1,65},{2,66},{3,67},{4,68},{5,69},{6,70},{7,71},{8,72},{9,... | collective-permute-start | bytes 2359304 | tf_op jit(solution)/shard_map/ppermute | solution.py:47
  95.3 1.3 collective-permute-start.23
  96.8 6.1 %shard_map.79 = bf16[4,128,3072]{2,1,0:T(8,128)(2,1)S(1)} custom-call(s32[16]{0:T(128)S(1)} %min.12.asked_ref, f32[8,128]{1,0:T(8,128)S(1)} %fusion.22.norm_ref, f32[6,2,128,128]{3,2,1,0:T(8,128)S(1)} %copy-done.8, f32[2,2,128,128]{3,2,1,0:T(8,128)S(1)} %get-tuple-element.46.refs_0_.refs_3_.refs_1_, bf16[128,3072]{1,0:T(8,128)(2,1)S(1)} %copy-done.6, ...), custom_call_target="tpu_custom_call" | custom-call | flops 1024 | bytes 1024 | tf_op jit(solution)/shard_map/pallas_call | solution.py:80
  103.0 3.8 %collective-permute-done.20.refs_6_ = bf16[128,3072]{1,0:T(8,128)(2,1)S(1)} collective-permute-done((bf16[128,3072]{1,0:T(8,128)(2,1)S(1)}, bf16[128,3072]{1,0:T(8,128)(2,1)S(1)}, u32[]{:S(2)}, u32[]{:S(2)}) %collective-permute-start.20) | collective-permute-done | bytes 786464 | tf_op jit(solution)/shard_map/ppermute | solution.py:47
  106.8 1.7 %collective-permute-done.19.refs_11_ = bf16[128,3072]{1,0:T(8,128)(2,1)S(1)} collective-permute-done((bf16[128,3072]{1,0:T(8,128)(2,1)S(1)}, bf16[128,3072]{1,0:T(8,128)(2,1)S(1)}, u32[]{:S(2)}, u32[]{:S(2)}) %collective-permute-start.19) | collective-permute-done | bytes 786464 | tf_op jit(solution)/shard_map/ppermute | solution.py:47
  108.5 2.2 %shard_map.78 = (bf16[128,3072]{1,0:T(8,128)(2,1)S(1)}, bf16[128,3072]{1,0:T(8,128)(2,1)S(1)}) custom-call(s32[16]{0:T(128)S(1)} %min.12.asked_ref, f32[8,128]{1,0:T(8,128)S(1)} %fusion.22.norm_ref, f32[6,2,128,128]{3,2,1,0:T(8,128)S(1)} %copy-done.8, bf16[4,128,3072]{2,1,0:T(8,128)(2,1)S(1)} %bitcast.186, bf16[4,128,3072]{2,1,0:T(8,128)(2,1)S(1)} %bitcast.202, ...), custom_call_target="tpu_custom_call" | custom-call | flops 1024 | bytes 1024 | tf_op jit(solution)/shard_map/pallas_call | solution.py:80
  110.7 2.9 %collective-permute-done.21 = bf16[128,3072]{1,0:T(8,128)(2,1)S(1)} collective-permute-done((bf16[128,3072]{1,0:T(8,128)(2,1)S(1)}, bf16[128,3072]{1,0:T(8,128)(2,1)S(1)}, u32[]{:S(2)}, u32[]{:S(2)}) %collective-permute-start.21) | collective-permute-done | bytes 786464 | tf_op jit(solution)/shard_map/ppermute | solution.py:47
  113.6 3.2 %collective-permute-done.24 = bf16[128,3072]{1,0:T(8,128)(2,1)S(1)} collective-permute-done((bf16[128,3072]{1,0:T(8,128)(2,1)S(1)}, bf16[128,3072]{1,0:T(8,128)(2,1)S(1)}, u32[]{:S(2)}, u32[]{:S(2)}) %collective-permute-start.24) | collective-permute-done | bytes 786464 | tf_op jit(solution)/shard_map/ppermute | solution.py:47
  117.6 0.7 collective-permute-start.22
  118.4 1.4 collective-permute-start.28
  119.8 0.5 add_convert_fusion
  120.2 0.6 collective-permute-start.31
  120.9 7.9 %collective-permute-done.22 = bf16[128,3072]{1,0:T(8,128)(2,1)S(1)} collective-permute-done((bf16[128,3072]{1,0:T(8,128)(2,1)S(1)}, bf16[128,3072]{1,0:T(8,128)(2,1)S(1)}, u32[]{:S(2)}, u32[]{:S(2)}) %collective-permute-start.22) | collective-permute-done | bytes 786464 | tf_op jit(solution)/shard_map/ppermute | solution.py:47
  128.8 0.4 convolution_convert_fusion
  129.7 2.7 %collective-permute-start.33 = (bf16[128,3072]{1,0:T(8,128)(2,1)S(1)}, bf16[128,3072]{1,0:T(8,128)(2,1)S(1)}, u32[]{:S(2)}, u32[]{:S(2)}) collective-permute-start(bf16[128,3072]{1,0:T(8,128)(2,1)S(1)} %fusion), channel_id=1, source_target_pairs={{0,16},{1,49},{2,18},{3,51},{4,20},{5,53},{6,22},{7,55},{8,24},{9,... | collective-permute-start | bytes 2359304 | tf_op jit(solution)/shard_map/ppermute | solution.py:47
  132.4 0.5 fusion.39
  133.0 3.8 %shard_map.80 = f32[128,3072]{1,0:T(8,128)S(1)} custom-call(s32[16]{0:T(128)S(1)} %min.12.asked_ref, f32[8,128]{1,0:T(8,128)S(1)} %fusion.22.norm_ref, f32[6,2,128,128]{3,2,1,0:T(8,128)S(1)} %copy-done.8, bf16[4,128,3072]{2,1,0:T(8,128)(2,1)S(1)} %bitcast.188, bf16[4,128,3072]{2,1,0:T(8,128)(2,1)S(1)} %bitcast.204, bf16[128,1024]{1,0:T(8,128)(2,1)S(1)} %bitcast.208, ...), custom_call_target="tpu_custom_call" | custom-call | flops 1024 | bytes 1024 | tf_op jit(solution)/shard_map/pallas_call | solution.py:80
  136.8 2.3 %collective-permute-done.28.refs_10_ = bf16[128,3072]{1,0:T(8,128)(2,1)S(1)} collective-permute-done((bf16[128,3072]{1,0:T(8,128)(2,1)S(1)}, bf16[128,3072]{1,0:T(8,128)(2,1)S(1)}, u32[]{:S(2)}, u32[]{:S(2)}) %collective-permute-start.28) | collective-permute-done | bytes 786464 | tf_op jit(solution)/shard_map/ppermute | solution.py:47
  139.1 2.9 %shard_map.82 = (bf16[128,3072]{1,0:T(8,128)(2,1)S(1)}, bf16[128,3072]{1,0:T(8,128)(2,1)S(1)}, bf16[128,3072]{1,0:T(8,128)(2,1)S(1)}) custom-call(s32[16]{0:T(128)S(1)} %min.12.asked_ref, f32[8,128]{1,0:T(8,128)S(1)} %fusion.22.norm_ref, f32[6,2,128,128]{3,2,1,0:T(8,128)S(1)} %copy-done.8, bf16[4,128,3072]{2,1,0:T(8,128)(2,1)S(1)} %bitcast.189, ...), custom_call_target="tpu_custom_call" | custom-call | flops 1024 | bytes 1024 | tf_op jit(solution)/shard_map/pallas_call | solution.py:80
  142.5 1.2 collective-permute-start.30
  144.1 2.7 %collective-permute-done.26 = bf16[128,3072]{1,0:T(8,128)(2,1)S(1)} collective-permute-done((bf16[128,3072]{1,0:T(8,128)(2,1)S(1)}, bf16[128,3072]{1,0:T(8,128)(2,1)S(1)}, u32[]{:S(2)}, u32[]{:S(2)}) %collective-permute-start.26) | collective-permute-done | bytes 786464 | tf_op jit(solution)/shard_map/ppermute | solution.py:47
  146.8 7.4 %shard_map.81 = f32[4,128,3072]{2,1,0:T(8,128)} custom-call(s32[16]{0:T(128)S(1)} %min.12.asked_ref, f32[8,128]{1,0:T(8,128)S(1)} %fusion.22.norm_ref, f32[6,2,128,128]{3,2,1,0:T(8,128)S(1)} %copy-done.8, f32[2,2,128,128]{3,2,1,0:T(8,128)S(1)} %get-tuple-element.46.refs_0_.refs_3_.refs_1_, bf16[128,3072]{1,0:T(8,128)(2,1)S(1)} %copy-done.6, ...), custom_call_target="tpu_custom_call" | custom-call | flops 1024 | bytes 1024 | tf_op jit(solution)/shard_map/pallas_call | solution.py:80
  154.2 1.6 add_multiply_fusion
  155.8 5.1 %collective-permute-done.32 = bf16[128,3072]{1,0:T(8,128)(2,1)S(1)} collective-permute-done((bf16[128,3072]{1,0:T(8,128)(2,1)S(1)}, bf16[128,3072]{1,0:T(8,128)(2,1)S(1)}, u32[]{:S(2)}, u32[]{:S(2)}) %collective-permute-start.32) | collective-permute-done | bytes 786464 | tf_op jit(solution)/shard_map/ppermute | solution.py:47
  160.9 1.6 collective-permute-done.30
  162.5 1.6 add_multiply_fusion.1
  (158 shorter events, 8.0 us)
Async XLA Ops:
  0.6 27.9 %collective-permute-start = (bf16[512,3072]{1,0:T(8,128)(2,1)}, bf16[512,3072]{1,0:T(8,128)(2,1)S(1)}, u32[]{:S(2)}, u32[]{:S(2)}) collective-permute-start(bf16[512,3072]{1,0:T(8,128)(2,1)} %param.6), channel_id=1, source_target_pairs={{0,1},{1,0},{2,3},{3,2},{4,5},{5,4},{6,7},{7,6},{8,9},{9,8},{10,11... | collective-permute-start | bytes 9437192 | tf_op jit(solution)/shard_map/ppermute | solution.py:47
  3.6 11.0 %all-to-all-start = ((s32[16,1,2]{2,1,0:T(1,128)}), s32[16,1,2]{2,1,0:T(1,128)S(1)}, u32[]{:S(2)}, u32[]{:S(2)}) async-start(s32[16,1,2]{2,1,0:T(1,128)} %bitcast.9), calls=%async_computation | async-start | bytes 16384 | tf_op jit(solution)/shard_map/all_to_all | solution.py:236
  9.2 19.4 %collective-permute-start.1 = (bf16[128,3072]{1,0:T(8,128)(2,1)}, bf16[128,3072]{1,0:T(8,128)(2,1)}, u32[]{:S(2)}, u32[]{:S(2)}) collective-permute-start(bf16[128,3072]{1,0:T(8,128)(2,1)} %refs_2_.3), channel_id=1, source_target_pairs={{0,8},{1,9},{2,10},{3,11},{4,12},{5,13},{6,14},{7,15},{8,0},{9,1},... | collective-permute-start | bytes 2359304 | tf_op jit(solution)/shard_map/ppermute | solution.py:47
  15.6 44.2 %copy-start.5 = (bf16[128,3072]{1,0:T(8,128)(2,1)S(1)}, bf16[128,3072]{1,0:T(8,128)(2,1)}, u32[]{:S(2)}) copy-start(bf16[128,3072]{1,0:T(8,128)(2,1)} %refs_2_.3) | copy-start | bytes 2359300
  15.6 13.1 %collective-permute-start.7 = (bf16[128,3072]{1,0:T(8,128)(2,1)}, bf16[128,3072]{1,0:T(8,128)(2,1)S(1)}, u32[]{:S(2)}, u32[]{:S(2)}) collective-permute-start(bf16[128,3072]{1,0:T(8,128)(2,1)} %refs_4_.1), channel_id=1, source_target_pairs={{0,16},{1,49},{2,18},{3,51},{4,20},{5,53},{6,22},{7,55},{8,24},{9,... | collective-permute-start | bytes 2359304 | tf_op jit(solution)/shard_map/ppermute | solution.py:47
  19.4 20.6 %collective-permute-start.3 = (bf16[128,3072]{1,0:T(8,128)(2,1)}, bf16[128,3072]{1,0:T(8,128)(2,1)S(1)}, u32[]{:S(2)}, u32[]{:S(2)}) collective-permute-start(bf16[128,3072]{1,0:T(8,128)(2,1)} %refs_2_.3), channel_id=1, source_target_pairs={{0,6},{1,3},{2,0},{3,5},{4,2},{5,7},{6,4},{7,1},{8,14},{9,11},{10,... | collective-permute-start | bytes 2359304 | tf_op jit(solution)/shard_map/ppermute | solution.py:47
  19.7 20.3 %collective-permute-start.2 = (bf16[128,3072]{1,0:T(8,128)(2,1)}, bf16[128,3072]{1,0:T(8,128)(2,1)S(1)}, u32[]{:S(2)}, u32[]{:S(2)}) collective-permute-start(bf16[128,3072]{1,0:T(8,128)(2,1)} %refs_2_.3), channel_id=1, source_target_pairs={{0,2},{1,7},{2,4},{3,1},{4,6},{5,3},{6,0},{7,5},{8,10},{9,15},{10,... | collective-permute-start | bytes 2359304 | tf_op jit(solution)/shard_map/ppermute | solution.py:47
  28.6 31.6 %copy-start.1 = (bf16[512,3072]{1,0:T(8,128)(2,1)}, bf16[512,3072]{1,0:T(8,128)(2,1)S(1)}, u32[]{:S(2)}) copy-start(bf16[512,3072]{1,0:T(8,128)(2,1)S(1)} %collective-permute-done) | copy-start | bytes 9437188
  28.6 32.8 %copy-start.22 = (bf16[128,3072]{1,0:T(8,128)(2,1)}, bf16[128,3072]{1,0:T(8,128)(2,1)S(1)}, u32[]{:S(2)}) copy-start(bf16[128,3072]{1,0:T(8,128)(2,1)S(1)} %collective-permute-done.7.refs_7_) | copy-start | bytes 2359300
  28.6 20.4 %collective-permute-start.4 = (bf16[128,3072]{1,0:T(8,128)(2,1)}, bf16[128,3072]{1,0:T(8,128)(2,1)S(1)}, u32[]{:S(2)}, u32[]{:S(2)}) collective-permute-start(bf16[128,3072]{1,0:T(8,128)(2,1)} %collective-permute-done.1.refs_3_.refs_6_), channel_id=1, source_target_pairs={{0,2},{1,7},{2,4},{3,1},{4,6},{5,3},{6,0},{7,5},{8,10},{9,15},{10,... | collective-permute-start | bytes 2359304 | tf_op jit(solution)/shard_map/ppermute | solution.py:47
  31.1 19.7 %collective-permute-start.8 = (bf16[128,3072]{1,0:T(8,128)(2,1)S(1)}, bf16[128,3072]{1,0:T(8,128)(2,1)S(1)}, u32[]{:S(2)}, u32[]{:S(2)}) collective-permute-start(bf16[128,3072]{1,0:T(8,128)(2,1)S(1)} %collective-permute-done.7.refs_7_), channel_id=1, source_target_pairs={{0,16},{1,49},{2,18},{3,51},{4,20},{5,53},{6,22},{7,55},{8,24},{9,... | collective-permute-start | bytes 2359304 | tf_op jit(solution)/shard_map/ppermute | solution.py:47
  34.8 19.8 %collective-permute-start.9 = (bf16[128,3072]{1,0:T(8,128)(2,1)}, bf16[128,3072]{1,0:T(8,128)(2,1)S(1)}, u32[]{:S(2)}, u32[]{:S(2)}) collective-permute-start(bf16[128,3072]{1,0:T(8,128)(2,1)} %refs_4_.1), channel_id=1, source_target_pairs={{0,64},{1,65},{2,66},{3,67},{4,68},{5,69},{6,70},{7,71},{8,72},{9,... | collective-permute-start | bytes 2359304 | tf_op jit(solution)/shard_map/ppermute | solution.py:47
  40.0 24.0 %copy-start.13 = (bf16[128,3072]{1,0:T(8,128)(2,1)}, bf16[128,3072]{1,0:T(8,128)(2,1)S(1)}, u32[]{:S(2)}) copy-start(bf16[128,3072]{1,0:T(8,128)(2,1)S(1)} %collective-permute-done.3.refs_9_.refs_3_) | copy-start | bytes 2359300
  40.0 24.0 %copy-start.15 = (bf16[128,3072]{1,0:T(8,128)(2,1)}, bf16[128,3072]{1,0:T(8,128)(2,1)S(1)}, u32[]{:S(2)}) copy-start(bf16[128,3072]{1,0:T(8,128)(2,1)S(1)} %collective-permute-done.2.refs_6_.refs_5_) | copy-start | bytes 2359300
  40.0 14.7 %collective-permute-start.6 = (bf16[128,3072]{1,0:T(8,128)(2,1)}, bf16[128,3072]{1,0:T(8,128)(2,1)S(1)}, u32[]{:S(2)}, u32[]{:S(2)}) collective-permute-start(bf16[128,3072]{1,0:T(8,128)(2,1)} %refs_4_.1), channel_id=1, source_target_pairs={{0,48},{1,17},{2,50},{3,19},{4,52},{5,21},{6,54},{7,23},{8,56},{9,... | collective-permute-start | bytes 2359304 | tf_op jit(solution)/shard_map/ppermute | solution.py:47
  40.1 19.7 %collective-permute-start.5 = (bf16[128,3072]{1,0:T(8,128)(2,1)}, bf16[128,3072]{1,0:T(8,128)(2,1)S(1)}, u32[]{:S(2)}, u32[]{:S(2)}) collective-permute-start(bf16[128,3072]{1,0:T(8,128)(2,1)} %collective-permute-done.1.refs_3_.refs_6_), channel_id=1, source_target_pairs={{0,6},{1,3},{2,0},{3,5},{4,2},{5,7},{6,4},{7,1},{8,14},{9,11},{10,... | collective-permute-start | bytes 2359304 | tf_op jit(solution)/shard_map/ppermute | solution.py:47
  49.1 14.9 %copy-start.17 = (bf16[128,3072]{1,0:T(8,128)(2,1)}, bf16[128,3072]{1,0:T(8,128)(2,1)S(1)}, u32[]{:S(2)}) copy-start(bf16[128,3072]{1,0:T(8,128)(2,1)S(1)} %collective-permute-done.4.refs_12_.refs_9_) | copy-start | bytes 2359300
  49.1 25.8 %collective-permute-start.13 = (bf16[128,3072]{1,0:T(8,128)(2,1)S(1)}, bf16[128,3072]{1,0:T(8,128)(2,1)S(1)}, u32[]{:S(2)}, u32[]{:S(2)}) collective-permute-start(bf16[128,3072]{1,0:T(8,128)(2,1)S(1)} %collective-permute-done.2.refs_6_.refs_5_), channel_id=1, source_target_pairs={{0,2},{1,7},{2,4},{3,1},{4,6},{5,3},{6,0},{7,5},{8,10},{9,15},{10,... | collective-permute-start | bytes 2359304 | tf_op jit(solution)/shard_map/ppermute | solution.py:47
  54.6 22.9 %collective-permute-start.10 = (bf16[128,3072]{1,0:T(8,128)(2,1)S(1)}, bf16[128,3072]{1,0:T(8,128)(2,1)S(1)}, u32[]{:S(2)}, u32[]{:S(2)}) collective-permute-start(bf16[128,3072]{1,0:T(8,128)(2,1)S(1)} %collective-permute-done.9.refs_8_), channel_id=1, source_target_pairs={{0,48},{1,17},{2,50},{3,19},{4,52},{5,21},{6,54},{7,23},{8,56},{9,... | collective-permute-start | bytes 2359304 | tf_op jit(solution)/shard_map/ppermute | solution.py:47
  54.6 23.3 %collective-permute-start.11 = (bf16[128,3072]{1,0:T(8,128)(2,1)S(1)}, bf16[128,3072]{1,0:T(8,128)(2,1)S(1)}, u32[]{:S(2)}, u32[]{:S(2)}) collective-permute-start(bf16[128,3072]{1,0:T(8,128)(2,1)S(1)} %collective-permute-done.8.refs_6_), channel_id=1, source_target_pairs={{0,64},{1,65},{2,66},{3,67},{4,68},{5,69},{6,70},{7,71},{8,72},{9,... | collective-permute-start | bytes 2359304 | tf_op jit(solution)/shard_map/ppermute | solution.py:47
  57.1 21.3 %collective-permute-start.12 = (bf16[128,3072]{1,0:T(8,128)(2,1)S(1)}, bf16[128,3072]{1,0:T(8,128)(2,1)S(1)}, u32[]{:S(2)}, u32[]{:S(2)}) collective-permute-start(bf16[128,3072]{1,0:T(8,128)(2,1)S(1)} %collective-permute-done.9.refs_8_), channel_id=1, source_target_pairs={{0,16},{1,49},{2,18},{3,51},{4,20},{5,53},{6,22},{7,55},{8,24},{9,... | collective-permute-start | bytes 2359304 | tf_op jit(solution)/shard_map/ppermute | solution.py:47
  59.8 4.2 %copy-start.19 = (bf16[128,3072]{1,0:T(8,128)(2,1)}, bf16[128,3072]{1,0:T(8,128)(2,1)S(1)}, u32[]{:S(2)}) copy-start(bf16[128,3072]{1,0:T(8,128)(2,1)S(1)} %collective-permute-done.5.refs_15_.refs_7_) | copy-start | bytes 2359300
  59.8 15.1 %collective-permute-start.14 = (bf16[128,3072]{1,0:T(8,128)(2,1)S(1)}, bf16[128,3072]{1,0:T(8,128)(2,1)S(1)}, u32[]{:S(2)}, u32[]{:S(2)}) collective-permute-start(bf16[128,3072]{1,0:T(8,128)(2,1)S(1)} %collective-permute-done.5.refs_15_.refs_7_), channel_id=1, source_target_pairs={{0,6},{1,3},{2,0},{3,5},{4,2},{5,7},{6,4},{7,1},{8,14},{9,11},{10,... | collective-permute-start | bytes 2359304 | tf_op jit(solution)/shard_map/ppermute | solution.py:47
  62.3 2.2 %copy-start = (bf16[512,3072]{1,0:T(8,128)(2,1)S(1)}, bf16[512,3072]{1,0:T(8,128)(2,1)}, u32[]{:S(2)}) copy-start(bf16[512,3072]{1,0:T(8,128)(2,1)} %param.6) | copy-start | bytes 9437188
  71.9 5.5 %copy-start.7 = (f32[6,2,128,128]{3,2,1,0:T(8,128)}, f32[6,2,128,128]{3,2,1,0:T(8,128)S(1)}, u32[]{:S(2)}) copy-start(f32[6,2,128,128]{3,2,1,0:T(8,128)S(1)} %get-tuple-element.52.refs_0_.refs_3_.refs_6_) | copy-start | bytes 2359300
  74.9 2.6 %copy-start.11 = (bf16[128,3072]{1,0:T(8,128)(2,1)}, bf16[128,3072]{1,0:T(8,128)(2,1)S(1)}, u32[]{:S(2)}) copy-start(bf16[128,3072]{1,0:T(8,128)(2,1)S(1)} %collective-permute-done.14.refs_3_.refs_8_) | copy-start | bytes 2359300
  74.9 2.6 %copy-start.9 = (bf16[128,3072]{1,0:T(8,128)(2,1)}, bf16[128,3072]{1,0:T(8,128)(2,1)S(1)}, u32[]{:S(2)}) copy-start(bf16[128,3072]{1,0:T(8,128)(2,1)S(1)} %collective-permute-done.13.refs_0_.refs_4_) | copy-start | bytes 2359300
  79.7 4.4 %collective-permute-start.15 = (f32[8,2,128]{2,0,1:T(8,128)S(1)}, f32[8,2,128]{2,0,1:T(8,128)S(1)}, u32[]{:S(2)}, u32[]{:S(2)}) collective-permute-start(f32[8,2,128]{2,0,1:T(8,128)S(1)} %concatenate.55), channel_id=1, source_target_pairs={{0,8},{1,9},{2,10},{3,11},{4,12},{5,13},{6,14},{7,15},{8,0},{9,1},... | collective-permute-start | bytes 24584 | tf_op jit(solution)/shard_map/ppermute | solution.py:47
  81.9 9.7 %copy-start.37 = (f32[1024,128]{0,1:T(8,128)S(1)}, f32[1024,128]{0,1:T(8,128)}, u32[]{:S(2)}) copy-start(f32[1024,128]{0,1:T(8,128)} %copy-done.36) | copy-start | bytes 1572868
  81.9 14.8 %copy-start.20 = (bf16[128,3072]{1,0:T(8,128)(2,1)S(1)}, bf16[128,3072]{1,0:T(8,128)(2,1)}, u32[]{:S(2)}) copy-start(bf16[128,3072]{1,0:T(8,128)(2,1)} %copy-done.19) | copy-start | bytes 2359300
  84.0 7.7 %copy-start.6 = (bf16[128,3072]{1,0:T(8,128)(2,1)S(1)}, bf16[128,3072]{1,0:T(8,128)(2,1)}, u32[]{:S(2)}) copy-start(bf16[128,3072]{1,0:T(8,128)(2,1)} %refs_2_.3) | copy-start | bytes 2359300
  84.1 4.6 %collective-permute-start.18 = (f32[8,2,128]{2,0,1:T(8,128)S(1)}, f32[8,2,128]{2,0,1:T(8,128)S(1)}, u32[]{:S(2)}, u32[]{:S(2)}) collective-permute-start(f32[8,2,128]{2,0,1:T(8,128)S(1)} %pad_maximum_fusion.3), channel_id=1, source_target_pairs={{0,4},{1,5},{2,6},{3,7},{4,0},{5,1},{6,2},{7,3},{8,12},{9,13},{10,... | collective-permute-start | bytes 24584 | tf_op jit(solution)/shard_map/ppermute | solution.py:47
  84.5 6.9 %collective-permute-start.16 = (f32[9,2,128]{2,0,1:T(8,128)S(1)}, f32[9,2,128]{2,0,1:T(8,128)S(1)}, u32[]{:S(2)}, u32[]{:S(2)}) collective-permute-start(f32[9,2,128]{2,0,1:T(8,128)S(1)} %get-tuple-element.80), channel_id=1, source_target_pairs={{0,6},{1,3},{2,0},{3,5},{4,2},{5,7},{6,4},{7,1},{8,14},{9,11},{10,... | collective-permute-start | bytes 27656 | tf_op jit(solution)/shard_map/ppermute | solution.py:47
  85.0 6.4 %collective-permute-start.17 = (f32[9,2,128]{2,0,1:T(8,128)S(1)}, f32[9,2,128]{2,0,1:T(8,128)S(1)}, u32[]{:S(2)}, u32[]{:S(2)}) collective-permute-start(f32[9,2,128]{2,0,1:T(8,128)S(1)} %get-tuple-element.81), channel_id=1, source_target_pairs={{0,2},{1,7},{2,4},{3,1},{4,6},{5,3},{6,0},{7,5},{8,10},{9,15},{10,... | collective-permute-start | bytes 27656 | tf_op jit(solution)/shard_map/ppermute | solution.py:47
  88.8 18.0 %collective-permute-start.20 = (bf16[128,3072]{1,0:T(8,128)(2,1)S(1)}, bf16[128,3072]{1,0:T(8,128)(2,1)S(1)}, u32[]{:S(2)}, u32[]{:S(2)}) collective-permute-start(bf16[128,3072]{1,0:T(8,128)(2,1)S(1)} %get-tuple-element.50), channel_id=1, source_target_pairs={{0,6},{1,3},{2,0},{3,5},{4,2},{5,7},{6,4},{7,1},{8,14},{9,11},{10,... | collective-permute-start | bytes 2359304 | tf_op jit(solution)/shard_map/ppermute | solution.py:47
  88.8 19.7 %collective-permute-start.19 = (bf16[128,3072]{1,0:T(8,128)(2,1)S(1)}, bf16[128,3072]{1,0:T(8,128)(2,1)S(1)}, u32[]{:S(2)}, u32[]{:S(2)}) collective-permute-start(bf16[128,3072]{1,0:T(8,128)(2,1)S(1)} %get-tuple-element.48), channel_id=1, source_target_pairs={{0,2},{1,7},{2,4},{3,1},{4,6},{5,3},{6,0},{7,5},{8,10},{9,15},{10,... | collective-permute-start | bytes 2359304 | tf_op jit(solution)/shard_map/ppermute | solution.py:47
  91.8 5.0 %copy-start.16 = (bf16[128,3072]{1,0:T(8,128)(2,1)S(1)}, bf16[128,3072]{1,0:T(8,128)(2,1)}, u32[]{:S(2)}) copy-start(bf16[128,3072]{1,0:T(8,128)(2,1)} %copy-done.15) | copy-start | bytes 2359300
  91.8 5.0 %copy-start.18 = (bf16[128,3072]{1,0:T(8,128)(2,1)S(1)}, bf16[128,3072]{1,0:T(8,128)(2,1)}, u32[]{:S(2)}) copy-start(bf16[128,3072]{1,0:T(8,128)(2,1)} %copy-done.17) | copy-start | bytes 2359300
  92.2 4.6 %copy-start.8 = (f32[6,2,128,128]{3,2,1,0:T(8,128)S(1)}, f32[6,2,128,128]{3,2,1,0:T(8,128)}, u32[]{:S(2)}) copy-start(f32[6,2,128,128]{3,2,1,0:T(8,128)} %copy-done.7) | copy-start | bytes 2359300
  92.2 4.6 %copy-start.10 = (bf16[128,3072]{1,0:T(8,128)(2,1)S(1)}, bf16[128,3072]{1,0:T(8,128)(2,1)}, u32[]{:S(2)}) copy-start(bf16[128,3072]{1,0:T(8,128)(2,1)} %copy-done.9) | copy-start | bytes 2359300
  92.2 4.6 %copy-start.12 = (bf16[128,3072]{1,0:T(8,128)(2,1)S(1)}, bf16[128,3072]{1,0:T(8,128)(2,1)}, u32[]{:S(2)}) copy-start(bf16[128,3072]{1,0:T(8,128)(2,1)} %copy-done.11) | copy-start | bytes 2359300
  92.2 4.6 %copy-start.14 = (bf16[128,3072]{1,0:T(8,128)(2,1)S(1)}, bf16[128,3072]{1,0:T(8,128)(2,1)}, u32[]{:S(2)}) copy-start(bf16[128,3072]{1,0:T(8,128)(2,1)} %copy-done.13) | copy-start | bytes 2359300
  93.0 20.6 %collective-permute-start.21 = (bf16[128,3072]{1,0:T(8,128)(2,1)S(1)}, bf16[128,3072]{1,0:T(8,128)(2,1)S(1)}, u32[]{:S(2)}, u32[]{:S(2)}) collective-permute-start(bf16[128,3072]{1,0:T(8,128)(2,1)S(1)} %convolution_convert_fusion.3), channel_id=1, source_target_pairs={{0,64},{1,65},{2,66},{3,67},{4,68},{5,69},{6,70},{7,71},{8,72},{9,... | collective-permute-start | bytes 2359304 | tf_op jit(solution)/shard_map/ppermute | solution.py:47
  95.3 18.3 %collective-permute-start.23 = (bf16[128,3072]{1,0:T(8,128)(2,1)S(1)}, bf16[128,3072]{1,0:T(8,128)(2,1)S(1)}, u32[]{:S(2)}, u32[]{:S(2)}) collective-permute-start(bf16[128,3072]{1,0:T(8,128)(2,1)S(1)} %convolution_convert_fusion.2), channel_id=1, source_target_pairs={{0,16},{1,49},{2,18},{3,51},{4,20},{5,53},{6,22},{7,55},{8,24},{9,... | collective-permute-start | bytes 2359304 | tf_op jit(solution)/shard_map/ppermute | solution.py:47
  96.6 20.2 %collective-permute-start.24 = (bf16[128,3072]{1,0:T(8,128)(2,1)S(1)}, bf16[128,3072]{1,0:T(8,128)(2,1)S(1)}, u32[]{:S(2)}, u32[]{:S(2)}) collective-permute-start(bf16[128,3072]{1,0:T(8,128)(2,1)S(1)} %convolution_convert_fusion.1), channel_id=1, source_target_pairs={{0,48},{1,17},{2,50},{3,19},{4,52},{5,21},{6,54},{7,23},{8,56},{9,... | collective-permute-start | bytes 2359304 | tf_op jit(solution)/shard_map/ppermute | solution.py:47
  96.8 11.7 %copy-start.4 = (bf16[512,3072]{1,0:T(8,128)(2,1)S(1)}, bf16[512,3072]{1,0:T(8,128)(2,1)}, u32[]{:S(2)}) copy-start(bf16[512,3072]{1,0:T(8,128)(2,1)} %copy-done.1) | copy-start | bytes 9437188
  116.8 12.0 %collective-permute-start.25 = (bf16[4,128,3072]{2,1,0:T(8,128)(2,1)S(1)}, bf16[4,128,3072]{2,1,0:T(8,128)(2,1)S(1)}, u32[]{:S(2)}, u32[]{:S(2)}) collective-permute-start(bf16[4,128,3072]{2,1,0:T(8,128)(2,1)S(1)} %shard_map.79), channel_id=1, source_target_pairs={{0,1},{1,0},{2,3},{3,2},{4,5},{5,4},{6,7},{7,6},{8,9},{9,8},{10,11... | collective-permute-start | bytes 9437192 | tf_op jit(solution)/shard_map/ppermute | solution.py:47
  117.6 11.2 %collective-permute-start.22 = (bf16[128,3072]{1,0:T(8,128)(2,1)S(1)}, bf16[128,3072]{1,0:T(8,128)(2,1)S(1)}, u32[]{:S(2)}, u32[]{:S(2)}) collective-permute-start(bf16[128,3072]{1,0:T(8,128)(2,1)S(1)} %add_convert_fusion.1), channel_id=1, source_target_pairs={{0,16},{1,49},{2,18},{3,51},{4,20},{5,53},{6,22},{7,55},{8,24},{9,... | collective-permute-start | bytes 2359304 | tf_op jit(solution)/shard_map/ppermute | solution.py:47
  118.3 20.8 %collective-permute-start.27 = (bf16[128,3072]{1,0:T(8,128)(2,1)S(1)}, bf16[128,3072]{1,0:T(8,128)(2,1)S(1)}, u32[]{:S(2)}, u32[]{:S(2)}) collective-permute-start(bf16[128,3072]{1,0:T(8,128)(2,1)S(1)} %get-tuple-element.53), channel_id=1, source_target_pairs={{0,2},{1,7},{2,4},{3,1},{4,6},{5,3},{6,0},{7,5},{8,10},{9,15},{10,... | collective-permute-start | bytes 2359304 | tf_op jit(solution)/shard_map/ppermute | solution.py:47
  118.4 20.7 %collective-permute-start.28 = (bf16[128,3072]{1,0:T(8,128)(2,1)S(1)}, bf16[128,3072]{1,0:T(8,128)(2,1)S(1)}, u32[]{:S(2)}, u32[]{:S(2)}) collective-permute-start(bf16[128,3072]{1,0:T(8,128)(2,1)S(1)} %get-tuple-element.60), channel_id=1, source_target_pairs={{0,6},{1,3},{2,0},{3,5},{4,2},{5,7},{6,4},{7,1},{8,14},{9,11},{10,... | collective-permute-start | bytes 2359304 | tf_op jit(solution)/shard_map/ppermute | solution.py:47
  119.8 13.2 %copy-start.31 = (bf16[128,3072]{1,0:T(8,128)(2,1)S(1)}, bf16[128,3072]{1,0:T(8,128)(2,1)}, u32[]{:S(2)}) copy-start(bf16[128,3072]{1,0:T(8,128)(2,1)} %copy-done.30) | copy-start | bytes 2359300
  119.8 13.2 %copy-start.33 = (bf16[128,3072]{1,0:T(8,128)(2,1)S(1)}, bf16[128,3072]{1,0:T(8,128)(2,1)}, u32[]{:S(2)}) copy-start(bf16[128,3072]{1,0:T(8,128)(2,1)} %copy-done.32) | copy-start | bytes 2359300
  119.8 13.2 %copy-start.35 = (bf16[128,3072]{1,0:T(8,128)(2,1)S(1)}, bf16[128,3072]{1,0:T(8,128)(2,1)}, u32[]{:S(2)}) copy-start(bf16[128,3072]{1,0:T(8,128)(2,1)} %copy-done.34) | copy-start | bytes 2359300
  120.2 21.8 %collective-permute-start.31 = (bf16[128,3072]{1,0:T(8,128)(2,1)S(1)}, bf16[128,3072]{1,0:T(8,128)(2,1)S(1)}, u32[]{:S(2)}, u32[]{:S(2)}) collective-permute-start(bf16[128,3072]{1,0:T(8,128)(2,1)S(1)} %add_convert_fusion), channel_id=1, source_target_pairs={{0,64},{1,65},{2,66},{3,67},{4,68},{5,69},{6,70},{7,71},{8,72},{9,... | collective-permute-start | bytes 2359304 | tf_op jit(solution)/shard_map/ppermute | solution.py:47
  128.8 4.2 %copy-start.27 = (bf16[128,3072]{1,0:T(8,128)(2,1)S(1)}, bf16[128,3072]{1,0:T(8,128)(2,1)}, u32[]{:S(2)}) copy-start(bf16[128,3072]{1,0:T(8,128)(2,1)} %copy-done.26) | copy-start | bytes 2359300
  128.8 4.2 %copy-start.29 = (bf16[128,3072]{1,0:T(8,128)(2,1)S(1)}, bf16[128,3072]{1,0:T(8,128)(2,1)}, u32[]{:S(2)}) copy-start(bf16[128,3072]{1,0:T(8,128)(2,1)} %copy-done.28) | copy-start | bytes 2359300
  129.2 3.8 %copy-start.21 = (bf16[128,3072]{1,0:T(8,128)(2,1)S(1)}, bf16[128,3072]{1,0:T(8,128)(2,1)}, u32[]{:S(2)}) copy-start(bf16[128,3072]{1,0:T(8,128)(2,1)} %refs_4_.1) | copy-start | bytes 2359300
  129.2 3.8 %copy-start.23 = (bf16[128,3072]{1,0:T(8,128)(2,1)S(1)}, bf16[128,3072]{1,0:T(8,128)(2,1)}, u32[]{:S(2)}) copy-start(bf16[128,3072]{1,0:T(8,128)(2,1)} %copy-done.22) | copy-start | bytes 2359300
  129.2 3.8 %copy-start.25 = (bf16[128,3072]{1,0:T(8,128)(2,1)S(1)}, bf16[128,3072]{1,0:T(8,128)(2,1)}, u32[]{:S(2)}) copy-start(bf16[128,3072]{1,0:T(8,128)(2,1)} %copy-done.24) | copy-start | bytes 2359300
  129.2 17.6 %collective-permute-start.26 = (bf16[128,3072]{1,0:T(8,128)(2,1)S(1)}, bf16[128,3072]{1,0:T(8,128)(2,1)S(1)}, u32[]{:S(2)}, u32[]{:S(2)}) collective-permute-start(bf16[128,3072]{1,0:T(8,128)(2,1)S(1)} %convolution_convert_fusion), channel_id=1, source_target_pairs={{0,48},{1,17},{2,50},{3,19},{4,52},{5,21},{6,54},{7,23},{8,56},{9,... | collective-permute-start | bytes 2359304 | tf_op jit(solution)/shard_map/ppermute | solution.py:47
  129.7 24.5 %collective-permute-start.33 = (bf16[128,3072]{1,0:T(8,128)(2,1)S(1)}, bf16[128,3072]{1,0:T(8,128)(2,1)S(1)}, u32[]{:S(2)}, u32[]{:S(2)}) collective-permute-start(bf16[128,3072]{1,0:T(8,128)(2,1)S(1)} %fusion), channel_id=1, source_target_pairs={{0,16},{1,49},{2,18},{3,51},{4,20},{5,53},{6,22},{7,55},{8,24},{9,... | collective-permute-start | bytes 2359304 | tf_op jit(solution)/shard_map/ppermute | solution.py:47
  142.0 18.9 %collective-permute-start.32 = (bf16[128,3072]{1,0:T(8,128)(2,1)S(1)}, bf16[128,3072]{1,0:T(8,128)(2,1)S(1)}, u32[]{:S(2)}, u32[]{:S(2)}) collective-permute-start(bf16[128,3072]{1,0:T(8,128)(2,1)S(1)} %get-tuple-element.65), channel_id=1, source_target_pairs={{0,8},{1,9},{2,10},{3,11},{4,12},{5,13},{6,14},{7,15},{8,0},{9,1},... | collective-permute-start | bytes 2359304 | tf_op jit(solution)/shard_map/ppermute | solution.py:47
  142.3 18.7 %collective-permute-start.29 = (bf16[128,3072]{1,0:T(8,128)(2,1)S(1)}, bf16[128,3072]{1,0:T(8,128)(2,1)S(1)}, u32[]{:S(2)}, u32[]{:S(2)}) collective-permute-start(bf16[128,3072]{1,0:T(8,128)(2,1)S(1)} %get-tuple-element.62), channel_id=1, source_target_pairs={{0,2},{1,7},{2,4},{3,1},{4,6},{5,3},{6,0},{7,5},{8,10},{9,15},{10,... | collective-permute-start | bytes 2359304 | tf_op jit(solution)/shard_map/ppermute | solution.py:47
  142.5 20.0 %collective-permute-start.30 = (bf16[128,3072]{1,0:T(8,128)(2,1)S(1)}, bf16[128,3072]{1,0:T(8,128)(2,1)S(1)}, u32[]{:S(2)}, u32[]{:S(2)}) collective-permute-start(bf16[128,3072]{1,0:T(8,128)(2,1)S(1)} %get-tuple-element.63), channel_id=1, source_target_pairs={{0,6},{1,3},{2,0},{3,5},{4,2},{5,7},{6,4},{7,1},{8,14},{9,11},{10,... | collective-permute-start | bytes 2359304 | tf_op jit(solution)/shard_map/ppermute | solution.py:47
  (9 other events, 10.0 us)

commit v2 on v1

--- a/solution.py
+++ b/solution.py
@@ -12,7 +12,7 @@
 OUT_SCALE = 0.25
 LOW = -1e30
 CHUNK = 512
-WIDE = 1024
+WIDE = 1536
 AXES = ("blk", "dp")
 F32 = jnp.float32
 BF16 = jnp.bfloat16
@@ -83,7 +83,7 @@
             num_scalar_prefetch=1, grid=(steps,), in_specs=specs, out_specs=out_spec, scratch_shapes=scratch
         ),
         out_shape=out,
-        compiler_params=pltpu.CompilerParams(vmem_limit_bytes=13 * 1024 * 1024),
+        compiler_params=pltpu.CompilerParams(vmem_limit_bytes=18 * 1024 * 1024),
         cost_estimate=pl.CostEstimate(flops=1024, bytes_accessed=1024, transcendentals=0),
     )(slots, *arrays)
 
@@ -226,18 +226,19 @@
     held = corpus.shape[0] // BLOCK
     mult = SCALE / math.sqrt(width)
     me = lax.axis_index("dp")
-    mx, my, mc = me // 8, (me // 2) % 4, me % 2
-    turn = 1 - 2 * mc
+    turn = 1 - 2 * (me % 2)
 
     owner = hard_ids[0] // held % 16
     matches = owner[:, None] == jnp.arange(16, dtype=jnp.int32)[None, :]
     wanted = jnp.sum(jnp.where(matches, (hard_ids[0] % held)[:, None] + 1, 0), axis=0) - 1
-    pairs = jnp.repeat(wanted.reshape(8, 1, 2), 2, axis=1).reshape(16, 2)
-    asked = lax.all_to_all(pairs, "dp", split_axis=0, concat_axis=0, tiled=True)
-    spot_place = jnp.stack([((mx + a) % 2) * 4 + (my + turn * b) % 4 for a, b in SPOTS])
-    asked = jnp.take(asked.reshape(8, 2, 2), spot_place, axis=0)
-    asked = lax.dynamic_index_in_dim(asked, mc, 1, keepdims=False)
-    asked = jnp.where(mc == 0, asked, asked[:, ::-1])
+    pair = wanted[None]
+    pair = cat(pair, send(pair, X_LO))
+    ring = (pair, send(pair, Y_BWD), send(pair, Y_TWO), send(pair, Y_FWD))
+    known = jnp.stack(ring, axis=1).reshape(8, 16)
+    every = jnp.arange(16, dtype=jnp.int32)[None, :]
+    asked = jnp.stack(
+        [jnp.sum(jnp.where(every == place, known, 0), axis=1) for place in (me, me + turn)], axis=1
+    )
     asked = jnp.clip(asked.reshape(16), -1, held - 1)
 
     q, p = {(0, 0): queries}, {(0, 0): positives}

time: 165 us -> 162 us (0.982)
  starting transfers between devices: 48 us -> 54.1 us
  waiting for transfers between devices: 59.6 us -> 54 us
  Pallas kernels: 32.6 us -> 30.8 us
    ppermute x34 -> x38, starting transfers between devices: 42.4 us -> 54.1 us  [send(): return lax.ppermute(value, AXES, route)]
    all_to_all x1 -> x0, starting transfers between devices: 5.61 us -> none  [local(): asked = lax.all_to_all(pairs, 'dp', split_axis=0, concat_axis=0, tiled=True)]
    all_to_all x1 -> x0, waiting for transfers between devices: 3.81 us -> none  [local(): asked = lax.all_to_all(pairs, 'dp', split_axis=0, concat_axis=0, tiled=True)]
    ppermute x34 -> x38, waiting for transfers between devices: 55.8 us -> 54 us  [send(): return lax.ppermute(value, AXES, route)]
    pallas_call x8, Pallas kernels: 32.6 us -> 30.8 us  [kernel(): pl.pallas_call(body, grid_spec=pltpu.PrefetchScalarGridSpec(num_scalar_pr...]
  transfers between devices with their start and end apart: 35 -> 38, of which waited for: 17 -> 20; matrix products, arithmetic and copies ran while one was open for 8% -> 7% of each run, Pallas kernels for 20% -> 19%
where the time goes in v2:
time: 162 us; the launch traced here: 161 us
  starting transfers between devices  54.1 us (33%)
  waiting for transfers between devices  54 us (33%)
  Pallas kernels  30.8 us (19%)
  local copies, waits for them, and re-layouts  8.24 us (5%)
  matrix products  7.59 us (5%)
  other arithmetic  5.31 us (3%)
    ppermute x38, starting transfers between devices, send(): return lax.ppermute(value, AXES, route)  54.1 us
    ppermute x38, waiting for transfers between devices, send(): return lax.ppermute(value, AXES, route)  54 us
    pallas_call x8, Pallas kernels, kernel(): pl.pallas_call(body, grid_spec=pltpu.PrefetchScalarGridSpec(num_scalar_pr...  30.8 us
    unnamed x76, local copies, waits for them, and re-layouts  7.61 us
    dot_general x8, matrix products, rows_dot(): lax.dot_general(left, right, (((1,), (1,)), ((), ())), preferred_element_...  4.34 us
    dot_general x8, matrix products, mm(): return jnp.dot(left, right, preferred_element_type=F32)  3.25 us
  transfers between devices with their start and end apart: 38, of which 20 were waited for; matrix products, arithmetic and copies ran while one was open for 7% of the time, Pallas kernels for 19%

profile of v2, /device:TPU:1, one launch (start us, length us, event | category | flops | bytes accessed | tf_op | source)
XLA Modules:
  0.0 161.4 jit_solution(11144967218937729153)
XLA Ops:
  0.6 1.5 collective-permute-start.4
  2.1 0.7 and_select_fusion.1
  2.9 1.4 collective-permute-start
  4.5 0.9 collective-permute-done
  5.4 3.1 %collective-permute-start.2 = (s32[2,16]{1,0:T(2,128)S(1)}, s32[2,16]{1,0:T(2,128)S(1)}, u32[]{:S(2)}, u32[]{:S(2)}) collective-permute-start(s32[2,16]{1,0:T(2,128)S(1)} %get-tuple-element.91), channel_id=1, source_target_pairs={{0,4},{1,5},{2,6},{3,7},{4,0},{5,1},{6,2},{7,3},{8,12},{9,13},{10,... | collective-permute-start | bytes 392 | tf_op jit(solution)/shard_map/ppermute | solution.py:47
  8.8 2.3 %collective-permute-start.3 = (s32[2,16]{1,0:T(2,128)S(1)}, s32[2,16]{1,0:T(2,128)S(1)}, u32[]{:S(2)}, u32[]{:S(2)}) collective-permute-start(s32[2,16]{1,0:T(2,128)S(1)} %get-tuple-element.91), channel_id=1, source_target_pairs={{0,2},{1,7},{2,4},{3,1},{4,6},{5,3},{6,0},{7,5},{8,10},{9,15},{10,... | collective-permute-start | bytes 392 | tf_op jit(solution)/shard_map/ppermute | solution.py:47
  11.1 0.9 collective-permute-done.1
  12.8 3.8 %collective-permute-start.11 = (bf16[128,3072]{1,0:T(8,128)(2,1)}, bf16[128,3072]{1,0:T(8,128)(2,1)S(1)}, u32[]{:S(2)}, u32[]{:S(2)}) collective-permute-start(bf16[128,3072]{1,0:T(8,128)(2,1)} %refs_4_.1), channel_id=1, source_target_pairs={{0,16},{1,49},{2,18},{3,51},{4,20},{5,53},{6,22},{7,55},{8,24},{9,... | collective-permute-start | bytes 2359304 | tf_op jit(solution)/shard_map/ppermute | solution.py:47
  16.7 3.0 %collective-permute-start.6 = (bf16[128,3072]{1,0:T(8,128)(2,1)}, bf16[128,3072]{1,0:T(8,128)(2,1)S(1)}, u32[]{:S(2)}, u32[]{:S(2)}) collective-permute-start(bf16[128,3072]{1,0:T(8,128)(2,1)} %refs_2_.3), channel_id=1, source_target_pairs={{0,2},{1,7},{2,4},{3,1},{4,6},{5,3},{6,0},{7,5},{8,10},{9,15},{10,... | collective-permute-start | bytes 2359304 | tf_op jit(solution)/shard_map/ppermute | solution.py:47
  19.6 3.8 %collective-permute-done.5.refs_3_.refs_6_ = bf16[128,3072]{1,0:T(8,128)(2,1)} collective-permute-done((bf16[128,3072]{1,0:T(8,128)(2,1)}, bf16[128,3072]{1,0:T(8,128)(2,1)}, u32[]{:S(2)}, u32[]{:S(2)}) %collective-permute-start.5) | collective-permute-done | bytes 786464 | tf_op jit(solution)/shard_map/ppermute | solution.py:47
  23.4 2.5 %collective-permute-done.11.refs_7_ = bf16[128,3072]{1,0:T(8,128)(2,1)S(1)} collective-permute-done((bf16[128,3072]{1,0:T(8,128)(2,1)}, bf16[128,3072]{1,0:T(8,128)(2,1)S(1)}, u32[]{:S(2)}, u32[]{:S(2)}) %collective-permute-start.11) | collective-permute-done | bytes 786464 | tf_op jit(solution)/shard_map/ppermute | solution.py:47
  25.9 3.0 %collective-permute-start.8 = (bf16[128,3072]{1,0:T(8,128)(2,1)}, bf16[128,3072]{1,0:T(8,128)(2,1)S(1)}, u32[]{:S(2)}, u32[]{:S(2)}) collective-permute-start(bf16[128,3072]{1,0:T(8,128)(2,1)} %collective-permute-done.5.refs_3_.refs_6_), channel_id=1, source_target_pairs={{0,2},{1,7},{2,4},{3,1},{4,6},{5,3},{6,0},{7,5},{8,10},{9,15},{10,... | collective-permute-start | bytes 2359304 | tf_op jit(solution)/shard_map/ppermute | solution.py:47
  28.9 3.3 %collective-permute-start.12 = (bf16[128,3072]{1,0:T(8,128)(2,1)S(1)}, bf16[128,3072]{1,0:T(8,128)(2,1)S(1)}, u32[]{:S(2)}, u32[]{:S(2)}) collective-permute-start(bf16[128,3072]{1,0:T(8,128)(2,1)S(1)} %collective-permute-done.11.refs_7_), channel_id=1, source_target_pairs={{0,16},{1,49},{2,18},{3,51},{4,20},{5,53},{6,22},{7,55},{8,24},{9,... | collective-permute-start | bytes 2359304 | tf_op jit(solution)/shard_map/ppermute | solution.py:47
  32.2 2.7 %collective-permute-start.13 = (bf16[128,3072]{1,0:T(8,128)(2,1)}, bf16[128,3072]{1,0:T(8,128)(2,1)S(1)}, u32[]{:S(2)}, u32[]{:S(2)}) collective-permute-start(bf16[128,3072]{1,0:T(8,128)(2,1)} %refs_4_.1), channel_id=1, source_target_pairs={{0,64},{1,65},{2,66},{3,67},{4,68},{5,69},{6,70},{7,71},{8,72},{9,... | collective-permute-start | bytes 2359304 | tf_op jit(solution)/shard_map/ppermute | solution.py:47
  34.9 1.0 collective-permute-done.7.refs_9_.refs_3_
  35.9 0.4 collective-permute-done.6.refs_6_.refs_5_
  36.3 1.8 %collective-permute-start.9 = (bf16[128,3072]{1,0:T(8,128)(2,1)}, bf16[128,3072]{1,0:T(8,128)(2,1)S(1)}, u32[]{:S(2)}, u32[]{:S(2)}) collective-permute-start(bf16[128,3072]{1,0:T(8,128)(2,1)} %collective-permute-done.5.refs_3_.refs_6_), channel_id=1, source_target_pairs={{0,6},{1,3},{2,0},{3,5},{4,2},{5,7},{6,4},{7,1},{8,14},{9,11},{10,... | collective-permute-start | bytes 2359304 | tf_op jit(solution)/shard_map/ppermute | solution.py:47
  38.2 1.7 %convolution_dynamic-update-slice_fusion.7 = f32[1024,128]{0,1:T(8,128)S(1)} fusion(bf16[128,3072]{1,0:T(8,128)(2,1)} %refs_4_.1, bf16[128,3072]{1,0:T(8,128)(2,1)} %refs_2_.3), kind=kOutput, calls=%fused_computation.17 | convolution fusion | flops 100663296 | bytes 1638400 | tf_op jit(solution)/shard_map/dot_general | solution.py:59
  39.9 6.0 %collective-permute-done.8.refs_12_.refs_9_ = bf16[128,3072]{1,0:T(8,128)(2,1)S(1)} collective-permute-done((bf16[128,3072]{1,0:T(8,128)(2,1)}, bf16[128,3072]{1,0:T(8,128)(2,1)S(1)}, u32[]{:S(2)}, u32[]{:S(2)}) %collective-permute-start.8) | collective-permute-done | bytes 786464 | tf_op jit(solution)/shard_map/ppermute | solution.py:47
  45.9 3.3 %collective-permute-start.17 = (bf16[128,3072]{1,0:T(8,128)(2,1)S(1)}, bf16[128,3072]{1,0:T(8,128)(2,1)S(1)}, u32[]{:S(2)}, u32[]{:S(2)}) collective-permute-start(bf16[128,3072]{1,0:T(8,128)(2,1)S(1)} %collective-permute-done.6.refs_6_.refs_5_), channel_id=1, source_target_pairs={{0,2},{1,7},{2,4},{3,1},{4,6},{5,3},{6,0},{7,5},{8,10},{9,15},{10,... | collective-permute-start | bytes 2359304 | tf_op jit(solution)/shard_map/ppermute | solution.py:47
  49.2 3.1 %collective-permute-done.13.refs_8_ = bf16[128,3072]{1,0:T(8,128)(2,1)S(1)} collective-permute-done((bf16[128,3072]{1,0:T(8,128)(2,1)}, bf16[128,3072]{1,0:T(8,128)(2,1)S(1)}, u32[]{:S(2)}, u32[]{:S(2)}) %collective-permute-start.13) | collective-permute-done | bytes 786464 | tf_op jit(solution)/shard_map/ppermute | solution.py:47
  52.3 2.7 %collective-permute-start.15 = (bf16[128,3072]{1,0:T(8,128)(2,1)S(1)}, bf16[128,3072]{1,0:T(8,128)(2,1)S(1)}, u32[]{:S(2)}, u32[]{:S(2)}) collective-permute-start(bf16[128,3072]{1,0:T(8,128)(2,1)S(1)} %collective-permute-done.12.refs_6_), channel_id=1, source_target_pairs={{0,64},{1,65},{2,66},{3,67},{4,68},{5,69},{6,70},{7,71},{8,72},{9,... | collective-permute-start | bytes 2359304 | tf_op jit(solution)/shard_map/ppermute | solution.py:47
  55.0 2.7 %collective-permute-start.16 = (bf16[128,3072]{1,0:T(8,128)(2,1)S(1)}, bf16[128,3072]{1,0:T(8,128)(2,1)S(1)}, u32[]{:S(2)}, u32[]{:S(2)}) collective-permute-start(bf16[128,3072]{1,0:T(8,128)(2,1)S(1)} %collective-permute-done.13.refs_8_), channel_id=1, source_target_pairs={{0,16},{1,49},{2,18},{3,51},{4,20},{5,53},{6,22},{7,55},{8,24},{9,... | collective-permute-start | bytes 2359304 | tf_op jit(solution)/shard_map/ppermute | solution.py:47
  58.1 0.9 copy-done.28
  59.4 0.9 copy-done.24
  61.1 0.9 copy-done.26
  62.0 0.5 copy-done
  62.5 1.9 %copy-done.2 = bf16[512,3072]{1,0:T(8,128)(2,1)S(1)} copy-done((bf16[512,3072]{1,0:T(8,128)(2,1)S(1)}, bf16[512,3072]{1,0:T(8,128)(2,1)}, u32[]{:S(2)}) %copy-start.2) | copy-done | bytes 3145752
  64.4 5.0 %shard_map.75 = (f32[6,2,128,128]{3,2,1,0:T(8,128)S(1)}, f32[6,2,128]{2,1,0:T(2,128)S(1)}) custom-call(s32[16]{0:T(128)S(1)} %min.12.asked_ref, bf16[128,3072]{1,0:T(8,128)(2,1)S(1)} %copy-done.5, bf16[4,128,3072]{2,1,0:T(8,128)(2,1)S(1)} %bitcast.161, bf16[4,128,3072]{2,1,0:T(8,128)(2,1)S(1)} %bitcast.177, ...), custom_call_target="tpu_custom_call" | custom-call | flops 1024 | bytes 1024 | tf_op jit(solution)/shard_map/pallas_call | solution.py:80
  69.5 3.7 %collective-permute-done.18.refs_3_.refs_8_ = bf16[128,3072]{1,0:T(8,128)(2,1)S(1)} collective-permute-done((bf16[128,3072]{1,0:T(8,128)(2,1)S(1)}, bf16[128,3072]{1,0:T(8,128)(2,1)S(1)}, u32[]{:S(2)}, u32[]{:S(2)}) %collective-permute-start.18) | collective-permute-done | bytes 786464 | tf_op jit(solution)/shard_map/ppermute | solution.py:47
  73.2 2.3 %shard_map.76 = (f32[2,2,128,128]{3,2,1,0:T(8,128)S(1)}, f32[2,2,128]{2,1,0:T(2,128)S(1)}) custom-call(s32[16]{0:T(128)S(1)} %min.12.asked_ref, bf16[128,3072]{1,0:T(8,128)(2,1)S(1)} %collective-permute-done.17.refs_0_.refs_4_, bf16[4,128,3072]{2,1,0:T(8,128)(2,1)S(1)} %bitcast.167, bf16[4,128,3072]{2,1,0:T(8,128)(2,1)S(1)} %bitcast.183, ...), custom_call_target="tpu_custom_call" | custom-call | flops 1024 | bytes 1024 | tf_op jit(solution)/shard_map/pallas_call | solution.py:80
  77.7 0.7 collective-permute-start.19
  78.4 1.9 %copy-done.3 = bf16[512,3072]{1,0:T(8,128)(2,1)S(1)} copy-done((bf16[512,3072]{1,0:T(8,128)(2,1)S(1)}, bf16[512,3072]{1,0:T(8,128)(2,1)}, u32[]{:S(2)}) %copy-start.3) | copy-done | bytes 3145752
  80.3 1.9 %shard_map.77 = (bf16[128,3072]{1,0:T(8,128)(2,1)S(1)}, bf16[128,3072]{1,0:T(8,128)(2,1)S(1)}) custom-call(s32[16]{0:T(128)S(1)} %min.12.asked_ref, f32[8,128]{1,0:T(8,128)S(1)} %slice_bitcast_fusion.norm_ref, f32[2,2,128,128]{3,2,1,0:T(8,128)S(1)} %get-tuple-element.46.refs_0_.refs_3_.refs_1_, bf16[4,128,3072]{2,1,0:T(8,128)(2,1)S(1)} %bitcast.169, ...), custom_call_target="tpu_custom_call" | custom-call | flops 1024 | bytes 1024 | tf_op jit(solution)/shard_map/pallas_call | solution.py:80
  82.4 0.8 collective-permute-start.20
  83.2 1.9 %collective-permute-start.21 = (f32[9,2,128]{2,0,1:T(8,128)S(1)}, f32[9,2,128]{2,0,1:T(8,128)S(1)}, u32[]{:S(2)}, u32[]{:S(2)}) collective-permute-start(f32[9,2,128]{2,0,1:T(8,128)S(1)} %get-tuple-element.83), channel_id=1, source_target_pairs={{0,2},{1,7},{2,4},{3,1},{4,6},{5,3},{6,0},{7,5},{8,10},{9,15},{10,... | collective-permute-start | bytes 27656 | tf_op jit(solution)/shard_map/ppermute | solution.py:47
  85.1 1.2 collective-permute-done.22
  86.4 2.7 %collective-permute-start.23 = (bf16[128,3072]{1,0:T(8,128)(2,1)S(1)}, bf16[128,3072]{1,0:T(8,128)(2,1)S(1)}, u32[]{:S(2)}, u32[]{:S(2)}) collective-permute-start(bf16[128,3072]{1,0:T(8,128)(2,1)S(1)} %get-tuple-element.48), channel_id=1, source_target_pairs={{0,2},{1,7},{2,4},{3,1},{4,6},{5,3},{6,0},{7,5},{8,10},{9,15},{10,... | collective-permute-start | bytes 2359304 | tf_op jit(solution)/shard_map/ppermute | solution.py:47
  90.6 3.2 %collective-permute-start.25 = (bf16[128,3072]{1,0:T(8,128)(2,1)S(1)}, bf16[128,3072]{1,0:T(8,128)(2,1)S(1)}, u32[]{:S(2)}, u32[]{:S(2)}) collective-permute-start(bf16[128,3072]{1,0:T(8,128)(2,1)S(1)} %convolution_convert_fusion.3), channel_id=1, source_target_pairs={{0,64},{1,65},{2,66},{3,67},{4,68},{5,69},{6,70},{7,71},{8,72},{9,... | collective-permute-start | bytes 2359304 | tf_op jit(solution)/shard_map/ppermute | solution.py:47
  93.9 1.5 collective-permute-start.28
  95.4 6.1 %shard_map.79 = bf16[4,128,3072]{2,1,0:T(8,128)(2,1)S(1)} custom-call(s32[16]{0:T(128)S(1)} %min.12.asked_ref, f32[8,128]{1,0:T(8,128)S(1)} %fusion.22.norm_ref, f32[6,2,128,128]{3,2,1,0:T(8,128)S(1)} %copy-done.8, f32[2,2,128,128]{3,2,1,0:T(8,128)S(1)} %get-tuple-element.46.refs_0_.refs_3_.refs_1_, bf16[128,3072]{1,0:T(8,128)(2,1)S(1)} %copy-done.6, ...), custom_call_target="tpu_custom_call" | custom-call | flops 1024 | bytes 1024 | tf_op jit(solution)/shard_map/pallas_call | solution.py:80
  101.5 2.3 %collective-permute-done.24.refs_6_ = bf16[128,3072]{1,0:T(8,128)(2,1)S(1)} collective-permute-done((bf16[128,3072]{1,0:T(8,128)(2,1)S(1)}, bf16[128,3072]{1,0:T(8,128)(2,1)S(1)}, u32[]{:S(2)}, u32[]{:S(2)}) %collective-permute-start.24) | collective-permute-done | bytes 786464 | tf_op jit(solution)/shard_map/ppermute | solution.py:47
  103.8 2.4 %collective-permute-done.23.refs_11_ = bf16[128,3072]{1,0:T(8,128)(2,1)S(1)} collective-permute-done((bf16[128,3072]{1,0:T(8,128)(2,1)S(1)}, bf16[128,3072]{1,0:T(8,128)(2,1)S(1)}, u32[]{:S(2)}, u32[]{:S(2)}) %collective-permute-start.23) | collective-permute-done | bytes 786464 | tf_op jit(solution)/shard_map/ppermute | solution.py:47
  106.2 2.0 %shard_map.78 = (bf16[128,3072]{1,0:T(8,128)(2,1)S(1)}, bf16[128,3072]{1,0:T(8,128)(2,1)S(1)}) custom-call(s32[16]{0:T(128)S(1)} %min.12.asked_ref, f32[8,128]{1,0:T(8,128)S(1)} %fusion.22.norm_ref, f32[6,2,128,128]{3,2,1,0:T(8,128)S(1)} %copy-done.8, bf16[4,128,3072]{2,1,0:T(8,128)(2,1)S(1)} %bitcast.171, bf16[4,128,3072]{2,1,0:T(8,128)(2,1)S(1)} %bitcast.187, ...), custom_call_target="tpu_custom_call" | custom-call | flops 1024 | bytes 1024 | tf_op jit(solution)/shard_map/pallas_call | solution.py:80
  108.1 2.3 %collective-permute-done.25 = bf16[128,3072]{1,0:T(8,128)(2,1)S(1)} collective-permute-done((bf16[128,3072]{1,0:T(8,128)(2,1)S(1)}, bf16[128,3072]{1,0:T(8,128)(2,1)S(1)}, u32[]{:S(2)}, u32[]{:S(2)}) %collective-permute-start.25) | collective-permute-done | bytes 786464 | tf_op jit(solution)/shard_map/ppermute | solution.py:47
  110.5 1.7 %collective-permute-done.27 = bf16[128,3072]{1,0:T(8,128)(2,1)S(1)} collective-permute-done((bf16[128,3072]{1,0:T(8,128)(2,1)S(1)}, bf16[128,3072]{1,0:T(8,128)(2,1)S(1)}, u32[]{:S(2)}, u32[]{:S(2)}) %collective-permute-start.27) | collective-permute-done | bytes 786464 | tf_op jit(solution)/shard_map/ppermute | solution.py:47
  112.2 1.2 collective-permute-done.28
  113.4 1.6 %collective-permute-start.29 = (bf16[4,128,3072]{2,1,0:T(8,128)(2,1)S(1)}, bf16[4,128,3072]{2,1,0:T(8,128)(2,1)S(1)}, u32[]{:S(2)}, u32[]{:S(2)}) collective-permute-start(bf16[4,128,3072]{2,1,0:T(8,128)(2,1)S(1)} %shard_map.79), channel_id=1, source_target_pairs={{0,1},{1,0},{2,3},{3,2},{4,5},{5,4},{6,7},{7,6},{8,9},{9,8},{10,11... | collective-permute-start | bytes 9437192 | tf_op jit(solution)/shard_map/ppermute | solution.py:47
  115.8 1.3 collective-permute-start.32
  117.1 0.5 add_convert_fusion
  117.9 8.7 %collective-permute-done.26 = bf16[128,3072]{1,0:T(8,128)(2,1)S(1)} collective-permute-done((bf16[128,3072]{1,0:T(8,128)(2,1)S(1)}, bf16[128,3072]{1,0:T(8,128)(2,1)S(1)}, u32[]{:S(2)}, u32[]{:S(2)}) %collective-permute-start.26) | collective-permute-done | bytes 786464 | tf_op jit(solution)/shard_map/ppermute | solution.py:47
  127.6 2.7 %collective-permute-start.37 = (bf16[128,3072]{1,0:T(8,128)(2,1)S(1)}, bf16[128,3072]{1,0:T(8,128)(2,1)S(1)}, u32[]{:S(2)}, u32[]{:S(2)}) collective-permute-start(bf16[128,3072]{1,0:T(8,128)(2,1)S(1)} %fusion), channel_id=1, source_target_pairs={{0,16},{1,49},{2,18},{3,51},{4,20},{5,53},{6,22},{7,55},{8,24},{9,... | collective-permute-start | bytes 2359304 | tf_op jit(solution)/shard_map/ppermute | solution.py:47
  130.3 0.5 fusion.38
  130.9 3.5 %shard_map.80 = f32[128,3072]{1,0:T(8,128)S(1)} custom-call(s32[16]{0:T(128)S(1)} %min.12.asked_ref, f32[8,128]{1,0:T(8,128)S(1)} %fusion.22.norm_ref, f32[6,2,128,128]{3,2,1,0:T(8,128)S(1)} %copy-done.8, bf16[4,128,3072]{2,1,0:T(8,128)(2,1)S(1)} %bitcast.173, bf16[4,128,3072]{2,1,0:T(8,128)(2,1)S(1)} %bitcast.189, bf16[128,1024]{1,0:T(8,128)(2,1)S(1)} %bitcast.193, ...), custom_call_target="tpu_custom_call" | custom-call | flops 1024 | bytes 1024 | tf_op jit(solution)/shard_map/pallas_call | solution.py:80
  134.4 1.9 %collective-permute-done.32.refs_10_ = bf16[128,3072]{1,0:T(8,128)(2,1)S(1)} collective-permute-done((bf16[128,3072]{1,0:T(8,128)(2,1)S(1)}, bf16[128,3072]{1,0:T(8,128)(2,1)S(1)}, u32[]{:S(2)}, u32[]{:S(2)}) %collective-permute-start.32) | collective-permute-done | bytes 786464 | tf_op jit(solution)/shard_map/ppermute | solution.py:47
  136.3 2.6 %shard_map.82 = (bf16[128,3072]{1,0:T(8,128)(2,1)S(1)}, bf16[128,3072]{1,0:T(8,128)(2,1)S(1)}, bf16[128,3072]{1,0:T(8,128)(2,1)S(1)}) custom-call(s32[16]{0:T(128)S(1)} %min.12.asked_ref, f32[8,128]{1,0:T(8,128)S(1)} %fusion.22.norm_ref, f32[6,2,128,128]{3,2,1,0:T(8,128)S(1)} %copy-done.8, bf16[4,128,3072]{2,1,0:T(8,128)(2,1)S(1)} %bitcast.174, ...), custom_call_target="tpu_custom_call" | custom-call | flops 1024 | bytes 1024 | tf_op jit(solution)/shard_map/pallas_call | solution.py:80
  139.0 0.6 collective-permute-start.33
  139.7 0.9 collective-permute-start.34
  141.0 3.9 %collective-permute-done.30 = bf16[128,3072]{1,0:T(8,128)(2,1)S(1)} collective-permute-done((bf16[128,3072]{1,0:T(8,128)(2,1)S(1)}, bf16[128,3072]{1,0:T(8,128)(2,1)S(1)}, u32[]{:S(2)}, u32[]{:S(2)}) %collective-permute-start.30) | collective-permute-done | bytes 786464 | tf_op jit(solution)/shard_map/ppermute | solution.py:47
  144.8 7.4 %shard_map.81 = f32[4,128,3072]{2,1,0:T(8,128)} custom-call(s32[16]{0:T(128)S(1)} %min.12.asked_ref, f32[8,128]{1,0:T(8,128)S(1)} %fusion.22.norm_ref, f32[6,2,128,128]{3,2,1,0:T(8,128)S(1)} %copy-done.8, f32[2,2,128,128]{3,2,1,0:T(8,128)S(1)} %get-tuple-element.46.refs_0_.refs_3_.refs_1_, bf16[128,3072]{1,0:T(8,128)(2,1)S(1)} %copy-done.6, ...), custom_call_target="tpu_custom_call" | custom-call | flops 1024 | bytes 1024 | tf_op jit(solution)/shard_map/pallas_call | solution.py:80
  152.2 1.6 add_multiply_fusion
  153.8 3.7 %collective-permute-done.36 = bf16[128,3072]{1,0:T(8,128)(2,1)S(1)} collective-permute-done((bf16[128,3072]{1,0:T(8,128)(2,1)S(1)}, bf16[128,3072]{1,0:T(8,128)(2,1)S(1)}, u32[]{:S(2)}, u32[]{:S(2)}) %collective-permute-start.36) | collective-permute-done | bytes 786464 | tf_op jit(solution)/shard_map/ppermute | solution.py:47
  157.5 2.3 %collective-permute-done.34 = bf16[128,3072]{1,0:T(8,128)(2,1)S(1)} collective-permute-done((bf16[128,3072]{1,0:T(8,128)(2,1)S(1)}, bf16[128,3072]{1,0:T(8,128)(2,1)S(1)}, u32[]{:S(2)}, u32[]{:S(2)}) %collective-permute-start.34) | collective-permute-done | bytes 786464 | tf_op jit(solution)/shard_map/ppermute | solution.py:47
  159.8 1.6 add_multiply_fusion.1
  (161 shorter events, 9.2 us)
Async XLA Ops:
  0.6 22.8 %collective-permute-start.4 = (bf16[512,3072]{1,0:T(8,128)(2,1)}, bf16[512,3072]{1,0:T(8,128)(2,1)S(1)}, u32[]{:S(2)}, u32[]{:S(2)}) collective-permute-start(bf16[512,3072]{1,0:T(8,128)(2,1)} %param.6), channel_id=1, source_target_pairs={{0,1},{1,0},{2,3},{3,2},{4,5},{5,4},{6,7},{7,6},{8,9},{9,8},{10,11... | collective-permute-start | bytes 9437192 | tf_op jit(solution)/shard_map/ppermute | solution.py:47
  2.9 2.5 %collective-permute-start = (s32[1,16]{1,0:T(1,128)S(1)}, s32[1,16]{1,0:T(1,128)S(1)}, u32[]{:S(2)}, u32[]{:S(2)}) collective-permute-start(s32[1,16]{1,0:T(1,128)S(1)} %add_bitcast_fusion), channel_id=1, source_target_pairs={{0,8},{1,9},{2,10},{3,11},{4,12},{5,13},{6,14},{7,15},{8,0},{9,1},... | collective-permute-start | bytes 200 | tf_op jit(solution)/shard_map/ppermute | solution.py:47
  4.3 19.2 %collective-permute-start.5 = (bf16[128,3072]{1,0:T(8,128)(2,1)}, bf16[128,3072]{1,0:T(8,128)(2,1)}, u32[]{:S(2)}, u32[]{:S(2)}) collective-permute-start(bf16[128,3072]{1,0:T(8,128)(2,1)} %refs_2_.3), channel_id=1, source_target_pairs={{0,8},{1,9},{2,10},{3,11},{4,12},{5,13},{6,14},{7,15},{8,0},{9,1},... | collective-permute-start | bytes 2359304 | tf_op jit(solution)/shard_map/ppermute | solution.py:47
  5.4 5.8 %collective-permute-start.2 = (s32[2,16]{1,0:T(2,128)S(1)}, s32[2,16]{1,0:T(2,128)S(1)}, u32[]{:S(2)}, u32[]{:S(2)}) collective-permute-start(s32[2,16]{1,0:T(2,128)S(1)} %get-tuple-element.91), channel_id=1, source_target_pairs={{0,4},{1,5},{2,6},{3,7},{4,0},{5,1},{6,2},{7,3},{8,12},{9,13},{10,... | collective-permute-start | bytes 392 | tf_op jit(solution)/shard_map/ppermute | solution.py:47
  8.4 3.6 %collective-permute-start.1 = (s32[2,16]{1,0:T(2,128)S(1)}, s32[2,16]{1,0:T(2,128)S(1)}, u32[]{:S(2)}, u32[]{:S(2)}) collective-permute-start(s32[2,16]{1,0:T(2,128)S(1)} %get-tuple-element.91), channel_id=1, source_target_pairs={{0,6},{1,3},{2,0},{3,5},{4,2},{5,7},{6,4},{7,1},{8,14},{9,11},{10,... | collective-permute-start | bytes 392 | tf_op jit(solution)/shard_map/ppermute | solution.py:47
  8.8 3.2 %collective-permute-start.3 = (s32[2,16]{1,0:T(2,128)S(1)}, s32[2,16]{1,0:T(2,128)S(1)}, u32[]{:S(2)}, u32[]{:S(2)}) collective-permute-start(s32[2,16]{1,0:T(2,128)S(1)} %get-tuple-element.91), channel_id=1, source_target_pairs={{0,2},{1,7},{2,4},{3,1},{4,6},{5,3},{6,0},{7,5},{8,10},{9,15},{10,... | collective-permute-start | bytes 392 | tf_op jit(solution)/shard_map/ppermute | solution.py:47
  12.8 44.9 %copy-start.5 = (bf16[128,3072]{1,0:T(8,128)(2,1)S(1)}, bf16[128,3072]{1,0:T(8,128)(2,1)}, u32[]{:S(2)}) copy-start(bf16[128,3072]{1,0:T(8,128)(2,1)} %refs_2_.3) | copy-start | bytes 2359300
  12.8 13.1 %collective-permute-start.11 = (bf16[128,3072]{1,0:T(8,128)(2,1)}, bf16[128,3072]{1,0:T(8,128)(2,1)S(1)}, u32[]{:S(2)}, u32[]{:S(2)}) collective-permute-start(bf16[128,3072]{1,0:T(8,128)(2,1)} %refs_4_.1), channel_id=1, source_target_pairs={{0,16},{1,49},{2,18},{3,51},{4,20},{5,53},{6,22},{7,55},{8,24},{9,... | collective-permute-start | bytes 2359304 | tf_op jit(solution)/shard_map/ppermute | solution.py:47
  16.7 19.2 %collective-permute-start.7 = (bf16[128,3072]{1,0:T(8,128)(2,1)}, bf16[128,3072]{1,0:T(8,128)(2,1)S(1)}, u32[]{:S(2)}, u32[]{:S(2)}) collective-permute-start(bf16[128,3072]{1,0:T(8,128)(2,1)} %refs_2_.3), channel_id=1, source_target_pairs={{0,6},{1,3},{2,0},{3,5},{4,2},{5,7},{6,4},{7,1},{8,14},{9,11},{10,... | collective-permute-start | bytes 2359304 | tf_op jit(solution)/shard_map/ppermute | solution.py:47
  16.7 19.7 %collective-permute-start.6 = (bf16[128,3072]{1,0:T(8,128)(2,1)}, bf16[128,3072]{1,0:T(8,128)(2,1)S(1)}, u32[]{:S(2)}, u32[]{:S(2)}) collective-permute-start(bf16[128,3072]{1,0:T(8,128)(2,1)} %refs_2_.3), channel_id=1, source_target_pairs={{0,2},{1,7},{2,4},{3,1},{4,6},{5,3},{6,0},{7,5},{8,10},{9,15},{10,... | collective-permute-start | bytes 2359304 | tf_op jit(solution)/shard_map/ppermute | solution.py:47
  23.4 34.7 %copy-start.1 = (bf16[512,3072]{1,0:T(8,128)(2,1)}, bf16[512,3072]{1,0:T(8,128)(2,1)S(1)}, u32[]{:S(2)}) copy-start(bf16[512,3072]{1,0:T(8,128)(2,1)S(1)} %collective-permute-done.4) | copy-start | bytes 9437188
  25.9 33.5 %copy-start.22 = (bf16[128,3072]{1,0:T(8,128)(2,1)}, bf16[128,3072]{1,0:T(8,128)(2,1)S(1)}, u32[]{:S(2)}) copy-start(bf16[128,3072]{1,0:T(8,128)(2,1)S(1)} %collective-permute-done.11.refs_7_) | copy-start | bytes 2359300
  25.9 20.0 %collective-permute-start.8 = (bf16[128,3072]{1,0:T(8,128)(2,1)}, bf16[128,3072]{1,0:T(8,128)(2,1)S(1)}, u32[]{:S(2)}, u32[]{:S(2)}) collective-permute-start(bf16[128,3072]{1,0:T(8,128)(2,1)} %collective-permute-done.5.refs_3_.refs_6_), channel_id=1, source_target_pairs={{0,2},{1,7},{2,4},{3,1},{4,6},{5,3},{6,0},{7,5},{8,10},{9,15},{10,... | collective-permute-start | bytes 2359304 | tf_op jit(solution)/shard_map/ppermute | solution.py:47
  28.9 20.3 %collective-permute-start.12 = (bf16[128,3072]{1,0:T(8,128)(2,1)S(1)}, bf16[128,3072]{1,0:T(8,128)(2,1)S(1)}, u32[]{:S(2)}, u32[]{:S(2)}) collective-permute-start(bf16[128,3072]{1,0:T(8,128)(2,1)S(1)} %collective-permute-done.11.refs_7_), channel_id=1, source_target_pairs={{0,16},{1,49},{2,18},{3,51},{4,20},{5,53},{6,22},{7,55},{8,24},{9,... | collective-permute-start | bytes 2359304 | tf_op jit(solution)/shard_map/ppermute | solution.py:47
  32.2 20.1 %collective-permute-start.13 = (bf16[128,3072]{1,0:T(8,128)(2,1)}, bf16[128,3072]{1,0:T(8,128)(2,1)S(1)}, u32[]{:S(2)}, u32[]{:S(2)}) collective-permute-start(bf16[128,3072]{1,0:T(8,128)(2,1)} %refs_4_.1), channel_id=1, source_target_pairs={{0,64},{1,65},{2,66},{3,67},{4,68},{5,69},{6,70},{7,71},{8,72},{9,... | collective-permute-start | bytes 2359304 | tf_op jit(solution)/shard_map/ppermute | solution.py:47
  35.9 26.1 %copy-start.13 = (bf16[128,3072]{1,0:T(8,128)(2,1)}, bf16[128,3072]{1,0:T(8,128)(2,1)S(1)}, u32[]{:S(2)}) copy-start(bf16[128,3072]{1,0:T(8,128)(2,1)S(1)} %collective-permute-done.7.refs_9_.refs_3_) | copy-start | bytes 2359300
  36.3 25.6 %copy-start.15 = (bf16[128,3072]{1,0:T(8,128)(2,1)}, bf16[128,3072]{1,0:T(8,128)(2,1)S(1)}, u32[]{:S(2)}) copy-start(bf16[128,3072]{1,0:T(8,128)(2,1)S(1)} %collective-permute-done.6.refs_6_.refs_5_) | copy-start | bytes 2359300
  36.3 16.0 %collective-permute-start.10 = (bf16[128,3072]{1,0:T(8,128)(2,1)}, bf16[128,3072]{1,0:T(8,128)(2,1)S(1)}, u32[]{:S(2)}, u32[]{:S(2)}) collective-permute-start(bf16[128,3072]{1,0:T(8,128)(2,1)} %refs_4_.1), channel_id=1, source_target_pairs={{0,48},{1,17},{2,50},{3,19},{4,52},{5,21},{6,54},{7,23},{8,56},{9,... | collective-permute-start | bytes 2359304 | tf_op jit(solution)/shard_map/ppermute | solution.py:47
  36.3 21.4 %collective-permute-start.9 = (bf16[128,3072]{1,0:T(8,128)(2,1)}, bf16[128,3072]{1,0:T(8,128)(2,1)S(1)}, u32[]{:S(2)}, u32[]{:S(2)}) collective-permute-start(bf16[128,3072]{1,0:T(8,128)(2,1)} %collective-permute-done.5.refs_3_.refs_6_), channel_id=1, source_target_pairs={{0,6},{1,3},{2,0},{3,5},{4,2},{5,7},{6,4},{7,1},{8,14},{9,11},{10,... | collective-permute-start | bytes 2359304 | tf_op jit(solution)/shard_map/ppermute | solution.py:47
  45.9 16.1 %copy-start.17 = (bf16[128,3072]{1,0:T(8,128)(2,1)}, bf16[128,3072]{1,0:T(8,128)(2,1)S(1)}, u32[]{:S(2)}) copy-start(bf16[128,3072]{1,0:T(8,128)(2,1)S(1)} %collective-permute-done.8.refs_12_.refs_9_) | copy-start | bytes 2359300
  45.9 27.3 %collective-permute-start.17 = (bf16[128,3072]{1,0:T(8,128)(2,1)S(1)}, bf16[128,3072]{1,0:T(8,128)(2,1)S(1)}, u32[]{:S(2)}, u32[]{:S(2)}) collective-permute-start(bf16[128,3072]{1,0:T(8,128)(2,1)S(1)} %collective-permute-done.6.refs_6_.refs_5_), channel_id=1, source_target_pairs={{0,2},{1,7},{2,4},{3,1},{4,6},{5,3},{6,0},{7,5},{8,10},{9,15},{10,... | collective-permute-start | bytes 2359304 | tf_op jit(solution)/shard_map/ppermute | solution.py:47
  52.3 23.3 %collective-permute-start.14 = (bf16[128,3072]{1,0:T(8,128)(2,1)S(1)}, bf16[128,3072]{1,0:T(8,128)(2,1)S(1)}, u32[]{:S(2)}, u32[]{:S(2)}) collective-permute-start(bf16[128,3072]{1,0:T(8,128)(2,1)S(1)} %collective-permute-done.13.refs_8_), channel_id=1, source_target_pairs={{0,48},{1,17},{2,50},{3,19},{4,52},{5,21},{6,54},{7,23},{8,56},{9,... | collective-permute-start | bytes 2359304 | tf_op jit(solution)/shard_map/ppermute | solution.py:47
  52.3 23.7 %collective-permute-start.15 = (bf16[128,3072]{1,0:T(8,128)(2,1)S(1)}, bf16[128,3072]{1,0:T(8,128)(2,1)S(1)}, u32[]{:S(2)}, u32[]{:S(2)}) collective-permute-start(bf16[128,3072]{1,0:T(8,128)(2,1)S(1)} %collective-permute-done.12.refs_6_), channel_id=1, source_target_pairs={{0,64},{1,65},{2,66},{3,67},{4,68},{5,69},{6,70},{7,71},{8,72},{9,... | collective-permute-start | bytes 2359304 | tf_op jit(solution)/shard_map/ppermute | solution.py:47
  55.0 21.4 %collective-permute-start.16 = (bf16[128,3072]{1,0:T(8,128)(2,1)S(1)}, bf16[128,3072]{1,0:T(8,128)(2,1)S(1)}, u32[]{:S(2)}, u32[]{:S(2)}) collective-permute-start(bf16[128,3072]{1,0:T(8,128)(2,1)S(1)} %collective-permute-done.13.refs_8_), channel_id=1, source_target_pairs={{0,16},{1,49},{2,18},{3,51},{4,20},{5,53},{6,22},{7,55},{8,24},{9,... | collective-permute-start | bytes 2359304 | tf_op jit(solution)/shard_map/ppermute | solution.py:47
  57.7 4.2 %copy-start.19 = (bf16[128,3072]{1,0:T(8,128)(2,1)}, bf16[128,3072]{1,0:T(8,128)(2,1)S(1)}, u32[]{:S(2)}) copy-start(bf16[128,3072]{1,0:T(8,128)(2,1)S(1)} %collective-permute-done.9.refs_15_.refs_7_) | copy-start | bytes 2359300
  57.7 15.5 %collective-permute-start.18 = (bf16[128,3072]{1,0:T(8,128)(2,1)S(1)}, bf16[128,3072]{1,0:T(8,128)(2,1)S(1)}, u32[]{:S(2)}, u32[]{:S(2)}) collective-permute-start(bf16[128,3072]{1,0:T(8,128)(2,1)S(1)} %collective-permute-done.9.refs_15_.refs_7_), channel_id=1, source_target_pairs={{0,6},{1,3},{2,0},{3,5},{4,2},{5,7},{6,4},{7,1},{8,14},{9,11},{10,... | collective-permute-start | bytes 2359304 | tf_op jit(solution)/shard_map/ppermute | solution.py:47
  69.4 6.1 %copy-start.7 = (f32[6,2,128,128]{3,2,1,0:T(8,128)}, f32[6,2,128,128]{3,2,1,0:T(8,128)S(1)}, u32[]{:S(2)}) copy-start(f32[6,2,128,128]{3,2,1,0:T(8,128)S(1)} %get-tuple-element.52.refs_0_.refs_3_.refs_6_) | copy-start | bytes 2359300
  77.7 4.5 %collective-permute-start.19 = (f32[8,2,128]{2,0,1:T(8,128)S(1)}, f32[8,2,128]{2,0,1:T(8,128)S(1)}, u32[]{:S(2)}, u32[]{:S(2)}) collective-permute-start(f32[8,2,128]{2,0,1:T(8,128)S(1)} %concatenate.38), channel_id=1, source_target_pairs={{0,8},{1,9},{2,10},{3,11},{4,12},{5,13},{6,14},{7,15},{8,0},{9,1},... | collective-permute-start | bytes 24584 | tf_op jit(solution)/shard_map/ppermute | solution.py:47
  80.3 8.9 %copy-start.37 = (f32[1024,128]{0,1:T(8,128)S(1)}, f32[1024,128]{0,1:T(8,128)}, u32[]{:S(2)}) copy-start(f32[1024,128]{0,1:T(8,128)} %copy-done.36) | copy-start | bytes 1572868
  80.3 15.0 %copy-start.20 = (bf16[128,3072]{1,0:T(8,128)(2,1)S(1)}, bf16[128,3072]{1,0:T(8,128)(2,1)}, u32[]{:S(2)}) copy-start(bf16[128,3072]{1,0:T(8,128)(2,1)} %copy-done.19) | copy-start | bytes 2359300
  82.2 7.2 %copy-start.6 = (bf16[128,3072]{1,0:T(8,128)(2,1)S(1)}, bf16[128,3072]{1,0:T(8,128)(2,1)}, u32[]{:S(2)}) copy-start(bf16[128,3072]{1,0:T(8,128)(2,1)} %refs_2_.3) | copy-start | bytes 2359300
  82.3 4.1 %collective-permute-start.22 = (f32[8,2,128]{2,0,1:T(8,128)S(1)}, f32[8,2,128]{2,0,1:T(8,128)S(1)}, u32[]{:S(2)}, u32[]{:S(2)}) collective-permute-start(f32[8,2,128]{2,0,1:T(8,128)S(1)} %pad_maximum_fusion.3), channel_id=1, source_target_pairs={{0,4},{1,5},{2,6},{3,7},{4,0},{5,1},{6,2},{7,3},{8,12},{9,13},{10,... | collective-permute-start | bytes 24584 | tf_op jit(solution)/shard_map/ppermute | solution.py:47
  82.4 6.7 %collective-permute-start.20 = (f32[9,2,128]{2,0,1:T(8,128)S(1)}, f32[9,2,128]{2,0,1:T(8,128)S(1)}, u32[]{:S(2)}, u32[]{:S(2)}) collective-permute-start(f32[9,2,128]{2,0,1:T(8,128)S(1)} %get-tuple-element.82), channel_id=1, source_target_pairs={{0,6},{1,3},{2,0},{3,5},{4,2},{5,7},{6,4},{7,1},{8,14},{9,11},{10,... | collective-permute-start | bytes 27656 | tf_op jit(solution)/shard_map/ppermute | solution.py:47
  83.2 5.9 %collective-permute-start.21 = (f32[9,2,128]{2,0,1:T(8,128)S(1)}, f32[9,2,128]{2,0,1:T(8,128)S(1)}, u32[]{:S(2)}, u32[]{:S(2)}) collective-permute-start(f32[9,2,128]{2,0,1:T(8,128)S(1)} %get-tuple-element.83), channel_id=1, source_target_pairs={{0,2},{1,7},{2,4},{3,1},{4,6},{5,3},{6,0},{7,5},{8,10},{9,15},{10,... | collective-permute-start | bytes 27656 | tf_op jit(solution)/shard_map/ppermute | solution.py:47
  86.4 17.4 %collective-permute-start.24 = (bf16[128,3072]{1,0:T(8,128)(2,1)S(1)}, bf16[128,3072]{1,0:T(8,128)(2,1)S(1)}, u32[]{:S(2)}, u32[]{:S(2)}) collective-permute-start(bf16[128,3072]{1,0:T(8,128)(2,1)S(1)} %get-tuple-element.50), channel_id=1, source_target_pairs={{0,6},{1,3},{2,0},{3,5},{4,2},{5,7},{6,4},{7,1},{8,14},{9,11},{10,... | collective-permute-start | bytes 2359304 | tf_op jit(solution)/shard_map/ppermute | solution.py:47
  86.4 19.8 %collective-permute-start.23 = (bf16[128,3072]{1,0:T(8,128)(2,1)S(1)}, bf16[128,3072]{1,0:T(8,128)(2,1)S(1)}, u32[]{:S(2)}, u32[]{:S(2)}) collective-permute-start(bf16[128,3072]{1,0:T(8,128)(2,1)S(1)} %get-tuple-element.48), channel_id=1, source_target_pairs={{0,2},{1,7},{2,4},{3,1},{4,6},{5,3},{6,0},{7,5},{8,10},{9,15},{10,... | collective-permute-start | bytes 2359304 | tf_op jit(solution)/shard_map/ppermute | solution.py:47
  89.4 5.9 %copy-start.16 = (bf16[128,3072]{1,0:T(8,128)(2,1)S(1)}, bf16[128,3072]{1,0:T(8,128)(2,1)}, u32[]{:S(2)}) copy-start(bf16[128,3072]{1,0:T(8,128)(2,1)} %copy-done.15) | copy-start | bytes 2359300
  89.4 5.9 %copy-start.18 = (bf16[128,3072]{1,0:T(8,128)(2,1)S(1)}, bf16[128,3072]{1,0:T(8,128)(2,1)}, u32[]{:S(2)}) copy-start(bf16[128,3072]{1,0:T(8,128)(2,1)} %copy-done.17) | copy-start | bytes 2359300
  89.8 5.5 %copy-start.8 = (f32[6,2,128,128]{3,2,1,0:T(8,128)S(1)}, f32[6,2,128,128]{3,2,1,0:T(8,128)}, u32[]{:S(2)}) copy-start(f32[6,2,128,128]{3,2,1,0:T(8,128)} %copy-done.7) | copy-start | bytes 2359300
  89.8 5.5 %copy-start.10 = (bf16[128,3072]{1,0:T(8,128)(2,1)S(1)}, bf16[128,3072]{1,0:T(8,128)(2,1)}, u32[]{:S(2)}) copy-start(bf16[128,3072]{1,0:T(8,128)(2,1)} %copy-done.9) | copy-start | bytes 2359300
  89.8 5.5 %copy-start.12 = (bf16[128,3072]{1,0:T(8,128)(2,1)S(1)}, bf16[128,3072]{1,0:T(8,128)(2,1)}, u32[]{:S(2)}) copy-start(bf16[128,3072]{1,0:T(8,128)(2,1)} %copy-done.11) | copy-start | bytes 2359300
  89.8 5.5 %copy-start.14 = (bf16[128,3072]{1,0:T(8,128)(2,1)S(1)}, bf16[128,3072]{1,0:T(8,128)(2,1)}, u32[]{:S(2)}) copy-start(bf16[128,3072]{1,0:T(8,128)(2,1)} %copy-done.13) | copy-start | bytes 2359300
  90.6 19.8 %collective-permute-start.25 = (bf16[128,3072]{1,0:T(8,128)(2,1)S(1)}, bf16[128,3072]{1,0:T(8,128)(2,1)S(1)}, u32[]{:S(2)}, u32[]{:S(2)}) collective-permute-start(bf16[128,3072]{1,0:T(8,128)(2,1)S(1)} %convolution_convert_fusion.3), channel_id=1, source_target_pairs={{0,64},{1,65},{2,66},{3,67},{4,68},{5,69},{6,70},{7,71},{8,72},{9,... | collective-permute-start | bytes 2359304 | tf_op jit(solution)/shard_map/ppermute | solution.py:47
  93.9 18.3 %collective-permute-start.27 = (bf16[128,3072]{1,0:T(8,128)(2,1)S(1)}, bf16[128,3072]{1,0:T(8,128)(2,1)S(1)}, u32[]{:S(2)}, u32[]{:S(2)}) collective-permute-start(bf16[128,3072]{1,0:T(8,128)(2,1)S(1)} %convolution_convert_fusion.2), channel_id=1, source_target_pairs={{0,16},{1,49},{2,18},{3,51},{4,20},{5,53},{6,22},{7,55},{8,24},{9,... | collective-permute-start | bytes 2359304 | tf_op jit(solution)/shard_map/ppermute | solution.py:47
  93.9 19.5 %collective-permute-start.28 = (bf16[128,3072]{1,0:T(8,128)(2,1)S(1)}, bf16[128,3072]{1,0:T(8,128)(2,1)S(1)}, u32[]{:S(2)}, u32[]{:S(2)}) collective-permute-start(bf16[128,3072]{1,0:T(8,128)(2,1)S(1)} %convolution_convert_fusion.1), channel_id=1, source_target_pairs={{0,48},{1,17},{2,50},{3,19},{4,52},{5,21},{6,54},{7,23},{8,56},{9,... | collective-permute-start | bytes 2359304 | tf_op jit(solution)/shard_map/ppermute | solution.py:47
  95.4 10.8 %copy-start.4 = (bf16[512,3072]{1,0:T(8,128)(2,1)S(1)}, bf16[512,3072]{1,0:T(8,128)(2,1)}, u32[]{:S(2)}) copy-start(bf16[512,3072]{1,0:T(8,128)(2,1)} %copy-done.1) | copy-start | bytes 9437188
  113.4 13.2 %collective-permute-start.29 = (bf16[4,128,3072]{2,1,0:T(8,128)(2,1)S(1)}, bf16[4,128,3072]{2,1,0:T(8,128)(2,1)S(1)}, u32[]{:S(2)}, u32[]{:S(2)}) collective-permute-start(bf16[4,128,3072]{2,1,0:T(8,128)(2,1)S(1)} %shard_map.79), channel_id=1, source_target_pairs={{0,1},{1,0},{2,3},{3,2},{4,5},{5,4},{6,7},{7,6},{8,9},{9,8},{10,11... | collective-permute-start | bytes 9437192 | tf_op jit(solution)/shard_map/ppermute | solution.py:47
  115.4 11.2 %collective-permute-start.26 = (bf16[128,3072]{1,0:T(8,128)(2,1)S(1)}, bf16[128,3072]{1,0:T(8,128)(2,1)S(1)}, u32[]{:S(2)}, u32[]{:S(2)}) collective-permute-start(bf16[128,3072]{1,0:T(8,128)(2,1)S(1)} %add_convert_fusion.1), channel_id=1, source_target_pairs={{0,16},{1,49},{2,18},{3,51},{4,20},{5,53},{6,22},{7,55},{8,24},{9,... | collective-permute-start | bytes 2359304 | tf_op jit(solution)/shard_map/ppermute | solution.py:47
  115.5 20.8 %collective-permute-start.31 = (bf16[128,3072]{1,0:T(8,128)(2,1)S(1)}, bf16[128,3072]{1,0:T(8,128)(2,1)S(1)}, u32[]{:S(2)}, u32[]{:S(2)}) collective-permute-start(bf16[128,3072]{1,0:T(8,128)(2,1)S(1)} %get-tuple-element.53), channel_id=1, source_target_pairs={{0,2},{1,7},{2,4},{3,1},{4,6},{5,3},{6,0},{7,5},{8,10},{9,15},{10,... | collective-permute-start | bytes 2359304 | tf_op jit(solution)/shard_map/ppermute | solution.py:47
  115.8 20.5 %collective-permute-start.32 = (bf16[128,3072]{1,0:T(8,128)(2,1)S(1)}, bf16[128,3072]{1,0:T(8,128)(2,1)S(1)}, u32[]{:S(2)}, u32[]{:S(2)}) collective-permute-start(bf16[128,3072]{1,0:T(8,128)(2,1)S(1)} %get-tuple-element.60), channel_id=1, source_target_pairs={{0,6},{1,3},{2,0},{3,5},{4,2},{5,7},{6,4},{7,1},{8,14},{9,11},{10,... | collective-permute-start | bytes 2359304 | tf_op jit(solution)/shard_map/ppermute | solution.py:47
  117.1 13.8 %copy-start.31 = (bf16[128,3072]{1,0:T(8,128)(2,1)S(1)}, bf16[128,3072]{1,0:T(8,128)(2,1)}, u32[]{:S(2)}) copy-start(bf16[128,3072]{1,0:T(8,128)(2,1)} %copy-done.30) | copy-start | bytes 2359300
  117.1 13.8 %copy-start.33 = (bf16[128,3072]{1,0:T(8,128)(2,1)S(1)}, bf16[128,3072]{1,0:T(8,128)(2,1)}, u32[]{:S(2)}) copy-start(bf16[128,3072]{1,0:T(8,128)(2,1)} %copy-done.32) | copy-start | bytes 2359300
  117.1 13.8 %copy-start.35 = (bf16[128,3072]{1,0:T(8,128)(2,1)S(1)}, bf16[128,3072]{1,0:T(8,128)(2,1)}, u32[]{:S(2)}) copy-start(bf16[128,3072]{1,0:T(8,128)(2,1)} %copy-done.34) | copy-start | bytes 2359300
  117.6 21.3 %collective-permute-start.35 = (bf16[128,3072]{1,0:T(8,128)(2,1)S(1)}, bf16[128,3072]{1,0:T(8,128)(2,1)S(1)}, u32[]{:S(2)}, u32[]{:S(2)}) collective-permute-start(bf16[128,3072]{1,0:T(8,128)(2,1)S(1)} %add_convert_fusion), channel_id=1, source_target_pairs={{0,64},{1,65},{2,66},{3,67},{4,68},{5,69},{6,70},{7,71},{8,72},{9,... | collective-permute-start | bytes 2359304 | tf_op jit(solution)/shard_map/ppermute | solution.py:47
  126.6 4.2 %copy-start.27 = (bf16[128,3072]{1,0:T(8,128)(2,1)S(1)}, bf16[128,3072]{1,0:T(8,128)(2,1)}, u32[]{:S(2)}) copy-start(bf16[128,3072]{1,0:T(8,128)(2,1)} %copy-done.26) | copy-start | bytes 2359300
  126.6 4.2 %copy-start.29 = (bf16[128,3072]{1,0:T(8,128)(2,1)S(1)}, bf16[128,3072]{1,0:T(8,128)(2,1)}, u32[]{:S(2)}) copy-start(bf16[128,3072]{1,0:T(8,128)(2,1)} %copy-done.28) | copy-start | bytes 2359300
  127.0 3.8 %copy-start.21 = (bf16[128,3072]{1,0:T(8,128)(2,1)S(1)}, bf16[128,3072]{1,0:T(8,128)(2,1)}, u32[]{:S(2)}) copy-start(bf16[128,3072]{1,0:T(8,128)(2,1)} %refs_4_.1) | copy-start | bytes 2359300
  127.1 3.8 %copy-start.23 = (bf16[128,3072]{1,0:T(8,128)(2,1)S(1)}, bf16[128,3072]{1,0:T(8,128)(2,1)}, u32[]{:S(2)}) copy-start(bf16[128,3072]{1,0:T(8,128)(2,1)} %copy-done.22) | copy-start | bytes 2359300
  127.1 3.8 %copy-start.25 = (bf16[128,3072]{1,0:T(8,128)(2,1)S(1)}, bf16[128,3072]{1,0:T(8,128)(2,1)}, u32[]{:S(2)}) copy-start(bf16[128,3072]{1,0:T(8,128)(2,1)} %copy-done.24) | copy-start | bytes 2359300
  127.1 17.8 %collective-permute-start.30 = (bf16[128,3072]{1,0:T(8,128)(2,1)S(1)}, bf16[128,3072]{1,0:T(8,128)(2,1)S(1)}, u32[]{:S(2)}, u32[]{:S(2)}) collective-permute-start(bf16[128,3072]{1,0:T(8,128)(2,1)S(1)} %convolution_convert_fusion), channel_id=1, source_target_pairs={{0,48},{1,17},{2,50},{3,19},{4,52},{5,21},{6,54},{7,23},{8,56},{9,... | collective-permute-start | bytes 2359304 | tf_op jit(solution)/shard_map/ppermute | solution.py:47
  127.6 24.7 %collective-permute-start.37 = (bf16[128,3072]{1,0:T(8,128)(2,1)S(1)}, bf16[128,3072]{1,0:T(8,128)(2,1)S(1)}, u32[]{:S(2)}, u32[]{:S(2)}) collective-permute-start(bf16[128,3072]{1,0:T(8,128)(2,1)S(1)} %fusion), channel_id=1, source_target_pairs={{0,16},{1,49},{2,18},{3,51},{4,20},{5,53},{6,22},{7,55},{8,24},{9,... | collective-permute-start | bytes 2359304 | tf_op jit(solution)/shard_map/ppermute | solution.py:47
  138.9 18.5 %collective-permute-start.36 = (bf16[128,3072]{1,0:T(8,128)(2,1)S(1)}, bf16[128,3072]{1,0:T(8,128)(2,1)S(1)}, u32[]{:S(2)}, u32[]{:S(2)}) collective-permute-start(bf16[128,3072]{1,0:T(8,128)(2,1)S(1)} %get-tuple-element.65), channel_id=1, source_target_pairs={{0,8},{1,9},{2,10},{3,11},{4,12},{5,13},{6,14},{7,15},{8,0},{9,1},... | collective-permute-start | bytes 2359304 | tf_op jit(solution)/shard_map/ppermute | solution.py:47
  139.0 18.4 %collective-permute-start.33 = (bf16[128,3072]{1,0:T(8,128)(2,1)S(1)}, bf16[128,3072]{1,0:T(8,128)(2,1)S(1)}, u32[]{:S(2)}, u32[]{:S(2)}) collective-permute-start(bf16[128,3072]{1,0:T(8,128)(2,1)S(1)} %get-tuple-element.62), channel_id=1, source_target_pairs={{0,2},{1,7},{2,4},{3,1},{4,6},{5,3},{6,0},{7,5},{8,10},{9,15},{10,... | collective-permute-start | bytes 2359304 | tf_op jit(solution)/shard_map/ppermute | solution.py:47
  139.7 20.1 %collective-permute-start.34 = (bf16[128,3072]{1,0:T(8,128)(2,1)S(1)}, bf16[128,3072]{1,0:T(8,128)(2,1)S(1)}, u32[]{:S(2)}, u32[]{:S(2)}) collective-permute-start(bf16[128,3072]{1,0:T(8,128)(2,1)S(1)} %get-tuple-element.63), channel_id=1, source_target_pairs={{0,6},{1,3},{2,0},{3,5},{4,2},{5,7},{6,4},{7,1},{8,14},{9,11},{10,... | collective-permute-start | bytes 2359304 | tf_op jit(solution)/shard_map/ppermute | solution.py:47
  (12 other events, 16.8 us)

commit v3 on v2

--- a/solution.py
+++ b/solution.py
@@ -326,14 +326,14 @@
     inner_3 = after(inner_2, z02, theirs)
     z01 = send(z_part((0, 1), inner_3, z02), Z_FWD)
     z03 = send(z_part((0, 3), inner_3), Z_BWD)
-    loop = (jnp.swapaxes(inner_3, 0, 1), *[p[o] for o in SPOTS])
-    (mine,) = y_parts(norm, (z02, theirs), ((0, 0), (), F32), loop=loop)
+    loop = (jnp.swapaxes(inner_2, 0, 1), *[p[o] for o in SPOTS])
+    (mine,) = y_parts(norm, (z13,), ((0, 0), (), F32), loop=loop)
     y10, y01, y03 = y_parts(
         norm, (y11, y13, mine), ((1, 0), ((y11, None), (y13, None)), BF16), ((0, 1), ((y02, 0),), BF16),
         ((0, 3), (), BF16), peers=peers
     )
-    y10 = send(after(y10, z10), X_LO)
-    y01, y03 = send(y01, Y_FWD), send(y03, Y_BWD)
+    y10 = send(y10, X_LO)
+    y01, y03 = send(y01, Y_FWD), send(after(y03, z10), Y_BWD)
     grad_corpus = corpus_part(asked, in_order, after(norm, z03), q_blocks, held, F32, 0, theirs)
     mine, first, grad_corpus = lax.optimization_barrier((mine, mm(inner_3[:BLOCK], queries), grad_corpus))
     grad_queries = OUT_SCALE * near(mine, y01, y03, y10)

time: 162 us -> 160 us (0.988)
  waiting for transfers between devices: 54 us -> 44.9 us
  starting transfers between devices: 54.1 us -> 61.8 us
    ppermute x38, waiting for transfers between devices: 54 us -> 44.9 us  [send(): return lax.ppermute(value, AXES, route)]
    ppermute x38, starting transfers between devices: 54.1 us -> 61.8 us  [send(): return lax.ppermute(value, AXES, route)]
where the time goes in v3:
time: 160 us
  starting transfers between devices  61.8 us (39%)
  waiting for transfers between devices  44.9 us (28%)
  Pallas kernels  30.7 us (19%)
  local copies, waits for them, and re-layouts  8.24 us (5%)
  matrix products  7.54 us (5%)
  other arithmetic  5.31 us (3%)
    ppermute x38, starting transfers between devices, send(): return lax.ppermute(value, AXES, route)  61.8 us
    ppermute x38, waiting for transfers between devices, send(): return lax.ppermute(value, AXES, route)  44.9 us
    pallas_call x8, Pallas kernels, kernel(): pl.pallas_call(body, grid_spec=pltpu.PrefetchScalarGridSpec(num_scalar_pr...  30.7 us
    unnamed x76, local copies, waits for them, and re-layouts  7.61 us
    dot_general x8, matrix products, rows_dot(): lax.dot_general(left, right, (((1,), (1,)), ((), ())), preferred_element_...  4.34 us
  transfers between devices with their start and end apart: 38, of which 20 were waited for; matrix products, arithmetic and copies ran while one was open for 7% of the time, Pallas kernels for 19%

profile of v3, /device:TPU:1, one launch (start us, length us, event | category | flops | bytes accessed | tf_op | source)
XLA Modules:
  0.0 159.9 jit_solution(12308191228243245383)
XLA Ops:
  0.6 1.5 collective-permute-start.4
  2.1 0.7 and_select_fusion.1
  2.9 1.4 collective-permute-start
  4.5 0.9 collective-permute-done
  5.4 3.1 %collective-permute-start.2 = (s32[2,16]{1,0:T(2,128)S(1)}, s32[2,16]{1,0:T(2,128)S(1)}, u32[]{:S(2)}, u32[]{:S(2)}) collective-permute-start(s32[2,16]{1,0:T(2,128)S(1)} %get-tuple-element.91), channel_id=1, source_target_pairs={{0,4},{1,5},{2,6},{3,7},{4,0},{5,1},{6,2},{7,3},{8,12},{9,13},{10,... | collective-permute-start | bytes 392 | tf_op jit(solution)/shard_map/ppermute | solution.py:47
  8.8 2.3 %collective-permute-start.3 = (s32[2,16]{1,0:T(2,128)S(1)}, s32[2,16]{1,0:T(2,128)S(1)}, u32[]{:S(2)}, u32[]{:S(2)}) collective-permute-start(s32[2,16]{1,0:T(2,128)S(1)} %get-tuple-element.91), channel_id=1, source_target_pairs={{0,2},{1,7},{2,4},{3,1},{4,6},{5,3},{6,0},{7,5},{8,10},{9,15},{10,... | collective-permute-start | bytes 392 | tf_op jit(solution)/shard_map/ppermute | solution.py:47
  11.1 0.9 collective-permute-done.1
  12.8 3.8 %collective-permute-start.11 = (bf16[128,3072]{1,0:T(8,128)(2,1)}, bf16[128,3072]{1,0:T(8,128)(2,1)S(1)}, u32[]{:S(2)}, u32[]{:S(2)}) collective-permute-start(bf16[128,3072]{1,0:T(8,128)(2,1)} %refs_4_.1), channel_id=1, source_target_pairs={{0,16},{1,49},{2,18},{3,51},{4,20},{5,53},{6,22},{7,55},{8,24},{9,... | collective-permute-start | bytes 2359304 | tf_op jit(solution)/shard_map/ppermute | solution.py:47
  16.7 3.0 %collective-permute-start.6 = (bf16[128,3072]{1,0:T(8,128)(2,1)}, bf16[128,3072]{1,0:T(8,128)(2,1)S(1)}, u32[]{:S(2)}, u32[]{:S(2)}) collective-permute-start(bf16[128,3072]{1,0:T(8,128)(2,1)} %refs_2_.3), channel_id=1, source_target_pairs={{0,2},{1,7},{2,4},{3,1},{4,6},{5,3},{6,0},{7,5},{8,10},{9,15},{10,... | collective-permute-start | bytes 2359304 | tf_op jit(solution)/shard_map/ppermute | solution.py:47
  19.6 3.8 %collective-permute-done.5.refs_3_.refs_6_ = bf16[128,3072]{1,0:T(8,128)(2,1)} collective-permute-done((bf16[128,3072]{1,0:T(8,128)(2,1)}, bf16[128,3072]{1,0:T(8,128)(2,1)}, u32[]{:S(2)}, u32[]{:S(2)}) %collective-permute-start.5) | collective-permute-done | bytes 786464 | tf_op jit(solution)/shard_map/ppermute | solution.py:47
  23.4 2.5 %collective-permute-done.11.refs_7_ = bf16[128,3072]{1,0:T(8,128)(2,1)S(1)} collective-permute-done((bf16[128,3072]{1,0:T(8,128)(2,1)}, bf16[128,3072]{1,0:T(8,128)(2,1)S(1)}, u32[]{:S(2)}, u32[]{:S(2)}) %collective-permute-start.11) | collective-permute-done | bytes 786464 | tf_op jit(solution)/shard_map/ppermute | solution.py:47
  25.9 3.0 %collective-permute-start.8 = (bf16[128,3072]{1,0:T(8,128)(2,1)}, bf16[128,3072]{1,0:T(8,128)(2,1)S(1)}, u32[]{:S(2)}, u32[]{:S(2)}) collective-permute-start(bf16[128,3072]{1,0:T(8,128)(2,1)} %collective-permute-done.5.refs_3_.refs_6_), channel_id=1, source_target_pairs={{0,2},{1,7},{2,4},{3,1},{4,6},{5,3},{6,0},{7,5},{8,10},{9,15},{10,... | collective-permute-start | bytes 2359304 | tf_op jit(solution)/shard_map/ppermute | solution.py:47
  28.9 3.3 %collective-permute-start.12 = (bf16[128,3072]{1,0:T(8,128)(2,1)S(1)}, bf16[128,3072]{1,0:T(8,128)(2,1)S(1)}, u32[]{:S(2)}, u32[]{:S(2)}) collective-permute-start(bf16[128,3072]{1,0:T(8,128)(2,1)S(1)} %collective-permute-done.11.refs_7_), channel_id=1, source_target_pairs={{0,16},{1,49},{2,18},{3,51},{4,20},{5,53},{6,22},{7,55},{8,24},{9,... | collective-permute-start | bytes 2359304 | tf_op jit(solution)/shard_map/ppermute | solution.py:47
  32.2 2.7 %collective-permute-start.13 = (bf16[128,3072]{1,0:T(8,128)(2,1)}, bf16[128,3072]{1,0:T(8,128)(2,1)S(1)}, u32[]{:S(2)}, u32[]{:S(2)}) collective-permute-start(bf16[128,3072]{1,0:T(8,128)(2,1)} %refs_4_.1), channel_id=1, source_target_pairs={{0,64},{1,65},{2,66},{3,67},{4,68},{5,69},{6,70},{7,71},{8,72},{9,... | collective-permute-start | bytes 2359304 | tf_op jit(solution)/shard_map/ppermute | solution.py:47
  34.9 1.0 collective-permute-done.7.refs_9_.refs_3_
  36.3 1.8 %collective-permute-start.9 = (bf16[128,3072]{1,0:T(8,128)(2,1)}, bf16[128,3072]{1,0:T(8,128)(2,1)S(1)}, u32[]{:S(2)}, u32[]{:S(2)}) collective-permute-start(bf16[128,3072]{1,0:T(8,128)(2,1)} %collective-permute-done.5.refs_3_.refs_6_), channel_id=1, source_target_pairs={{0,6},{1,3},{2,0},{3,5},{4,2},{5,7},{6,4},{7,1},{8,14},{9,11},{10,... | collective-permute-start | bytes 2359304 | tf_op jit(solution)/shard_map/ppermute | solution.py:47
  38.2 1.7 %convolution_dynamic-update-slice_fusion.7 = f32[1024,128]{0,1:T(8,128)S(1)} fusion(bf16[128,3072]{1,0:T(8,128)(2,1)} %refs_4_.1, bf16[128,3072]{1,0:T(8,128)(2,1)} %refs_2_.3), kind=kOutput, calls=%fused_computation.17 | convolution fusion | flops 100663296 | bytes 1638400 | tf_op jit(solution)/shard_map/dot_general | solution.py:59
  39.9 6.0 %collective-permute-done.8.refs_12_.refs_9_ = bf16[128,3072]{1,0:T(8,128)(2,1)S(1)} collective-permute-done((bf16[128,3072]{1,0:T(8,128)(2,1)}, bf16[128,3072]{1,0:T(8,128)(2,1)S(1)}, u32[]{:S(2)}, u32[]{:S(2)}) %collective-permute-start.8) | collective-permute-done | bytes 786464 | tf_op jit(solution)/shard_map/ppermute | solution.py:47
  45.9 3.3 %collective-permute-start.17 = (bf16[128,3072]{1,0:T(8,128)(2,1)S(1)}, bf16[128,3072]{1,0:T(8,128)(2,1)S(1)}, u32[]{:S(2)}, u32[]{:S(2)}) collective-permute-start(bf16[128,3072]{1,0:T(8,128)(2,1)S(1)} %collective-permute-done.6.refs_6_.refs_5_), channel_id=1, source_target_pairs={{0,2},{1,7},{2,4},{3,1},{4,6},{5,3},{6,0},{7,5},{8,10},{9,15},{10,... | collective-permute-start | bytes 2359304 | tf_op jit(solution)/shard_map/ppermute | solution.py:47
  49.2 3.1 %collective-permute-done.13.refs_8_ = bf16[128,3072]{1,0:T(8,128)(2,1)S(1)} collective-permute-done((bf16[128,3072]{1,0:T(8,128)(2,1)}, bf16[128,3072]{1,0:T(8,128)(2,1)S(1)}, u32[]{:S(2)}, u32[]{:S(2)}) %collective-permute-start.13) | collective-permute-done | bytes 786464 | tf_op jit(solution)/shard_map/ppermute | solution.py:47
  52.3 2.7 %collective-permute-start.15 = (bf16[128,3072]{1,0:T(8,128)(2,1)S(1)}, bf16[128,3072]{1,0:T(8,128)(2,1)S(1)}, u32[]{:S(2)}, u32[]{:S(2)}) collective-permute-start(bf16[128,3072]{1,0:T(8,128)(2,1)S(1)} %collective-permute-done.12.refs_6_), channel_id=1, source_target_pairs={{0,64},{1,65},{2,66},{3,67},{4,68},{5,69},{6,70},{7,71},{8,72},{9,... | collective-permute-start | bytes 2359304 | tf_op jit(solution)/shard_map/ppermute | solution.py:47
  55.0 2.7 %collective-permute-start.16 = (bf16[128,3072]{1,0:T(8,128)(2,1)S(1)}, bf16[128,3072]{1,0:T(8,128)(2,1)S(1)}, u32[]{:S(2)}, u32[]{:S(2)}) collective-permute-start(bf16[128,3072]{1,0:T(8,128)(2,1)S(1)} %collective-permute-done.13.refs_8_), channel_id=1, source_target_pairs={{0,16},{1,49},{2,18},{3,51},{4,20},{5,53},{6,22},{7,55},{8,24},{9,... | collective-permute-start | bytes 2359304 | tf_op jit(solution)/shard_map/ppermute | solution.py:47
  58.1 0.9 copy-done.28
  59.4 0.9 copy-done.24
  61.1 0.9 copy-done.26
  62.0 0.5 copy-done
  62.5 1.9 %copy-done.2 = bf16[512,3072]{1,0:T(8,128)(2,1)S(1)} copy-done((bf16[512,3072]{1,0:T(8,128)(2,1)S(1)}, bf16[512,3072]{1,0:T(8,128)(2,1)}, u32[]{:S(2)}) %copy-start.2) | copy-done | bytes 3145752
  64.4 5.0 %shard_map.75 = (f32[6,2,128,128]{3,2,1,0:T(8,128)S(1)}, f32[6,2,128]{2,1,0:T(2,128)S(1)}) custom-call(s32[16]{0:T(128)S(1)} %min.12.asked_ref, bf16[128,3072]{1,0:T(8,128)(2,1)S(1)} %copy-done.5, bf16[4,128,3072]{2,1,0:T(8,128)(2,1)S(1)} %bitcast.161, bf16[4,128,3072]{2,1,0:T(8,128)(2,1)S(1)} %bitcast.177, ...), custom_call_target="tpu_custom_call" | custom-call | flops 1024 | bytes 1024 | tf_op jit(solution)/shard_map/pallas_call | solution.py:80
  69.5 3.7 %collective-permute-done.18.refs_3_.refs_8_ = bf16[128,3072]{1,0:T(8,128)(2,1)S(1)} collective-permute-done((bf16[128,3072]{1,0:T(8,128)(2,1)S(1)}, bf16[128,3072]{1,0:T(8,128)(2,1)S(1)}, u32[]{:S(2)}, u32[]{:S(2)}) %collective-permute-start.18) | collective-permute-done | bytes 786464 | tf_op jit(solution)/shard_map/ppermute | solution.py:47
  73.2 2.3 %shard_map.76 = (f32[2,2,128,128]{3,2,1,0:T(8,128)S(1)}, f32[2,2,128]{2,1,0:T(2,128)S(1)}) custom-call(s32[16]{0:T(128)S(1)} %min.12.asked_ref, bf16[128,3072]{1,0:T(8,128)(2,1)S(1)} %collective-permute-done.17.refs_0_.refs_4_, bf16[4,128,3072]{2,1,0:T(8,128)(2,1)S(1)} %bitcast.167, bf16[4,128,3072]{2,1,0:T(8,128)(2,1)S(1)} %bitcast.183, ...), custom_call_target="tpu_custom_call" | custom-call | flops 1024 | bytes 1024 | tf_op jit(solution)/shard_map/pallas_call | solution.py:80
  77.7 0.7 collective-permute-start.19
  78.4 1.9 %copy-done.3 = bf16[512,3072]{1,0:T(8,128)(2,1)S(1)} copy-done((bf16[512,3072]{1,0:T(8,128)(2,1)S(1)}, bf16[512,3072]{1,0:T(8,128)(2,1)}, u32[]{:S(2)}) %copy-start.3) | copy-done | bytes 3145752
  80.3 1.9 %shard_map.77 = (bf16[128,3072]{1,0:T(8,128)(2,1)S(1)}, bf16[128,3072]{1,0:T(8,128)(2,1)S(1)}) custom-call(s32[16]{0:T(128)S(1)} %min.12.asked_ref, f32[8,128]{1,0:T(8,128)S(1)} %slice_bitcast_fusion.norm_ref, f32[2,2,128,128]{3,2,1,0:T(8,128)S(1)} %get-tuple-element.48.refs_0_.refs_3_.refs_1_, bf16[4,128,3072]{2,1,0:T(8,128)(2,1)S(1)} %bitcast.169, ...), custom_call_target="tpu_custom_call" | custom-call | flops 1024 | bytes 1024 | tf_op jit(solution)/shard_map/pallas_call | solution.py:80
  82.4 0.8 collective-permute-start.20
  83.2 1.9 %collective-permute-start.21 = (f32[9,2,128]{2,0,1:T(8,128)S(1)}, f32[9,2,128]{2,0,1:T(8,128)S(1)}, u32[]{:S(2)}, u32[]{:S(2)}) collective-permute-start(f32[9,2,128]{2,0,1:T(8,128)S(1)} %get-tuple-element.83), channel_id=1, source_target_pairs={{0,2},{1,7},{2,4},{3,1},{4,6},{5,3},{6,0},{7,5},{8,10},{9,15},{10,... | collective-permute-start | bytes 27656 | tf_op jit(solution)/shard_map/ppermute | solution.py:47
  85.1 1.2 collective-permute-done.22
  86.4 2.7 %collective-permute-start.24 = (bf16[128,3072]{1,0:T(8,128)(2,1)S(1)}, bf16[128,3072]{1,0:T(8,128)(2,1)S(1)}, u32[]{:S(2)}, u32[]{:S(2)}) collective-permute-start(bf16[128,3072]{1,0:T(8,128)(2,1)S(1)} %get-tuple-element.50), channel_id=1, source_target_pairs={{0,2},{1,7},{2,4},{3,1},{4,6},{5,3},{6,0},{7,5},{8,10},{9,15},{10,... | collective-permute-start | bytes 2359304 | tf_op jit(solution)/shard_map/ppermute | solution.py:47
  90.7 3.2 %collective-permute-start.26 = (bf16[128,3072]{1,0:T(8,128)(2,1)S(1)}, bf16[128,3072]{1,0:T(8,128)(2,1)S(1)}, u32[]{:S(2)}, u32[]{:S(2)}) collective-permute-start(bf16[128,3072]{1,0:T(8,128)(2,1)S(1)} %convolution_convert_fusion.2), channel_id=1, source_target_pairs={{0,64},{1,65},{2,66},{3,67},{4,68},{5,69},{6,70},{7,71},{8,72},{9,... | collective-permute-start | bytes 2359304 | tf_op jit(solution)/shard_map/ppermute | solution.py:47
  93.9 2.6 %collective-permute-start.28 = (bf16[128,3072]{1,0:T(8,128)(2,1)S(1)}, bf16[128,3072]{1,0:T(8,128)(2,1)S(1)}, u32[]{:S(2)}, u32[]{:S(2)}) collective-permute-start(bf16[128,3072]{1,0:T(8,128)(2,1)S(1)} %convolution_convert_fusion.1), channel_id=1, source_target_pairs={{0,16},{1,49},{2,18},{3,51},{4,20},{5,53},{6,22},{7,55},{8,24},{9,... | collective-permute-start | bytes 2359304 | tf_op jit(solution)/shard_map/ppermute | solution.py:47
  96.6 6.1 %shard_map.80 = bf16[4,128,3072]{2,1,0:T(8,128)(2,1)S(1)} custom-call(s32[16]{0:T(128)S(1)} %min.12.asked_ref, f32[8,128]{1,0:T(8,128)S(1)} %fusion.22.norm_ref, f32[6,2,128,128]{3,2,1,0:T(8,128)S(1)} %copy-done.8, f32[2,2,128,128]{3,2,1,0:T(8,128)S(1)} %get-tuple-element.48.refs_0_.refs_3_.refs_1_, bf16[128,3072]{1,0:T(8,128)(2,1)S(1)} %copy-done.6, ...), custom_call_target="tpu_custom_call" | custom-call | flops 1024 | bytes 1024 | tf_op jit(solution)/shard_map/pallas_call | solution.py:80
  102.7 1.1 collective-permute-done.25.refs_6_
  103.8 2.4 %collective-permute-done.24.refs_11_ = bf16[128,3072]{1,0:T(8,128)(2,1)S(1)} collective-permute-done((bf16[128,3072]{1,0:T(8,128)(2,1)S(1)}, bf16[128,3072]{1,0:T(8,128)(2,1)S(1)}, u32[]{:S(2)}, u32[]{:S(2)}) %collective-permute-start.24) | collective-permute-done | bytes 786464 | tf_op jit(solution)/shard_map/ppermute | solution.py:47
  106.2 2.0 %shard_map.78 = (bf16[128,3072]{1,0:T(8,128)(2,1)S(1)}, bf16[128,3072]{1,0:T(8,128)(2,1)S(1)}) custom-call(s32[16]{0:T(128)S(1)} %min.12.asked_ref, f32[8,128]{1,0:T(8,128)S(1)} %fusion.22.norm_ref, f32[6,2,128,128]{3,2,1,0:T(8,128)S(1)} %copy-done.8, bf16[4,128,3072]{2,1,0:T(8,128)(2,1)S(1)} %bitcast.171, bf16[4,128,3072]{2,1,0:T(8,128)(2,1)S(1)} %bitcast.187, ...), custom_call_target="tpu_custom_call" | custom-call | flops 1024 | bytes 1024 | tf_op jit(solution)/shard_map/pallas_call | solution.py:80
  108.6 3.3 %collective-permute-done.28 = bf16[128,3072]{1,0:T(8,128)(2,1)S(1)} collective-permute-done((bf16[128,3072]{1,0:T(8,128)(2,1)S(1)}, bf16[128,3072]{1,0:T(8,128)(2,1)S(1)}, u32[]{:S(2)}, u32[]{:S(2)}) %collective-permute-start.28) | collective-permute-done | bytes 786464 | tf_op jit(solution)/shard_map/ppermute | solution.py:47
  111.9 0.5 collective-permute-start.29
  112.8 2.7 %collective-permute-start.27 = (bf16[128,3072]{1,0:T(8,128)(2,1)S(1)}, bf16[128,3072]{1,0:T(8,128)(2,1)S(1)}, u32[]{:S(2)}, u32[]{:S(2)}) collective-permute-start(bf16[128,3072]{1,0:T(8,128)(2,1)S(1)} %add_convert_fusion.1), channel_id=1, source_target_pairs={{0,16},{1,49},{2,18},{3,51},{4,20},{5,53},{6,22},{7,55},{8,24},{9,... | collective-permute-start | bytes 2359304 | tf_op jit(solution)/shard_map/ppermute | solution.py:47
  115.5 1.2 collective-permute-start.31
  117.0 0.5 add_convert_fusion
  117.5 2.7 %collective-permute-start.34 = (bf16[128,3072]{1,0:T(8,128)(2,1)S(1)}, bf16[128,3072]{1,0:T(8,128)(2,1)S(1)}, u32[]{:S(2)}, u32[]{:S(2)}) collective-permute-start(bf16[128,3072]{1,0:T(8,128)(2,1)S(1)} %add_convert_fusion), channel_id=1, source_target_pairs={{0,64},{1,65},{2,66},{3,67},{4,68},{5,69},{6,70},{7,71},{8,72},{9,... | collective-permute-start | bytes 2359304 | tf_op jit(solution)/shard_map/ppermute | solution.py:47
  120.2 4.2 %collective-permute-done.27 = bf16[128,3072]{1,0:T(8,128)(2,1)S(1)} collective-permute-done((bf16[128,3072]{1,0:T(8,128)(2,1)S(1)}, bf16[128,3072]{1,0:T(8,128)(2,1)S(1)}, u32[]{:S(2)}, u32[]{:S(2)}) %collective-permute-start.27) | collective-permute-done | bytes 786464 | tf_op jit(solution)/shard_map/ppermute | solution.py:47
  125.3 3.5 %collective-permute-start.37 = (bf16[128,3072]{1,0:T(8,128)(2,1)S(1)}, bf16[128,3072]{1,0:T(8,128)(2,1)S(1)}, u32[]{:S(2)}, u32[]{:S(2)}) collective-permute-start(bf16[128,3072]{1,0:T(8,128)(2,1)S(1)} %fusion), channel_id=1, source_target_pairs={{0,16},{1,49},{2,18},{3,51},{4,20},{5,53},{6,22},{7,55},{8,24},{9,... | collective-permute-start | bytes 2359304 | tf_op jit(solution)/shard_map/ppermute | solution.py:47
  128.8 0.5 fusion.38
  129.4 3.5 %shard_map.79 = f32[128,3072]{1,0:T(8,128)S(1)} custom-call(s32[16]{0:T(128)S(1)} %min.12.asked_ref, f32[8,128]{1,0:T(8,128)S(1)} %fusion.22.norm_ref, f32[6,2,128,128]{3,2,1,0:T(8,128)S(1)} %copy-done.8, bf16[4,128,3072]{2,1,0:T(8,128)(2,1)S(1)} %bitcast.173, bf16[4,128,3072]{2,1,0:T(8,128)(2,1)S(1)} %bitcast.189, bf16[128,1024]{1,0:T(8,128)(2,1)S(1)} %bitcast.193, ...), custom_call_target="tpu_custom_call" | custom-call | flops 1024 | bytes 1024 | tf_op jit(solution)/shard_map/pallas_call | solution.py:80
  132.9 1.5 collective-permute-done.32.refs_10_
  134.4 2.6 %shard_map.82 = (bf16[128,3072]{1,0:T(8,128)(2,1)S(1)}, bf16[128,3072]{1,0:T(8,128)(2,1)S(1)}, bf16[128,3072]{1,0:T(8,128)(2,1)S(1)}) custom-call(s32[16]{0:T(128)S(1)} %min.12.asked_ref, f32[8,128]{1,0:T(8,128)S(1)} %fusion.22.norm_ref, f32[6,2,128,128]{3,2,1,0:T(8,128)S(1)} %copy-done.8, bf16[4,128,3072]{2,1,0:T(8,128)(2,1)S(1)} %bitcast.174, ...), custom_call_target="tpu_custom_call" | custom-call | flops 1024 | bytes 1024 | tf_op jit(solution)/shard_map/pallas_call | solution.py:80
  137.0 3.0 %collective-permute-start.33 = (bf16[128,3072]{1,0:T(8,128)(2,1)S(1)}, bf16[128,3072]{1,0:T(8,128)(2,1)S(1)}, u32[]{:S(2)}, u32[]{:S(2)}) collective-permute-start(bf16[128,3072]{1,0:T(8,128)(2,1)S(1)} %get-tuple-element.62), channel_id=1, source_target_pairs={{0,2},{1,7},{2,4},{3,1},{4,6},{5,3},{6,0},{7,5},{8,10},{9,15},{10,... | collective-permute-start | bytes 2359304 | tf_op jit(solution)/shard_map/ppermute | solution.py:47
  140.0 0.6 collective-permute-start.36
  141.0 1.3 collective-permute-done.30
  142.3 7.3 %shard_map.81 = f32[4,128,3072]{2,1,0:T(8,128)} custom-call(s32[16]{0:T(128)S(1)} %min.12.asked_ref, f32[8,128]{1,0:T(8,128)S(1)} %fusion.22.norm_ref, f32[6,2,128,128]{3,2,1,0:T(8,128)S(1)} %copy-done.8, f32[2,2,128,128]{3,2,1,0:T(8,128)S(1)} %get-tuple-element.48.refs_0_.refs_3_.refs_1_, bf16[128,3072]{1,0:T(8,128)(2,1)S(1)} %copy-done.6, ...), custom_call_target="tpu_custom_call" | custom-call | flops 1024 | bytes 1024 | tf_op jit(solution)/shard_map/pallas_call | solution.py:80
  149.7 1.6 add_multiply_fusion
  151.2 4.3 %collective-permute-done.33 = bf16[128,3072]{1,0:T(8,128)(2,1)S(1)} collective-permute-done((bf16[128,3072]{1,0:T(8,128)(2,1)S(1)}, bf16[128,3072]{1,0:T(8,128)(2,1)S(1)}, u32[]{:S(2)}, u32[]{:S(2)}) %collective-permute-start.33) | collective-permute-done | bytes 786464 | tf_op jit(solution)/shard_map/ppermute | solution.py:47
  155.6 1.2 collective-permute-done.36
  156.8 1.6 collective-permute-done.35
  158.3 1.6 add_multiply_fusion.1
  (161 shorter events, 9.7 us)
Async XLA Ops:
  0.6 22.8 %collective-permute-start.4 = (bf16[512,3072]{1,0:T(8,128)(2,1)}, bf16[512,3072]{1,0:T(8,128)(2,1)S(1)}, u32[]{:S(2)}, u32[]{:S(2)}) collective-permute-start(bf16[512,3072]{1,0:T(8,128)(2,1)} %param.6), channel_id=1, source_target_pairs={{0,1},{1,0},{2,3},{3,2},{4,5},{5,4},{6,7},{7,6},{8,9},{9,8},{10,11... | collective-permute-start | bytes 9437192 | tf_op jit(solution)/shard_map/ppermute | solution.py:47
  2.9 2.5 %collective-permute-start = (s32[1,16]{1,0:T(1,128)S(1)}, s32[1,16]{1,0:T(1,128)S(1)}, u32[]{:S(2)}, u32[]{:S(2)}) collective-permute-start(s32[1,16]{1,0:T(1,128)S(1)} %add_bitcast_fusion), channel_id=1, source_target_pairs={{0,8},{1,9},{2,10},{3,11},{4,12},{5,13},{6,14},{7,15},{8,0},{9,1},... | collective-permute-start | bytes 200 | tf_op jit(solution)/shard_map/ppermute | solution.py:47
  4.3 19.2 %collective-permute-start.5 = (bf16[128,3072]{1,0:T(8,128)(2,1)}, bf16[128,3072]{1,0:T(8,128)(2,1)}, u32[]{:S(2)}, u32[]{:S(2)}) collective-permute-start(bf16[128,3072]{1,0:T(8,128)(2,1)} %refs_2_.3), channel_id=1, source_target_pairs={{0,8},{1,9},{2,10},{3,11},{4,12},{5,13},{6,14},{7,15},{8,0},{9,1},... | collective-permute-start | bytes 2359304 | tf_op jit(solution)/shard_map/ppermute | solution.py:47
  5.4 5.8 %collective-permute-start.2 = (s32[2,16]{1,0:T(2,128)S(1)}, s32[2,16]{1,0:T(2,128)S(1)}, u32[]{:S(2)}, u32[]{:S(2)}) collective-permute-start(s32[2,16]{1,0:T(2,128)S(1)} %get-tuple-element.91), channel_id=1, source_target_pairs={{0,4},{1,5},{2,6},{3,7},{4,0},{5,1},{6,2},{7,3},{8,12},{9,13},{10,... | collective-permute-start | bytes 392 | tf_op jit(solution)/shard_map/ppermute | solution.py:47
  8.4 3.6 %collective-permute-start.1 = (s32[2,16]{1,0:T(2,128)S(1)}, s32[2,16]{1,0:T(2,128)S(1)}, u32[]{:S(2)}, u32[]{:S(2)}) collective-permute-start(s32[2,16]{1,0:T(2,128)S(1)} %get-tuple-element.91), channel_id=1, source_target_pairs={{0,6},{1,3},{2,0},{3,5},{4,2},{5,7},{6,4},{7,1},{8,14},{9,11},{10,... | collective-permute-start | bytes 392 | tf_op jit(solution)/shard_map/ppermute | solution.py:47
  8.8 3.2 %collective-permute-start.3 = (s32[2,16]{1,0:T(2,128)S(1)}, s32[2,16]{1,0:T(2,128)S(1)}, u32[]{:S(2)}, u32[]{:S(2)}) collective-permute-start(s32[2,16]{1,0:T(2,128)S(1)} %get-tuple-element.91), channel_id=1, source_target_pairs={{0,2},{1,7},{2,4},{3,1},{4,6},{5,3},{6,0},{7,5},{8,10},{9,15},{10,... | collective-permute-start | bytes 392 | tf_op jit(solution)/shard_map/ppermute | solution.py:47
  12.8 44.9 %copy-start.5 = (bf16[128,3072]{1,0:T(8,128)(2,1)S(1)}, bf16[128,3072]{1,0:T(8,128)(2,1)}, u32[]{:S(2)}) copy-start(bf16[128,3072]{1,0:T(8,128)(2,1)} %refs_2_.3) | copy-start | bytes 2359300
  12.8 13.1 %collective-permute-start.11 = (bf16[128,3072]{1,0:T(8,128)(2,1)}, bf16[128,3072]{1,0:T(8,128)(2,1)S(1)}, u32[]{:S(2)}, u32[]{:S(2)}) collective-permute-start(bf16[128,3072]{1,0:T(8,128)(2,1)} %refs_4_.1), channel_id=1, source_target_pairs={{0,16},{1,49},{2,18},{3,51},{4,20},{5,53},{6,22},{7,55},{8,24},{9,... | collective-permute-start | bytes 2359304 | tf_op jit(solution)/shard_map/ppermute | solution.py:47
  16.7 19.2 %collective-permute-start.7 = (bf16[128,3072]{1,0:T(8,128)(2,1)}, bf16[128,3072]{1,0:T(8,128)(2,1)S(1)}, u32[]{:S(2)}, u32[]{:S(2)}) collective-permute-start(bf16[128,3072]{1,0:T(8,128)(2,1)} %refs_2_.3), channel_id=1, source_target_pairs={{0,6},{1,3},{2,0},{3,5},{4,2},{5,7},{6,4},{7,1},{8,14},{9,11},{10,... | collective-permute-start | bytes 2359304 | tf_op jit(solution)/shard_map/ppermute | solution.py:47
  16.7 19.7 %collective-permute-start.6 = (bf16[128,3072]{1,0:T(8,128)(2,1)}, bf16[128,3072]{1,0:T(8,128)(2,1)S(1)}, u32[]{:S(2)}, u32[]{:S(2)}) collective-permute-start(bf16[128,3072]{1,0:T(8,128)(2,1)} %refs_2_.3), channel_id=1, source_target_pairs={{0,2},{1,7},{2,4},{3,1},{4,6},{5,3},{6,0},{7,5},{8,10},{9,15},{10,... | collective-permute-start | bytes 2359304 | tf_op jit(solution)/shard_map/ppermute | solution.py:47
  23.4 34.7 %copy-start.1 = (bf16[512,3072]{1,0:T(8,128)(2,1)}, bf16[512,3072]{1,0:T(8,128)(2,1)S(1)}, u32[]{:S(2)}) copy-start(bf16[512,3072]{1,0:T(8,128)(2,1)S(1)} %collective-permute-done.4) | copy-start | bytes 9437188
  25.9 33.5 %copy-start.22 = (bf16[128,3072]{1,0:T(8,128)(2,1)}, bf16[128,3072]{1,0:T(8,128)(2,1)S(1)}, u32[]{:S(2)}) copy-start(bf16[128,3072]{1,0:T(8,128)(2,1)S(1)} %collective-permute-done.11.refs_7_) | copy-start | bytes 2359300
  25.9 20.0 %collective-permute-start.8 = (bf16[128,3072]{1,0:T(8,128)(2,1)}, bf16[128,3072]{1,0:T(8,128)(2,1)S(1)}, u32[]{:S(2)}, u32[]{:S(2)}) collective-permute-start(bf16[128,3072]{1,0:T(8,128)(2,1)} %collective-permute-done.5.refs_3_.refs_6_), channel_id=1, source_target_pairs={{0,2},{1,7},{2,4},{3,1},{4,6},{5,3},{6,0},{7,5},{8,10},{9,15},{10,... | collective-permute-start | bytes 2359304 | tf_op jit(solution)/shard_map/ppermute | solution.py:47
  28.9 20.3 %collective-permute-start.12 = (bf16[128,3072]{1,0:T(8,128)(2,1)S(1)}, bf16[128,3072]{1,0:T(8,128)(2,1)S(1)}, u32[]{:S(2)}, u32[]{:S(2)}) collective-permute-start(bf16[128,3072]{1,0:T(8,128)(2,1)S(1)} %collective-permute-done.11.refs_7_), channel_id=1, source_target_pairs={{0,16},{1,49},{2,18},{3,51},{4,20},{5,53},{6,22},{7,55},{8,24},{9,... | collective-permute-start | bytes 2359304 | tf_op jit(solution)/shard_map/ppermute | solution.py:47
  32.2 20.1 %collective-permute-start.13 = (bf16[128,3072]{1,0:T(8,128)(2,1)}, bf16[128,3072]{1,0:T(8,128)(2,1)S(1)}, u32[]{:S(2)}, u32[]{:S(2)}) collective-permute-start(bf16[128,3072]{1,0:T(8,128)(2,1)} %refs_4_.1), channel_id=1, source_target_pairs={{0,64},{1,65},{2,66},{3,67},{4,68},{5,69},{6,70},{7,71},{8,72},{9,... | collective-permute-start | bytes 2359304 | tf_op jit(solution)/shard_map/ppermute | solution.py:47
  35.9 26.1 %copy-start.13 = (bf16[128,3072]{1,0:T(8,128)(2,1)}, bf16[128,3072]{1,0:T(8,128)(2,1)S(1)}, u32[]{:S(2)}) copy-start(bf16[128,3072]{1,0:T(8,128)(2,1)S(1)} %collective-permute-done.7.refs_9_.refs_3_) | copy-start | bytes 2359300
  36.3 25.6 %copy-start.15 = (bf16[128,3072]{1,0:T(8,128)(2,1)}, bf16[128,3072]{1,0:T(8,128)(2,1)S(1)}, u32[]{:S(2)}) copy-start(bf16[128,3072]{1,0:T(8,128)(2,1)S(1)} %collective-permute-done.6.refs_6_.refs_5_) | copy-start | bytes 2359300
  36.3 16.0 %collective-permute-start.10 = (bf16[128,3072]{1,0:T(8,128)(2,1)}, bf16[128,3072]{1,0:T(8,128)(2,1)S(1)}, u32[]{:S(2)}, u32[]{:S(2)}) collective-permute-start(bf16[128,3072]{1,0:T(8,128)(2,1)} %refs_4_.1), channel_id=1, source_target_pairs={{0,48},{1,17},{2,50},{3,19},{4,52},{5,21},{6,54},{7,23},{8,56},{9,... | collective-permute-start | bytes 2359304 | tf_op jit(solution)/shard_map/ppermute | solution.py:47
  36.3 21.4 %collective-permute-start.9 = (bf16[128,3072]{1,0:T(8,128)(2,1)}, bf16[128,3072]{1,0:T(8,128)(2,1)S(1)}, u32[]{:S(2)}, u32[]{:S(2)}) collective-permute-start(bf16[128,3072]{1,0:T(8,128)(2,1)} %collective-permute-done.5.refs_3_.refs_6_), channel_id=1, source_target_pairs={{0,6},{1,3},{2,0},{3,5},{4,2},{5,7},{6,4},{7,1},{8,14},{9,11},{10,... | collective-permute-start | bytes 2359304 | tf_op jit(solution)/shard_map/ppermute | solution.py:47
  45.9 16.1 %copy-start.17 = (bf16[128,3072]{1,0:T(8,128)(2,1)}, bf16[128,3072]{1,0:T(8,128)(2,1)S(1)}, u32[]{:S(2)}) copy-start(bf16[128,3072]{1,0:T(8,128)(2,1)S(1)} %collective-permute-done.8.refs_12_.refs_9_) | copy-start | bytes 2359300
  45.9 27.3 %collective-permute-start.17 = (bf16[128,3072]{1,0:T(8,128)(2,1)S(1)}, bf16[128,3072]{1,0:T(8,128)(2,1)S(1)}, u32[]{:S(2)}, u32[]{:S(2)}) collective-permute-start(bf16[128,3072]{1,0:T(8,128)(2,1)S(1)} %collective-permute-done.6.refs_6_.refs_5_), channel_id=1, source_target_pairs={{0,2},{1,7},{2,4},{3,1},{4,6},{5,3},{6,0},{7,5},{8,10},{9,15},{10,... | collective-permute-start | bytes 2359304 | tf_op jit(solution)/shard_map/ppermute | solution.py:47
  52.3 23.3 %collective-permute-start.14 = (bf16[128,3072]{1,0:T(8,128)(2,1)S(1)}, bf16[128,3072]{1,0:T(8,128)(2,1)S(1)}, u32[]{:S(2)}, u32[]{:S(2)}) collective-permute-start(bf16[128,3072]{1,0:T(8,128)(2,1)S(1)} %collective-permute-done.13.refs_8_), channel_id=1, source_target_pairs={{0,48},{1,17},{2,50},{3,19},{4,52},{5,21},{6,54},{7,23},{8,56},{9,... | collective-permute-start | bytes 2359304 | tf_op jit(solution)/shard_map/ppermute | solution.py:47
  52.3 23.7 %collective-permute-start.15 = (bf16[128,3072]{1,0:T(8,128)(2,1)S(1)}, bf16[128,3072]{1,0:T(8,128)(2,1)S(1)}, u32[]{:S(2)}, u32[]{:S(2)}) collective-permute-start(bf16[128,3072]{1,0:T(8,128)(2,1)S(1)} %collective-permute-done.12.refs_6_), channel_id=1, source_target_pairs={{0,64},{1,65},{2,66},{3,67},{4,68},{5,69},{6,70},{7,71},{8,72},{9,... | collective-permute-start | bytes 2359304 | tf_op jit(solution)/shard_map/ppermute | solution.py:47
  55.0 21.4 %collective-permute-start.16 = (bf16[128,3072]{1,0:T(8,128)(2,1)S(1)}, bf16[128,3072]{1,0:T(8,128)(2,1)S(1)}, u32[]{:S(2)}, u32[]{:S(2)}) collective-permute-start(bf16[128,3072]{1,0:T(8,128)(2,1)S(1)} %collective-permute-done.13.refs_8_), channel_id=1, source_target_pairs={{0,16},{1,49},{2,18},{3,51},{4,20},{5,53},{6,22},{7,55},{8,24},{9,... | collective-permute-start | bytes 2359304 | tf_op jit(solution)/shard_map/ppermute | solution.py:47
  57.7 4.2 %copy-start.19 = (bf16[128,3072]{1,0:T(8,128)(2,1)}, bf16[128,3072]{1,0:T(8,128)(2,1)S(1)}, u32[]{:S(2)}) copy-start(bf16[128,3072]{1,0:T(8,128)(2,1)S(1)} %collective-permute-done.9.refs_15_.refs_7_) | copy-start | bytes 2359300
  57.7 15.5 %collective-permute-start.18 = (bf16[128,3072]{1,0:T(8,128)(2,1)S(1)}, bf16[128,3072]{1,0:T(8,128)(2,1)S(1)}, u32[]{:S(2)}, u32[]{:S(2)}) collective-permute-start(bf16[128,3072]{1,0:T(8,128)(2,1)S(1)} %collective-permute-done.9.refs_15_.refs_7_), channel_id=1, source_target_pairs={{0,6},{1,3},{2,0},{3,5},{4,2},{5,7},{6,4},{7,1},{8,14},{9,11},{10,... | collective-permute-start | bytes 2359304 | tf_op jit(solution)/shard_map/ppermute | solution.py:47
  69.4 6.1 %copy-start.7 = (f32[6,2,128,128]{3,2,1,0:T(8,128)}, f32[6,2,128,128]{3,2,1,0:T(8,128)S(1)}, u32[]{:S(2)}) copy-start(f32[6,2,128,128]{3,2,1,0:T(8,128)S(1)} %get-tuple-element.47.refs_0_.refs_3_.refs_6_) | copy-start | bytes 2359300
  77.7 4.5 %collective-permute-start.19 = (f32[8,2,128]{2,0,1:T(8,128)S(1)}, f32[8,2,128]{2,0,1:T(8,128)S(1)}, u32[]{:S(2)}, u32[]{:S(2)}) collective-permute-start(f32[8,2,128]{2,0,1:T(8,128)S(1)} %concatenate.38), channel_id=1, source_target_pairs={{0,8},{1,9},{2,10},{3,11},{4,12},{5,13},{6,14},{7,15},{8,0},{9,1},... | collective-permute-start | bytes 24584 | tf_op jit(solution)/shard_map/ppermute | solution.py:47
  80.3 8.9 %copy-start.37 = (f32[1024,128]{0,1:T(8,128)S(1)}, f32[1024,128]{0,1:T(8,128)}, u32[]{:S(2)}) copy-start(f32[1024,128]{0,1:T(8,128)} %copy-done.36) | copy-start | bytes 1572868
  80.3 16.2 %copy-start.20 = (bf16[128,3072]{1,0:T(8,128)(2,1)S(1)}, bf16[128,3072]{1,0:T(8,128)(2,1)}, u32[]{:S(2)}) copy-start(bf16[128,3072]{1,0:T(8,128)(2,1)} %copy-done.19) | copy-start | bytes 2359300
  82.2 7.2 %copy-start.6 = (bf16[128,3072]{1,0:T(8,128)(2,1)S(1)}, bf16[128,3072]{1,0:T(8,128)(2,1)}, u32[]{:S(2)}) copy-start(bf16[128,3072]{1,0:T(8,128)(2,1)} %refs_2_.3) | copy-start | bytes 2359300
  82.3 4.1 %collective-permute-start.22 = (f32[8,2,128]{2,0,1:T(8,128)S(1)}, f32[8,2,128]{2,0,1:T(8,128)S(1)}, u32[]{:S(2)}, u32[]{:S(2)}) collective-permute-start(f32[8,2,128]{2,0,1:T(8,128)S(1)} %pad_maximum_fusion.3), channel_id=1, source_target_pairs={{0,4},{1,5},{2,6},{3,7},{4,0},{5,1},{6,2},{7,3},{8,12},{9,13},{10,... | collective-permute-start | bytes 24584 | tf_op jit(solution)/shard_map/ppermute | solution.py:47
  82.4 6.7 %collective-permute-start.20 = (f32[9,2,128]{2,0,1:T(8,128)S(1)}, f32[9,2,128]{2,0,1:T(8,128)S(1)}, u32[]{:S(2)}, u32[]{:S(2)}) collective-permute-start(f32[9,2,128]{2,0,1:T(8,128)S(1)} %get-tuple-element.82), channel_id=1, source_target_pairs={{0,6},{1,3},{2,0},{3,5},{4,2},{5,7},{6,4},{7,1},{8,14},{9,11},{10,... | collective-permute-start | bytes 27656 | tf_op jit(solution)/shard_map/ppermute | solution.py:47
  83.2 5.9 %collective-permute-start.21 = (f32[9,2,128]{2,0,1:T(8,128)S(1)}, f32[9,2,128]{2,0,1:T(8,128)S(1)}, u32[]{:S(2)}, u32[]{:S(2)}) collective-permute-start(f32[9,2,128]{2,0,1:T(8,128)S(1)} %get-tuple-element.83), channel_id=1, source_target_pairs={{0,2},{1,7},{2,4},{3,1},{4,6},{5,3},{6,0},{7,5},{8,10},{9,15},{10,... | collective-permute-start | bytes 27656 | tf_op jit(solution)/shard_map/ppermute | solution.py:47
  86.4 17.4 %collective-permute-start.25 = (bf16[128,3072]{1,0:T(8,128)(2,1)S(1)}, bf16[128,3072]{1,0:T(8,128)(2,1)S(1)}, u32[]{:S(2)}, u32[]{:S(2)}) collective-permute-start(bf16[128,3072]{1,0:T(8,128)(2,1)S(1)} %get-tuple-element.52), channel_id=1, source_target_pairs={{0,6},{1,3},{2,0},{3,5},{4,2},{5,7},{6,4},{7,1},{8,14},{9,11},{10,... | collective-permute-start | bytes 2359304 | tf_op jit(solution)/shard_map/ppermute | solution.py:47
  86.4 19.8 %collective-permute-start.24 = (bf16[128,3072]{1,0:T(8,128)(2,1)S(1)}, bf16[128,3072]{1,0:T(8,128)(2,1)S(1)}, u32[]{:S(2)}, u32[]{:S(2)}) collective-permute-start(bf16[128,3072]{1,0:T(8,128)(2,1)S(1)} %get-tuple-element.50), channel_id=1, source_target_pairs={{0,2},{1,7},{2,4},{3,1},{4,6},{5,3},{6,0},{7,5},{8,10},{9,15},{10,... | collective-permute-start | bytes 2359304 | tf_op jit(solution)/shard_map/ppermute | solution.py:47
  89.4 7.1 %copy-start.16 = (bf16[128,3072]{1,0:T(8,128)(2,1)S(1)}, bf16[128,3072]{1,0:T(8,128)(2,1)}, u32[]{:S(2)}) copy-start(bf16[128,3072]{1,0:T(8,128)(2,1)} %copy-done.15) | copy-start | bytes 2359300
  89.4 7.1 %copy-start.18 = (bf16[128,3072]{1,0:T(8,128)(2,1)S(1)}, bf16[128,3072]{1,0:T(8,128)(2,1)}, u32[]{:S(2)}) copy-start(bf16[128,3072]{1,0:T(8,128)(2,1)} %copy-done.17) | copy-start | bytes 2359300
  89.8 6.7 %copy-start.8 = (f32[6,2,128,128]{3,2,1,0:T(8,128)S(1)}, f32[6,2,128,128]{3,2,1,0:T(8,128)}, u32[]{:S(2)}) copy-start(f32[6,2,128,128]{3,2,1,0:T(8,128)} %copy-done.7) | copy-start | bytes 2359300
  89.8 6.7 %copy-start.10 = (bf16[128,3072]{1,0:T(8,128)(2,1)S(1)}, bf16[128,3072]{1,0:T(8,128)(2,1)}, u32[]{:S(2)}) copy-start(bf16[128,3072]{1,0:T(8,128)(2,1)} %copy-done.9) | copy-start | bytes 2359300
  89.8 6.7 %copy-start.12 = (bf16[128,3072]{1,0:T(8,128)(2,1)S(1)}, bf16[128,3072]{1,0:T(8,128)(2,1)}, u32[]{:S(2)}) copy-start(bf16[128,3072]{1,0:T(8,128)(2,1)} %copy-done.11) | copy-start | bytes 2359300
  89.8 6.7 %copy-start.14 = (bf16[128,3072]{1,0:T(8,128)(2,1)S(1)}, bf16[128,3072]{1,0:T(8,128)(2,1)}, u32[]{:S(2)}) copy-start(bf16[128,3072]{1,0:T(8,128)(2,1)} %copy-done.13) | copy-start | bytes 2359300
  90.6 17.5 %collective-permute-start.23 = (bf16[128,3072]{1,0:T(8,128)(2,1)S(1)}, bf16[128,3072]{1,0:T(8,128)(2,1)S(1)}, u32[]{:S(2)}, u32[]{:S(2)}) collective-permute-start(bf16[128,3072]{1,0:T(8,128)(2,1)S(1)} %convolution_convert_fusion.3), channel_id=1, source_target_pairs={{0,48},{1,17},{2,50},{3,19},{4,52},{5,21},{6,54},{7,23},{8,56},{9,... | collective-permute-start | bytes 2359304 | tf_op jit(solution)/shard_map/ppermute | solution.py:47
  90.7 17.9 %collective-permute-start.26 = (bf16[128,3072]{1,0:T(8,128)(2,1)S(1)}, bf16[128,3072]{1,0:T(8,128)(2,1)S(1)}, u32[]{:S(2)}, u32[]{:S(2)}) collective-permute-start(bf16[128,3072]{1,0:T(8,128)(2,1)S(1)} %convolution_convert_fusion.2), channel_id=1, source_target_pairs={{0,64},{1,65},{2,66},{3,67},{4,68},{5,69},{6,70},{7,71},{8,72},{9,... | collective-permute-start | bytes 2359304 | tf_op jit(solution)/shard_map/ppermute | solution.py:47
  93.9 18.0 %collective-permute-start.28 = (bf16[128,3072]{1,0:T(8,128)(2,1)S(1)}, bf16[128,3072]{1,0:T(8,128)(2,1)S(1)}, u32[]{:S(2)}, u32[]{:S(2)}) collective-permute-start(bf16[128,3072]{1,0:T(8,128)(2,1)S(1)} %convolution_convert_fusion.1), channel_id=1, source_target_pairs={{0,16},{1,49},{2,18},{3,51},{4,20},{5,53},{6,22},{7,55},{8,24},{9,... | collective-permute-start | bytes 2359304 | tf_op jit(solution)/shard_map/ppermute | solution.py:47
  96.6 9.6 %copy-start.4 = (bf16[512,3072]{1,0:T(8,128)(2,1)S(1)}, bf16[512,3072]{1,0:T(8,128)(2,1)}, u32[]{:S(2)}) copy-start(bf16[512,3072]{1,0:T(8,128)(2,1)} %copy-done.1) | copy-start | bytes 9437188
  111.9 12.5 %collective-permute-start.29 = (bf16[4,128,3072]{2,1,0:T(8,128)(2,1)S(1)}, bf16[4,128,3072]{2,1,0:T(8,128)(2,1)S(1)}, u32[]{:S(2)}, u32[]{:S(2)}) collective-permute-start(bf16[4,128,3072]{2,1,0:T(8,128)(2,1)S(1)} %shard_map.80), channel_id=1, source_target_pairs={{0,1},{1,0},{2,3},{3,2},{4,5},{5,4},{6,7},{7,6},{8,9},{9,8},{10,11... | collective-permute-start | bytes 9437192 | tf_op jit(solution)/shard_map/ppermute | solution.py:47
  112.8 11.6 %collective-permute-start.27 = (bf16[128,3072]{1,0:T(8,128)(2,1)S(1)}, bf16[128,3072]{1,0:T(8,128)(2,1)S(1)}, u32[]{:S(2)}, u32[]{:S(2)}) collective-permute-start(bf16[128,3072]{1,0:T(8,128)(2,1)S(1)} %add_convert_fusion.1), channel_id=1, source_target_pairs={{0,16},{1,49},{2,18},{3,51},{4,20},{5,53},{6,22},{7,55},{8,24},{9,... | collective-permute-start | bytes 2359304 | tf_op jit(solution)/shard_map/ppermute | solution.py:47
  115.5 18.9 %collective-permute-start.31 = (bf16[128,3072]{1,0:T(8,128)(2,1)S(1)}, bf16[128,3072]{1,0:T(8,128)(2,1)S(1)}, u32[]{:S(2)}, u32[]{:S(2)}) collective-permute-start(bf16[128,3072]{1,0:T(8,128)(2,1)S(1)} %get-tuple-element.54), channel_id=1, source_target_pairs={{0,2},{1,7},{2,4},{3,1},{4,6},{5,3},{6,0},{7,5},{8,10},{9,15},{10,... | collective-permute-start | bytes 2359304 | tf_op jit(solution)/shard_map/ppermute | solution.py:47
  116.7 17.7 %collective-permute-start.32 = (bf16[128,3072]{1,0:T(8,128)(2,1)S(1)}, bf16[128,3072]{1,0:T(8,128)(2,1)S(1)}, u32[]{:S(2)}, u32[]{:S(2)}) collective-permute-start(bf16[128,3072]{1,0:T(8,128)(2,1)S(1)} %get-tuple-element.60), channel_id=1, source_target_pairs={{0,6},{1,3},{2,0},{3,5},{4,2},{5,7},{6,4},{7,1},{8,14},{9,11},{10,... | collective-permute-start | bytes 2359304 | tf_op jit(solution)/shard_map/ppermute | solution.py:47
  117.0 12.4 %copy-start.31 = (bf16[128,3072]{1,0:T(8,128)(2,1)S(1)}, bf16[128,3072]{1,0:T(8,128)(2,1)}, u32[]{:S(2)}) copy-start(bf16[128,3072]{1,0:T(8,128)(2,1)} %copy-done.30) | copy-start | bytes 2359300
  117.0 12.4 %copy-start.33 = (bf16[128,3072]{1,0:T(8,128)(2,1)S(1)}, bf16[128,3072]{1,0:T(8,128)(2,1)}, u32[]{:S(2)}) copy-start(bf16[128,3072]{1,0:T(8,128)(2,1)} %copy-done.32) | copy-start | bytes 2359300
  117.0 12.4 %copy-start.35 = (bf16[128,3072]{1,0:T(8,128)(2,1)S(1)}, bf16[128,3072]{1,0:T(8,128)(2,1)}, u32[]{:S(2)}) copy-start(bf16[128,3072]{1,0:T(8,128)(2,1)} %copy-done.34) | copy-start | bytes 2359300
  117.5 23.2 %collective-permute-start.34 = (bf16[128,3072]{1,0:T(8,128)(2,1)S(1)}, bf16[128,3072]{1,0:T(8,128)(2,1)S(1)}, u32[]{:S(2)}, u32[]{:S(2)}) collective-permute-start(bf16[128,3072]{1,0:T(8,128)(2,1)S(1)} %add_convert_fusion), channel_id=1, source_target_pairs={{0,64},{1,65},{2,66},{3,67},{4,68},{5,69},{6,70},{7,71},{8,72},{9,... | collective-permute-start | bytes 2359304 | tf_op jit(solution)/shard_map/ppermute | solution.py:47
  124.4 4.9 %copy-start.27 = (bf16[128,3072]{1,0:T(8,128)(2,1)S(1)}, bf16[128,3072]{1,0:T(8,128)(2,1)}, u32[]{:S(2)}) copy-start(bf16[128,3072]{1,0:T(8,128)(2,1)} %copy-done.26) | copy-start | bytes 2359300
  124.4 4.9 %copy-start.29 = (bf16[128,3072]{1,0:T(8,128)(2,1)S(1)}, bf16[128,3072]{1,0:T(8,128)(2,1)}, u32[]{:S(2)}) copy-start(bf16[128,3072]{1,0:T(8,128)(2,1)} %copy-done.28) | copy-start | bytes 2359300
  124.8 4.5 %copy-start.21 = (bf16[128,3072]{1,0:T(8,128)(2,1)S(1)}, bf16[128,3072]{1,0:T(8,128)(2,1)}, u32[]{:S(2)}) copy-start(bf16[128,3072]{1,0:T(8,128)(2,1)} %refs_4_.1) | copy-start | bytes 2359300
  124.8 4.5 %copy-start.23 = (bf16[128,3072]{1,0:T(8,128)(2,1)S(1)}, bf16[128,3072]{1,0:T(8,128)(2,1)}, u32[]{:S(2)}) copy-start(bf16[128,3072]{1,0:T(8,128)(2,1)} %copy-done.22) | copy-start | bytes 2359300
  124.9 4.5 %copy-start.25 = (bf16[128,3072]{1,0:T(8,128)(2,1)S(1)}, bf16[128,3072]{1,0:T(8,128)(2,1)}, u32[]{:S(2)}) copy-start(bf16[128,3072]{1,0:T(8,128)(2,1)} %copy-done.24) | copy-start | bytes 2359300
  124.9 17.5 %collective-permute-start.30 = (bf16[128,3072]{1,0:T(8,128)(2,1)S(1)}, bf16[128,3072]{1,0:T(8,128)(2,1)S(1)}, u32[]{:S(2)}, u32[]{:S(2)}) collective-permute-start(bf16[128,3072]{1,0:T(8,128)(2,1)S(1)} %convolution_convert_fusion), channel_id=1, source_target_pairs={{0,48},{1,17},{2,50},{3,19},{4,52},{5,21},{6,54},{7,23},{8,56},{9,... | collective-permute-start | bytes 2359304 | tf_op jit(solution)/shard_map/ppermute | solution.py:47
  125.3 24.3 %collective-permute-start.37 = (bf16[128,3072]{1,0:T(8,128)(2,1)S(1)}, bf16[128,3072]{1,0:T(8,128)(2,1)S(1)}, u32[]{:S(2)}, u32[]{:S(2)}) collective-permute-start(bf16[128,3072]{1,0:T(8,128)(2,1)S(1)} %fusion), channel_id=1, source_target_pairs={{0,16},{1,49},{2,18},{3,51},{4,20},{5,53},{6,22},{7,55},{8,24},{9,... | collective-permute-start | bytes 2359304 | tf_op jit(solution)/shard_map/ppermute | solution.py:47
  137.0 18.6 %collective-permute-start.33 = (bf16[128,3072]{1,0:T(8,128)(2,1)S(1)}, bf16[128,3072]{1,0:T(8,128)(2,1)S(1)}, u32[]{:S(2)}, u32[]{:S(2)}) collective-permute-start(bf16[128,3072]{1,0:T(8,128)(2,1)S(1)} %get-tuple-element.62), channel_id=1, source_target_pairs={{0,2},{1,7},{2,4},{3,1},{4,6},{5,3},{6,0},{7,5},{8,10},{9,15},{10,... | collective-permute-start | bytes 2359304 | tf_op jit(solution)/shard_map/ppermute | solution.py:47
  140.0 16.7 %collective-permute-start.36 = (bf16[128,3072]{1,0:T(8,128)(2,1)S(1)}, bf16[128,3072]{1,0:T(8,128)(2,1)S(1)}, u32[]{:S(2)}, u32[]{:S(2)}) collective-permute-start(bf16[128,3072]{1,0:T(8,128)(2,1)S(1)} %get-tuple-element.65), channel_id=1, source_target_pairs={{0,8},{1,9},{2,10},{3,11},{4,12},{5,13},{6,14},{7,15},{8,0},{9,1},... | collective-permute-start | bytes 2359304 | tf_op jit(solution)/shard_map/ppermute | solution.py:47
  140.6 17.7 %collective-permute-start.35 = (bf16[128,3072]{1,0:T(8,128)(2,1)S(1)}, bf16[128,3072]{1,0:T(8,128)(2,1)S(1)}, u32[]{:S(2)}, u32[]{:S(2)}) collective-permute-start(bf16[128,3072]{1,0:T(8,128)(2,1)S(1)} %get-tuple-element.64), channel_id=1, source_target_pairs={{0,6},{1,3},{2,0},{3,5},{4,2},{5,7},{6,4},{7,1},{8,14},{9,11},{10,... | collective-permute-start | bytes 2359304 | tf_op jit(solution)/shard_map/ppermute | solution.py:47
  (12 other events, 16.8 us)

commit v4 on v3

--- a/solution.py
+++ b/solution.py
@@ -11,7 +11,7 @@
 SCALE = 3.0
 OUT_SCALE = 0.25
 LOW = -1e30
-CHUNK = 512
+CHUNK = 1024
 WIDE = 1536
 AXES = ("blk", "dp")
 F32 = jnp.float32

time: 160 us -> 160 us (level)
  waiting for transfers between devices: 44.9 us -> 47.2 us
  Pallas kernels: 30.7 us -> 28.5 us
    ppermute x38, waiting for transfers between devices: 44.9 us -> 47.2 us  [send(): return lax.ppermute(value, AXES, route)]
    pallas_call x8, Pallas kernels: 30.7 us -> 28.5 us  [kernel(): pl.pallas_call(body, grid_spec=pltpu.PrefetchScalarGridSpec(num_scalar_pr...]
  transfers between devices with their start and end apart: 38 -> 38, of which waited for: 20 -> 20; matrix products, arithmetic and copies ran while one was open for 7% -> 7% of each run, Pallas kernels for 19% -> 18%
where the time goes in v4:
time: 160 us
  starting transfers between devices  61.8 us (39%)
  waiting for transfers between devices  47.2 us (30%)
  Pallas kernels  28.5 us (18%)
  local copies, waits for them, and re-layouts  8.24 us (5%)
  matrix products  7.55 us (5%)
  other arithmetic  5.31 us (3%)
    ppermute x38, starting transfers between devices, send(): return lax.ppermute(value, AXES, route)  61.8 us
    ppermute x38, waiting for transfers between devices, send(): return lax.ppermute(value, AXES, route)  47.2 us
    pallas_call x8, Pallas kernels, kernel(): pl.pallas_call(body, grid_spec=pltpu.PrefetchScalarGridSpec(num_scalar_pr...  28.5 us
    unnamed x76, local copies, waits for them, and re-layouts  7.61 us
    dot_general x8, matrix products, rows_dot(): lax.dot_general(left, right, (((1,), (1,)), ((), ())), preferred_element_...  4.34 us
    dot_general x8, matrix products, mm(): return jnp.dot(left, right, preferred_element_type=F32)  3.2 us
  transfers between devices with their start and end apart: 38, of which 20 were waited for; matrix products, arithmetic and copies ran while one was open for 7% of the time, Pallas kernels for 18%

profile of v4, /device:TPU:1, one launch (start us, length us, event | category | flops | bytes accessed | tf_op | source)
XLA Modules:
  0.0 159.9 jit_solution(14146609202815945812)
XLA Ops:
  0.6 1.5 collective-permute-start.4
  2.1 0.7 and_select_fusion.1
  2.9 1.4 collective-permute-start
  4.5 0.9 collective-permute-done
  5.4 3.1 %collective-permute-start.2 = (s32[2,16]{1,0:T(2,128)S(1)}, s32[2,16]{1,0:T(2,128)S(1)}, u32[]{:S(2)}, u32[]{:S(2)}) collective-permute-start(s32[2,16]{1,0:T(2,128)S(1)} %get-tuple-element.91), channel_id=1, source_target_pairs={{0,4},{1,5},{2,6},{3,7},{4,0},{5,1},{6,2},{7,3},{8,12},{9,13},{10,... | collective-permute-start | bytes 392 | tf_op jit(solution)/shard_map/ppermute | solution.py:47
  8.8 2.3 %collective-permute-start.3 = (s32[2,16]{1,0:T(2,128)S(1)}, s32[2,16]{1,0:T(2,128)S(1)}, u32[]{:S(2)}, u32[]{:S(2)}) collective-permute-start(s32[2,16]{1,0:T(2,128)S(1)} %get-tuple-element.91), channel_id=1, source_target_pairs={{0,2},{1,7},{2,4},{3,1},{4,6},{5,3},{6,0},{7,5},{8,10},{9,15},{10,... | collective-permute-start | bytes 392 | tf_op jit(solution)/shard_map/ppermute | solution.py:47
  11.1 0.9 collective-permute-done.1
  12.8 3.8 %collective-permute-start.11 = (bf16[128,3072]{1,0:T(8,128)(2,1)}, bf16[128,3072]{1,0:T(8,128)(2,1)S(1)}, u32[]{:S(2)}, u32[]{:S(2)}) collective-permute-start(bf16[128,3072]{1,0:T(8,128)(2,1)} %refs_4_.1), channel_id=1, source_target_pairs={{0,16},{1,49},{2,18},{3,51},{4,20},{5,53},{6,22},{7,55},{8,24},{9,... | collective-permute-start | bytes 2359304 | tf_op jit(solution)/shard_map/ppermute | solution.py:47
  16.7 3.0 %collective-permute-start.6 = (bf16[128,3072]{1,0:T(8,128)(2,1)}, bf16[128,3072]{1,0:T(8,128)(2,1)S(1)}, u32[]{:S(2)}, u32[]{:S(2)}) collective-permute-start(bf16[128,3072]{1,0:T(8,128)(2,1)} %refs_2_.3), channel_id=1, source_target_pairs={{0,2},{1,7},{2,4},{3,1},{4,6},{5,3},{6,0},{7,5},{8,10},{9,15},{10,... | collective-permute-start | bytes 2359304 | tf_op jit(solution)/shard_map/ppermute | solution.py:47
  19.6 3.8 %collective-permute-done.5.refs_3_.refs_6_ = bf16[128,3072]{1,0:T(8,128)(2,1)} collective-permute-done((bf16[128,3072]{1,0:T(8,128)(2,1)}, bf16[128,3072]{1,0:T(8,128)(2,1)}, u32[]{:S(2)}, u32[]{:S(2)}) %collective-permute-start.5) | collective-permute-done | bytes 786464 | tf_op jit(solution)/shard_map/ppermute | solution.py:47
  23.4 2.5 %collective-permute-done.11.refs_7_ = bf16[128,3072]{1,0:T(8,128)(2,1)S(1)} collective-permute-done((bf16[128,3072]{1,0:T(8,128)(2,1)}, bf16[128,3072]{1,0:T(8,128)(2,1)S(1)}, u32[]{:S(2)}, u32[]{:S(2)}) %collective-permute-start.11) | collective-permute-done | bytes 786464 | tf_op jit(solution)/shard_map/ppermute | solution.py:47
  25.9 3.0 %collective-permute-start.8 = (bf16[128,3072]{1,0:T(8,128)(2,1)}, bf16[128,3072]{1,0:T(8,128)(2,1)S(1)}, u32[]{:S(2)}, u32[]{:S(2)}) collective-permute-start(bf16[128,3072]{1,0:T(8,128)(2,1)} %collective-permute-done.5.refs_3_.refs_6_), channel_id=1, source_target_pairs={{0,2},{1,7},{2,4},{3,1},{4,6},{5,3},{6,0},{7,5},{8,10},{9,15},{10,... | collective-permute-start | bytes 2359304 | tf_op jit(solution)/shard_map/ppermute | solution.py:47
  28.9 3.3 %collective-permute-start.12 = (bf16[128,3072]{1,0:T(8,128)(2,1)S(1)}, bf16[128,3072]{1,0:T(8,128)(2,1)S(1)}, u32[]{:S(2)}, u32[]{:S(2)}) collective-permute-start(bf16[128,3072]{1,0:T(8,128)(2,1)S(1)} %collective-permute-done.11.refs_7_), channel_id=1, source_target_pairs={{0,16},{1,49},{2,18},{3,51},{4,20},{5,53},{6,22},{7,55},{8,24},{9,... | collective-permute-start | bytes 2359304 | tf_op jit(solution)/shard_map/ppermute | solution.py:47
  32.2 2.7 %collective-permute-start.13 = (bf16[128,3072]{1,0:T(8,128)(2,1)}, bf16[128,3072]{1,0:T(8,128)(2,1)S(1)}, u32[]{:S(2)}, u32[]{:S(2)}) collective-permute-start(bf16[128,3072]{1,0:T(8,128)(2,1)} %refs_4_.1), channel_id=1, source_target_pairs={{0,64},{1,65},{2,66},{3,67},{4,68},{5,69},{6,70},{7,71},{8,72},{9,... | collective-permute-start | bytes 2359304 | tf_op jit(solution)/shard_map/ppermute | solution.py:47
  34.9 1.0 collective-permute-done.7.refs_9_.refs_3_
  36.3 1.8 %collective-permute-start.9 = (bf16[128,3072]{1,0:T(8,128)(2,1)}, bf16[128,3072]{1,0:T(8,128)(2,1)S(1)}, u32[]{:S(2)}, u32[]{:S(2)}) collective-permute-start(bf16[128,3072]{1,0:T(8,128)(2,1)} %collective-permute-done.5.refs_3_.refs_6_), channel_id=1, source_target_pairs={{0,6},{1,3},{2,0},{3,5},{4,2},{5,7},{6,4},{7,1},{8,14},{9,11},{10,... | collective-permute-start | bytes 2359304 | tf_op jit(solution)/shard_map/ppermute | solution.py:47
  38.2 1.7 %convolution_dynamic-update-slice_fusion.7 = f32[1024,128]{0,1:T(8,128)S(1)} fusion(bf16[128,3072]{1,0:T(8,128)(2,1)} %refs_4_.1, bf16[128,3072]{1,0:T(8,128)(2,1)} %refs_2_.3), kind=kOutput, calls=%fused_computation.17 | convolution fusion | flops 100663296 | bytes 1638400 | tf_op jit(solution)/shard_map/dot_general | solution.py:59
  39.9 6.0 %collective-permute-done.8.refs_12_.refs_9_ = bf16[128,3072]{1,0:T(8,128)(2,1)S(1)} collective-permute-done((bf16[128,3072]{1,0:T(8,128)(2,1)}, bf16[128,3072]{1,0:T(8,128)(2,1)S(1)}, u32[]{:S(2)}, u32[]{:S(2)}) %collective-permute-start.8) | collective-permute-done | bytes 786464 | tf_op jit(solution)/shard_map/ppermute | solution.py:47
  45.9 3.3 %collective-permute-start.17 = (bf16[128,3072]{1,0:T(8,128)(2,1)S(1)}, bf16[128,3072]{1,0:T(8,128)(2,1)S(1)}, u32[]{:S(2)}, u32[]{:S(2)}) collective-permute-start(bf16[128,3072]{1,0:T(8,128)(2,1)S(1)} %collective-permute-done.6.refs_6_.refs_5_), channel_id=1, source_target_pairs={{0,2},{1,7},{2,4},{3,1},{4,6},{5,3},{6,0},{7,5},{8,10},{9,15},{10,... | collective-permute-start | bytes 2359304 | tf_op jit(solution)/shard_map/ppermute | solution.py:47
  49.2 3.1 %collective-permute-done.13.refs_8_ = bf16[128,3072]{1,0:T(8,128)(2,1)S(1)} collective-permute-done((bf16[128,3072]{1,0:T(8,128)(2,1)}, bf16[128,3072]{1,0:T(8,128)(2,1)S(1)}, u32[]{:S(2)}, u32[]{:S(2)}) %collective-permute-start.13) | collective-permute-done | bytes 786464 | tf_op jit(solution)/shard_map/ppermute | solution.py:47
  52.3 2.7 %collective-permute-start.15 = (bf16[128,3072]{1,0:T(8,128)(2,1)S(1)}, bf16[128,3072]{1,0:T(8,128)(2,1)S(1)}, u32[]{:S(2)}, u32[]{:S(2)}) collective-permute-start(bf16[128,3072]{1,0:T(8,128)(2,1)S(1)} %collective-permute-done.12.refs_6_), channel_id=1, source_target_pairs={{0,64},{1,65},{2,66},{3,67},{4,68},{5,69},{6,70},{7,71},{8,72},{9,... | collective-permute-start | bytes 2359304 | tf_op jit(solution)/shard_map/ppermute | solution.py:47
  55.0 2.7 %collective-permute-start.16 = (bf16[128,3072]{1,0:T(8,128)(2,1)S(1)}, bf16[128,3072]{1,0:T(8,128)(2,1)S(1)}, u32[]{:S(2)}, u32[]{:S(2)}) collective-permute-start(bf16[128,3072]{1,0:T(8,128)(2,1)S(1)} %collective-permute-done.13.refs_8_), channel_id=1, source_target_pairs={{0,16},{1,49},{2,18},{3,51},{4,20},{5,53},{6,22},{7,55},{8,24},{9,... | collective-permute-start | bytes 2359304 | tf_op jit(solution)/shard_map/ppermute | solution.py:47
  58.1 0.9 copy-done.28
  59.4 0.9 copy-done.24
  61.1 0.9 copy-done.26
  62.0 0.5 copy-done
  62.5 1.9 %copy-done.2 = bf16[512,3072]{1,0:T(8,128)(2,1)S(1)} copy-done((bf16[512,3072]{1,0:T(8,128)(2,1)S(1)}, bf16[512,3072]{1,0:T(8,128)(2,1)}, u32[]{:S(2)}) %copy-start.2) | copy-done | bytes 3145752
  64.4 5.0 %shard_map.75 = (f32[6,2,128,128]{3,2,1,0:T(8,128)S(1)}, f32[6,2,128]{2,1,0:T(2,128)S(1)}) custom-call(s32[16]{0:T(128)S(1)} %min.12.asked_ref, bf16[128,3072]{1,0:T(8,128)(2,1)S(1)} %copy-done.5, bf16[4,128,3072]{2,1,0:T(8,128)(2,1)S(1)} %bitcast.161, bf16[4,128,3072]{2,1,0:T(8,128)(2,1)S(1)} %bitcast.177, ...), custom_call_target="tpu_custom_call" | custom-call | flops 1024 | bytes 1024 | tf_op jit(solution)/shard_map/pallas_call | solution.py:80
  69.5 3.7 %collective-permute-done.18.refs_3_.refs_8_ = bf16[128,3072]{1,0:T(8,128)(2,1)S(1)} collective-permute-done((bf16[128,3072]{1,0:T(8,128)(2,1)S(1)}, bf16[128,3072]{1,0:T(8,128)(2,1)S(1)}, u32[]{:S(2)}, u32[]{:S(2)}) %collective-permute-start.18) | collective-permute-done | bytes 786464 | tf_op jit(solution)/shard_map/ppermute | solution.py:47
  73.2 2.3 %shard_map.76 = (f32[2,2,128,128]{3,2,1,0:T(8,128)S(1)}, f32[2,2,128]{2,1,0:T(2,128)S(1)}) custom-call(s32[16]{0:T(128)S(1)} %min.12.asked_ref, bf16[128,3072]{1,0:T(8,128)(2,1)S(1)} %collective-permute-done.17.refs_0_.refs_4_, bf16[4,128,3072]{2,1,0:T(8,128)(2,1)S(1)} %bitcast.167, bf16[4,128,3072]{2,1,0:T(8,128)(2,1)S(1)} %bitcast.183, ...), custom_call_target="tpu_custom_call" | custom-call | flops 1024 | bytes 1024 | tf_op jit(solution)/shard_map/pallas_call | solution.py:80
  77.7 0.7 collective-permute-start.19
  78.4 1.9 %copy-done.3 = bf16[512,3072]{1,0:T(8,128)(2,1)S(1)} copy-done((bf16[512,3072]{1,0:T(8,128)(2,1)S(1)}, bf16[512,3072]{1,0:T(8,128)(2,1)}, u32[]{:S(2)}) %copy-start.3) | copy-done | bytes 3145752
  80.3 1.9 %shard_map.77 = (bf16[128,3072]{1,0:T(8,128)(2,1)S(1)}, bf16[128,3072]{1,0:T(8,128)(2,1)S(1)}) custom-call(s32[16]{0:T(128)S(1)} %min.12.asked_ref, f32[8,128]{1,0:T(8,128)S(1)} %slice_bitcast_fusion.norm_ref, f32[2,2,128,128]{3,2,1,0:T(8,128)S(1)} %get-tuple-element.48.refs_0_.refs_3_.refs_1_, bf16[4,128,3072]{2,1,0:T(8,128)(2,1)S(1)} %bitcast.169, ...), custom_call_target="tpu_custom_call" | custom-call | flops 1024 | bytes 1024 | tf_op jit(solution)/shard_map/pallas_call | solution.py:80
  82.4 0.8 collective-permute-start.20
  83.2 1.9 %collective-permute-start.21 = (f32[9,2,128]{2,0,1:T(8,128)S(1)}, f32[9,2,128]{2,0,1:T(8,128)S(1)}, u32[]{:S(2)}, u32[]{:S(2)}) collective-permute-start(f32[9,2,128]{2,0,1:T(8,128)S(1)} %get-tuple-element.83), channel_id=1, source_target_pairs={{0,2},{1,7},{2,4},{3,1},{4,6},{5,3},{6,0},{7,5},{8,10},{9,15},{10,... | collective-permute-start | bytes 27656 | tf_op jit(solution)/shard_map/ppermute | solution.py:47
  85.1 1.2 collective-permute-done.22
  86.4 2.7 %collective-permute-start.24 = (bf16[128,3072]{1,0:T(8,128)(2,1)S(1)}, bf16[128,3072]{1,0:T(8,128)(2,1)S(1)}, u32[]{:S(2)}, u32[]{:S(2)}) collective-permute-start(bf16[128,3072]{1,0:T(8,128)(2,1)S(1)} %get-tuple-element.50), channel_id=1, source_target_pairs={{0,2},{1,7},{2,4},{3,1},{4,6},{5,3},{6,0},{7,5},{8,10},{9,15},{10,... | collective-permute-start | bytes 2359304 | tf_op jit(solution)/shard_map/ppermute | solution.py:47
  90.7 3.2 %collective-permute-start.26 = (bf16[128,3072]{1,0:T(8,128)(2,1)S(1)}, bf16[128,3072]{1,0:T(8,128)(2,1)S(1)}, u32[]{:S(2)}, u32[]{:S(2)}) collective-permute-start(bf16[128,3072]{1,0:T(8,128)(2,1)S(1)} %convolution_convert_fusion.2), channel_id=1, source_target_pairs={{0,64},{1,65},{2,66},{3,67},{4,68},{5,69},{6,70},{7,71},{8,72},{9,... | collective-permute-start | bytes 2359304 | tf_op jit(solution)/shard_map/ppermute | solution.py:47
  93.9 2.6 %collective-permute-start.28 = (bf16[128,3072]{1,0:T(8,128)(2,1)S(1)}, bf16[128,3072]{1,0:T(8,128)(2,1)S(1)}, u32[]{:S(2)}, u32[]{:S(2)}) collective-permute-start(bf16[128,3072]{1,0:T(8,128)(2,1)S(1)} %convolution_convert_fusion.1), channel_id=1, source_target_pairs={{0,16},{1,49},{2,18},{3,51},{4,20},{5,53},{6,22},{7,55},{8,24},{9,... | collective-permute-start | bytes 2359304 | tf_op jit(solution)/shard_map/ppermute | solution.py:47
  96.6 5.0 %shard_map.80 = bf16[4,128,3072]{2,1,0:T(8,128)(2,1)S(1)} custom-call(s32[16]{0:T(128)S(1)} %min.12.asked_ref, f32[8,128]{1,0:T(8,128)S(1)} %fusion.22.norm_ref, f32[6,2,128,128]{3,2,1,0:T(8,128)S(1)} %copy-done.8, f32[2,2,128,128]{3,2,1,0:T(8,128)S(1)} %get-tuple-element.48.refs_0_.refs_3_.refs_1_, bf16[128,3072]{1,0:T(8,128)(2,1)S(1)} %copy-done.6, ...), custom_call_target="tpu_custom_call" | custom-call | flops 1024 | bytes 1024 | tf_op jit(solution)/shard_map/pallas_call | solution.py:80
  101.6 2.1 %collective-permute-done.25.refs_6_ = bf16[128,3072]{1,0:T(8,128)(2,1)S(1)} collective-permute-done((bf16[128,3072]{1,0:T(8,128)(2,1)S(1)}, bf16[128,3072]{1,0:T(8,128)(2,1)S(1)}, u32[]{:S(2)}, u32[]{:S(2)}) %collective-permute-start.25) | collective-permute-done | bytes 786464 | tf_op jit(solution)/shard_map/ppermute | solution.py:47
  103.8 2.4 %collective-permute-done.24.refs_11_ = bf16[128,3072]{1,0:T(8,128)(2,1)S(1)} collective-permute-done((bf16[128,3072]{1,0:T(8,128)(2,1)S(1)}, bf16[128,3072]{1,0:T(8,128)(2,1)S(1)}, u32[]{:S(2)}, u32[]{:S(2)}) %collective-permute-start.24) | collective-permute-done | bytes 786464 | tf_op jit(solution)/shard_map/ppermute | solution.py:47
  106.2 2.0 %shard_map.78 = (bf16[128,3072]{1,0:T(8,128)(2,1)S(1)}, bf16[128,3072]{1,0:T(8,128)(2,1)S(1)}) custom-call(s32[16]{0:T(128)S(1)} %min.12.asked_ref, f32[8,128]{1,0:T(8,128)S(1)} %fusion.22.norm_ref, f32[6,2,128,128]{3,2,1,0:T(8,128)S(1)} %copy-done.8, bf16[4,128,3072]{2,1,0:T(8,128)(2,1)S(1)} %bitcast.171, bf16[4,128,3072]{2,1,0:T(8,128)(2,1)S(1)} %bitcast.187, ...), custom_call_target="tpu_custom_call" | custom-call | flops 1024 | bytes 1024 | tf_op jit(solution)/shard_map/pallas_call | solution.py:80
  108.6 3.3 %collective-permute-done.28 = bf16[128,3072]{1,0:T(8,128)(2,1)S(1)} collective-permute-done((bf16[128,3072]{1,0:T(8,128)(2,1)S(1)}, bf16[128,3072]{1,0:T(8,128)(2,1)S(1)}, u32[]{:S(2)}, u32[]{:S(2)}) %collective-permute-start.28) | collective-permute-done | bytes 786464 | tf_op jit(solution)/shard_map/ppermute | solution.py:47
  111.9 0.5 collective-permute-start.29
  112.8 2.7 %collective-permute-start.27 = (bf16[128,3072]{1,0:T(8,128)(2,1)S(1)}, bf16[128,3072]{1,0:T(8,128)(2,1)S(1)}, u32[]{:S(2)}, u32[]{:S(2)}) collective-permute-start(bf16[128,3072]{1,0:T(8,128)(2,1)S(1)} %add_convert_fusion.1), channel_id=1, source_target_pairs={{0,16},{1,49},{2,18},{3,51},{4,20},{5,53},{6,22},{7,55},{8,24},{9,... | collective-permute-start | bytes 2359304 | tf_op jit(solution)/shard_map/ppermute | solution.py:47
  115.5 1.2 collective-permute-start.31
  117.0 0.5 add_convert_fusion
  117.5 2.8 %collective-permute-start.34 = (bf16[128,3072]{1,0:T(8,128)(2,1)S(1)}, bf16[128,3072]{1,0:T(8,128)(2,1)S(1)}, u32[]{:S(2)}, u32[]{:S(2)}) collective-permute-start(bf16[128,3072]{1,0:T(8,128)(2,1)S(1)} %add_convert_fusion), channel_id=1, source_target_pairs={{0,64},{1,65},{2,66},{3,67},{4,68},{5,69},{6,70},{7,71},{8,72},{9,... | collective-permute-start | bytes 2359304 | tf_op jit(solution)/shard_map/ppermute | solution.py:47
  120.2 4.2 %collective-permute-done.27 = bf16[128,3072]{1,0:T(8,128)(2,1)S(1)} collective-permute-done((bf16[128,3072]{1,0:T(8,128)(2,1)S(1)}, bf16[128,3072]{1,0:T(8,128)(2,1)S(1)}, u32[]{:S(2)}, u32[]{:S(2)}) %collective-permute-start.27) | collective-permute-done | bytes 786464 | tf_op jit(solution)/shard_map/ppermute | solution.py:47
  125.3 3.5 %collective-permute-start.37 = (bf16[128,3072]{1,0:T(8,128)(2,1)S(1)}, bf16[128,3072]{1,0:T(8,128)(2,1)S(1)}, u32[]{:S(2)}, u32[]{:S(2)}) collective-permute-start(bf16[128,3072]{1,0:T(8,128)(2,1)S(1)} %fusion), channel_id=1, source_target_pairs={{0,16},{1,49},{2,18},{3,51},{4,20},{5,53},{6,22},{7,55},{8,24},{9,... | collective-permute-start | bytes 2359304 | tf_op jit(solution)/shard_map/ppermute | solution.py:47
  128.8 0.5 fusion.38
  129.4 3.5 %shard_map.79 = f32[128,3072]{1,0:T(8,128)S(1)} custom-call(s32[16]{0:T(128)S(1)} %min.12.asked_ref, f32[8,128]{1,0:T(8,128)S(1)} %fusion.22.norm_ref, f32[6,2,128,128]{3,2,1,0:T(8,128)S(1)} %copy-done.8, bf16[4,128,3072]{2,1,0:T(8,128)(2,1)S(1)} %bitcast.173, bf16[4,128,3072]{2,1,0:T(8,128)(2,1)S(1)} %bitcast.189, bf16[128,1024]{1,0:T(8,128)(2,1)S(1)} %bitcast.193, ...), custom_call_target="tpu_custom_call" | custom-call | flops 1024 | bytes 1024 | tf_op jit(solution)/shard_map/pallas_call | solution.py:80
  132.9 1.5 collective-permute-done.32.refs_10_
  134.4 2.6 %shard_map.82 = (bf16[128,3072]{1,0:T(8,128)(2,1)S(1)}, bf16[128,3072]{1,0:T(8,128)(2,1)S(1)}, bf16[128,3072]{1,0:T(8,128)(2,1)S(1)}) custom-call(s32[16]{0:T(128)S(1)} %min.12.asked_ref, f32[8,128]{1,0:T(8,128)S(1)} %fusion.22.norm_ref, f32[6,2,128,128]{3,2,1,0:T(8,128)S(1)} %copy-done.8, bf16[4,128,3072]{2,1,0:T(8,128)(2,1)S(1)} %bitcast.174, ...), custom_call_target="tpu_custom_call" | custom-call | flops 1024 | bytes 1024 | tf_op jit(solution)/shard_map/pallas_call | solution.py:80
  137.0 3.0 %collective-permute-start.33 = (bf16[128,3072]{1,0:T(8,128)(2,1)S(1)}, bf16[128,3072]{1,0:T(8,128)(2,1)S(1)}, u32[]{:S(2)}, u32[]{:S(2)}) collective-permute-start(bf16[128,3072]{1,0:T(8,128)(2,1)S(1)} %get-tuple-element.62), channel_id=1, source_target_pairs={{0,2},{1,7},{2,4},{3,1},{4,6},{5,3},{6,0},{7,5},{8,10},{9,15},{10,... | collective-permute-start | bytes 2359304 | tf_op jit(solution)/shard_map/ppermute | solution.py:47
  140.0 0.6 collective-permute-start.36
  141.0 1.3 collective-permute-done.30
  142.3 6.1 %shard_map.81 = f32[4,128,3072]{2,1,0:T(8,128)} custom-call(s32[16]{0:T(128)S(1)} %min.12.asked_ref, f32[8,128]{1,0:T(8,128)S(1)} %fusion.22.norm_ref, f32[6,2,128,128]{3,2,1,0:T(8,128)S(1)} %copy-done.8, f32[2,2,128,128]{3,2,1,0:T(8,128)S(1)} %get-tuple-element.48.refs_0_.refs_3_.refs_1_, bf16[128,3072]{1,0:T(8,128)(2,1)S(1)} %copy-done.6, ...), custom_call_target="tpu_custom_call" | custom-call | flops 1024 | bytes 1024 | tf_op jit(solution)/shard_map/pallas_call | solution.py:80
  148.5 1.6 add_multiply_fusion
  150.1 5.5 %collective-permute-done.33 = bf16[128,3072]{1,0:T(8,128)(2,1)S(1)} collective-permute-done((bf16[128,3072]{1,0:T(8,128)(2,1)S(1)}, bf16[128,3072]{1,0:T(8,128)(2,1)S(1)}, u32[]{:S(2)}, u32[]{:S(2)}) %collective-permute-start.33) | collective-permute-done | bytes 786464 | tf_op jit(solution)/shard_map/ppermute | solution.py:47
  155.6 1.2 collective-permute-done.36
  156.8 1.6 collective-permute-done.35
  158.4 1.6 add_multiply_fusion.1
  (161 shorter events, 9.7 us)
Async XLA Ops:
  0.6 22.8 %collective-permute-start.4 = (bf16[512,3072]{1,0:T(8,128)(2,1)}, bf16[512,3072]{1,0:T(8,128)(2,1)S(1)}, u32[]{:S(2)}, u32[]{:S(2)}) collective-permute-start(bf16[512,3072]{1,0:T(8,128)(2,1)} %param.6), channel_id=1, source_target_pairs={{0,1},{1,0},{2,3},{3,2},{4,5},{5,4},{6,7},{7,6},{8,9},{9,8},{10,11... | collective-permute-start | bytes 9437192 | tf_op jit(solution)/shard_map/ppermute | solution.py:47
  2.9 2.5 %collective-permute-start = (s32[1,16]{1,0:T(1,128)S(1)}, s32[1,16]{1,0:T(1,128)S(1)}, u32[]{:S(2)}, u32[]{:S(2)}) collective-permute-start(s32[1,16]{1,0:T(1,128)S(1)} %add_bitcast_fusion), channel_id=1, source_target_pairs={{0,8},{1,9},{2,10},{3,11},{4,12},{5,13},{6,14},{7,15},{8,0},{9,1},... | collective-permute-start | bytes 200 | tf_op jit(solution)/shard_map/ppermute | solution.py:47
  4.3 19.2 %collective-permute-start.5 = (bf16[128,3072]{1,0:T(8,128)(2,1)}, bf16[128,3072]{1,0:T(8,128)(2,1)}, u32[]{:S(2)}, u32[]{:S(2)}) collective-permute-start(bf16[128,3072]{1,0:T(8,128)(2,1)} %refs_2_.3), channel_id=1, source_target_pairs={{0,8},{1,9},{2,10},{3,11},{4,12},{5,13},{6,14},{7,15},{8,0},{9,1},... | collective-permute-start | bytes 2359304 | tf_op jit(solution)/shard_map/ppermute | solution.py:47
  5.4 5.8 %collective-permute-start.2 = (s32[2,16]{1,0:T(2,128)S(1)}, s32[2,16]{1,0:T(2,128)S(1)}, u32[]{:S(2)}, u32[]{:S(2)}) collective-permute-start(s32[2,16]{1,0:T(2,128)S(1)} %get-tuple-element.91), channel_id=1, source_target_pairs={{0,4},{1,5},{2,6},{3,7},{4,0},{5,1},{6,2},{7,3},{8,12},{9,13},{10,... | collective-permute-start | bytes 392 | tf_op jit(solution)/shard_map/ppermute | solution.py:47
  8.4 3.6 %collective-permute-start.1 = (s32[2,16]{1,0:T(2,128)S(1)}, s32[2,16]{1,0:T(2,128)S(1)}, u32[]{:S(2)}, u32[]{:S(2)}) collective-permute-start(s32[2,16]{1,0:T(2,128)S(1)} %get-tuple-element.91), channel_id=1, source_target_pairs={{0,6},{1,3},{2,0},{3,5},{4,2},{5,7},{6,4},{7,1},{8,14},{9,11},{10,... | collective-permute-start | bytes 392 | tf_op jit(solution)/shard_map/ppermute | solution.py:47
  8.8 3.2 %collective-permute-start.3 = (s32[2,16]{1,0:T(2,128)S(1)}, s32[2,16]{1,0:T(2,128)S(1)}, u32[]{:S(2)}, u32[]{:S(2)}) collective-permute-start(s32[2,16]{1,0:T(2,128)S(1)} %get-tuple-element.91), channel_id=1, source_target_pairs={{0,2},{1,7},{2,4},{3,1},{4,6},{5,3},{6,0},{7,5},{8,10},{9,15},{10,... | collective-permute-start | bytes 392 | tf_op jit(solution)/shard_map/ppermute | solution.py:47
  12.8 44.9 %copy-start.5 = (bf16[128,3072]{1,0:T(8,128)(2,1)S(1)}, bf16[128,3072]{1,0:T(8,128)(2,1)}, u32[]{:S(2)}) copy-start(bf16[128,3072]{1,0:T(8,128)(2,1)} %refs_2_.3) | copy-start | bytes 2359300
  12.8 13.1 %collective-permute-start.11 = (bf16[128,3072]{1,0:T(8,128)(2,1)}, bf16[128,3072]{1,0:T(8,128)(2,1)S(1)}, u32[]{:S(2)}, u32[]{:S(2)}) collective-permute-start(bf16[128,3072]{1,0:T(8,128)(2,1)} %refs_4_.1), channel_id=1, source_target_pairs={{0,16},{1,49},{2,18},{3,51},{4,20},{5,53},{6,22},{7,55},{8,24},{9,... | collective-permute-start | bytes 2359304 | tf_op jit(solution)/shard_map/ppermute | solution.py:47
  16.7 19.2 %collective-permute-start.7 = (bf16[128,3072]{1,0:T(8,128)(2,1)}, bf16[128,3072]{1,0:T(8,128)(2,1)S(1)}, u32[]{:S(2)}, u32[]{:S(2)}) collective-permute-start(bf16[128,3072]{1,0:T(8,128)(2,1)} %refs_2_.3), channel_id=1, source_target_pairs={{0,6},{1,3},{2,0},{3,5},{4,2},{5,7},{6,4},{7,1},{8,14},{9,11},{10,... | collective-permute-start | bytes 2359304 | tf_op jit(solution)/shard_map/ppermute | solution.py:47
  16.7 19.7 %collective-permute-start.6 = (bf16[128,3072]{1,0:T(8,128)(2,1)}, bf16[128,3072]{1,0:T(8,128)(2,1)S(1)}, u32[]{:S(2)}, u32[]{:S(2)}) collective-permute-start(bf16[128,3072]{1,0:T(8,128)(2,1)} %refs_2_.3), channel_id=1, source_target_pairs={{0,2},{1,7},{2,4},{3,1},{4,6},{5,3},{6,0},{7,5},{8,10},{9,15},{10,... | collective-permute-start | bytes 2359304 | tf_op jit(solution)/shard_map/ppermute | solution.py:47
  23.4 34.7 %copy-start.1 = (bf16[512,3072]{1,0:T(8,128)(2,1)}, bf16[512,3072]{1,0:T(8,128)(2,1)S(1)}, u32[]{:S(2)}) copy-start(bf16[512,3072]{1,0:T(8,128)(2,1)S(1)} %collective-permute-done.4) | copy-start | bytes 9437188
  25.9 33.5 %copy-start.22 = (bf16[128,3072]{1,0:T(8,128)(2,1)}, bf16[128,3072]{1,0:T(8,128)(2,1)S(1)}, u32[]{:S(2)}) copy-start(bf16[128,3072]{1,0:T(8,128)(2,1)S(1)} %collective-permute-done.11.refs_7_) | copy-start | bytes 2359300
  25.9 20.0 %collective-permute-start.8 = (bf16[128,3072]{1,0:T(8,128)(2,1)}, bf16[128,3072]{1,0:T(8,128)(2,1)S(1)}, u32[]{:S(2)}, u32[]{:S(2)}) collective-permute-start(bf16[128,3072]{1,0:T(8,128)(2,1)} %collective-permute-done.5.refs_3_.refs_6_), channel_id=1, source_target_pairs={{0,2},{1,7},{2,4},{3,1},{4,6},{5,3},{6,0},{7,5},{8,10},{9,15},{10,... | collective-permute-start | bytes 2359304 | tf_op jit(solution)/shard_map/ppermute | solution.py:47
  28.9 20.3 %collective-permute-start.12 = (bf16[128,3072]{1,0:T(8,128)(2,1)S(1)}, bf16[128,3072]{1,0:T(8,128)(2,1)S(1)}, u32[]{:S(2)}, u32[]{:S(2)}) collective-permute-start(bf16[128,3072]{1,0:T(8,128)(2,1)S(1)} %collective-permute-done.11.refs_7_), channel_id=1, source_target_pairs={{0,16},{1,49},{2,18},{3,51},{4,20},{5,53},{6,22},{7,55},{8,24},{9,... | collective-permute-start | bytes 2359304 | tf_op jit(solution)/shard_map/ppermute | solution.py:47
  32.2 20.1 %collective-permute-start.13 = (bf16[128,3072]{1,0:T(8,128)(2,1)}, bf16[128,3072]{1,0:T(8,128)(2,1)S(1)}, u32[]{:S(2)}, u32[]{:S(2)}) collective-permute-start(bf16[128,3072]{1,0:T(8,128)(2,1)} %refs_4_.1), channel_id=1, source_target_pairs={{0,64},{1,65},{2,66},{3,67},{4,68},{5,69},{6,70},{7,71},{8,72},{9,... | collective-permute-start | bytes 2359304 | tf_op jit(solution)/shard_map/ppermute | solution.py:47
  35.9 26.1 %copy-start.13 = (bf16[128,3072]{1,0:T(8,128)(2,1)}, bf16[128,3072]{1,0:T(8,128)(2,1)S(1)}, u32[]{:S(2)}) copy-start(bf16[128,3072]{1,0:T(8,128)(2,1)S(1)} %collective-permute-done.7.refs_9_.refs_3_) | copy-start | bytes 2359300
  36.3 25.6 %copy-start.15 = (bf16[128,3072]{1,0:T(8,128)(2,1)}, bf16[128,3072]{1,0:T(8,128)(2,1)S(1)}, u32[]{:S(2)}) copy-start(bf16[128,3072]{1,0:T(8,128)(2,1)S(1)} %collective-permute-done.6.refs_6_.refs_5_) | copy-start | bytes 2359300
  36.3 16.0 %collective-permute-start.10 = (bf16[128,3072]{1,0:T(8,128)(2,1)}, bf16[128,3072]{1,0:T(8,128)(2,1)S(1)}, u32[]{:S(2)}, u32[]{:S(2)}) collective-permute-start(bf16[128,3072]{1,0:T(8,128)(2,1)} %refs_4_.1), channel_id=1, source_target_pairs={{0,48},{1,17},{2,50},{3,19},{4,52},{5,21},{6,54},{7,23},{8,56},{9,... | collective-permute-start | bytes 2359304 | tf_op jit(solution)/shard_map/ppermute | solution.py:47
  36.3 21.4 %collective-permute-start.9 = (bf16[128,3072]{1,0:T(8,128)(2,1)}, bf16[128,3072]{1,0:T(8,128)(2,1)S(1)}, u32[]{:S(2)}, u32[]{:S(2)}) collective-permute-start(bf16[128,3072]{1,0:T(8,128)(2,1)} %collective-permute-done.5.refs_3_.refs_6_), channel_id=1, source_target_pairs={{0,6},{1,3},{2,0},{3,5},{4,2},{5,7},{6,4},{7,1},{8,14},{9,11},{10,... | collective-permute-start | bytes 2359304 | tf_op jit(solution)/shard_map/ppermute | solution.py:47
  45.9 16.1 %copy-start.17 = (bf16[128,3072]{1,0:T(8,128)(2,1)}, bf16[128,3072]{1,0:T(8,128)(2,1)S(1)}, u32[]{:S(2)}) copy-start(bf16[128,3072]{1,0:T(8,128)(2,1)S(1)} %collective-permute-done.8.refs_12_.refs_9_) | copy-start | bytes 2359300
  45.9 27.3 %collective-permute-start.17 = (bf16[128,3072]{1,0:T(8,128)(2,1)S(1)}, bf16[128,3072]{1,0:T(8,128)(2,1)S(1)}, u32[]{:S(2)}, u32[]{:S(2)}) collective-permute-start(bf16[128,3072]{1,0:T(8,128)(2,1)S(1)} %collective-permute-done.6.refs_6_.refs_5_), channel_id=1, source_target_pairs={{0,2},{1,7},{2,4},{3,1},{4,6},{5,3},{6,0},{7,5},{8,10},{9,15},{10,... | collective-permute-start | bytes 2359304 | tf_op jit(solution)/shard_map/ppermute | solution.py:47
  52.3 23.3 %collective-permute-start.14 = (bf16[128,3072]{1,0:T(8,128)(2,1)S(1)}, bf16[128,3072]{1,0:T(8,128)(2,1)S(1)}, u32[]{:S(2)}, u32[]{:S(2)}) collective-permute-start(bf16[128,3072]{1,0:T(8,128)(2,1)S(1)} %collective-permute-done.13.refs_8_), channel_id=1, source_target_pairs={{0,48},{1,17},{2,50},{3,19},{4,52},{5,21},{6,54},{7,23},{8,56},{9,... | collective-permute-start | bytes 2359304 | tf_op jit(solution)/shard_map/ppermute | solution.py:47
  52.3 23.7 %collective-permute-start.15 = (bf16[128,3072]{1,0:T(8,128)(2,1)S(1)}, bf16[128,3072]{1,0:T(8,128)(2,1)S(1)}, u32[]{:S(2)}, u32[]{:S(2)}) collective-permute-start(bf16[128,3072]{1,0:T(8,128)(2,1)S(1)} %collective-permute-done.12.refs_6_), channel_id=1, source_target_pairs={{0,64},{1,65},{2,66},{3,67},{4,68},{5,69},{6,70},{7,71},{8,72},{9,... | collective-permute-start | bytes 2359304 | tf_op jit(solution)/shard_map/ppermute | solution.py:47
  55.0 21.4 %collective-permute-start.16 = (bf16[128,3072]{1,0:T(8,128)(2,1)S(1)}, bf16[128,3072]{1,0:T(8,128)(2,1)S(1)}, u32[]{:S(2)}, u32[]{:S(2)}) collective-permute-start(bf16[128,3072]{1,0:T(8,128)(2,1)S(1)} %collective-permute-done.13.refs_8_), channel_id=1, source_target_pairs={{0,16},{1,49},{2,18},{3,51},{4,20},{5,53},{6,22},{7,55},{8,24},{9,... | collective-permute-start | bytes 2359304 | tf_op jit(solution)/shard_map/ppermute | solution.py:47
  57.7 4.2 %copy-start.19 = (bf16[128,3072]{1,0:T(8,128)(2,1)}, bf16[128,3072]{1,0:T(8,128)(2,1)S(1)}, u32[]{:S(2)}) copy-start(bf16[128,3072]{1,0:T(8,128)(2,1)S(1)} %collective-permute-done.9.refs_15_.refs_7_) | copy-start | bytes 2359300
  57.7 15.5 %collective-permute-start.18 = (bf16[128,3072]{1,0:T(8,128)(2,1)S(1)}, bf16[128,3072]{1,0:T(8,128)(2,1)S(1)}, u32[]{:S(2)}, u32[]{:S(2)}) collective-permute-start(bf16[128,3072]{1,0:T(8,128)(2,1)S(1)} %collective-permute-done.9.refs_15_.refs_7_), channel_id=1, source_target_pairs={{0,6},{1,3},{2,0},{3,5},{4,2},{5,7},{6,4},{7,1},{8,14},{9,11},{10,... | collective-permute-start | bytes 2359304 | tf_op jit(solution)/shard_map/ppermute | solution.py:47
  69.4 6.1 %copy-start.7 = (f32[6,2,128,128]{3,2,1,0:T(8,128)}, f32[6,2,128,128]{3,2,1,0:T(8,128)S(1)}, u32[]{:S(2)}) copy-start(f32[6,2,128,128]{3,2,1,0:T(8,128)S(1)} %get-tuple-element.47.refs_0_.refs_3_.refs_6_) | copy-start | bytes 2359300
  77.7 4.5 %collective-permute-start.19 = (f32[8,2,128]{2,0,1:T(8,128)S(1)}, f32[8,2,128]{2,0,1:T(8,128)S(1)}, u32[]{:S(2)}, u32[]{:S(2)}) collective-permute-start(f32[8,2,128]{2,0,1:T(8,128)S(1)} %concatenate.38), channel_id=1, source_target_pairs={{0,8},{1,9},{2,10},{3,11},{4,12},{5,13},{6,14},{7,15},{8,0},{9,1},... | collective-permute-start | bytes 24584 | tf_op jit(solution)/shard_map/ppermute | solution.py:47
  80.3 8.9 %copy-start.37 = (f32[1024,128]{0,1:T(8,128)S(1)}, f32[1024,128]{0,1:T(8,128)}, u32[]{:S(2)}) copy-start(f32[1024,128]{0,1:T(8,128)} %copy-done.36) | copy-start | bytes 1572868
  80.3 16.2 %copy-start.20 = (bf16[128,3072]{1,0:T(8,128)(2,1)S(1)}, bf16[128,3072]{1,0:T(8,128)(2,1)}, u32[]{:S(2)}) copy-start(bf16[128,3072]{1,0:T(8,128)(2,1)} %copy-done.19) | copy-start | bytes 2359300
  82.2 7.2 %copy-start.6 = (bf16[128,3072]{1,0:T(8,128)(2,1)S(1)}, bf16[128,3072]{1,0:T(8,128)(2,1)}, u32[]{:S(2)}) copy-start(bf16[128,3072]{1,0:T(8,128)(2,1)} %refs_2_.3) | copy-start | bytes 2359300
  82.3 4.1 %collective-permute-start.22 = (f32[8,2,128]{2,0,1:T(8,128)S(1)}, f32[8,2,128]{2,0,1:T(8,128)S(1)}, u32[]{:S(2)}, u32[]{:S(2)}) collective-permute-start(f32[8,2,128]{2,0,1:T(8,128)S(1)} %pad_maximum_fusion.3), channel_id=1, source_target_pairs={{0,4},{1,5},{2,6},{3,7},{4,0},{5,1},{6,2},{7,3},{8,12},{9,13},{10,... | collective-permute-start | bytes 24584 | tf_op jit(solution)/shard_map/ppermute | solution.py:47
  82.4 6.7 %collective-permute-start.20 = (f32[9,2,128]{2,0,1:T(8,128)S(1)}, f32[9,2,128]{2,0,1:T(8,128)S(1)}, u32[]{:S(2)}, u32[]{:S(2)}) collective-permute-start(f32[9,2,128]{2,0,1:T(8,128)S(1)} %get-tuple-element.82), channel_id=1, source_target_pairs={{0,6},{1,3},{2,0},{3,5},{4,2},{5,7},{6,4},{7,1},{8,14},{9,11},{10,... | collective-permute-start | bytes 27656 | tf_op jit(solution)/shard_map/ppermute | solution.py:47
  83.2 5.9 %collective-permute-start.21 = (f32[9,2,128]{2,0,1:T(8,128)S(1)}, f32[9,2,128]{2,0,1:T(8,128)S(1)}, u32[]{:S(2)}, u32[]{:S(2)}) collective-permute-start(f32[9,2,128]{2,0,1:T(8,128)S(1)} %get-tuple-element.83), channel_id=1, source_target_pairs={{0,2},{1,7},{2,4},{3,1},{4,6},{5,3},{6,0},{7,5},{8,10},{9,15},{10,... | collective-permute-start | bytes 27656 | tf_op jit(solution)/shard_map/ppermute | solution.py:47
  86.4 17.4 %collective-permute-start.25 = (bf16[128,3072]{1,0:T(8,128)(2,1)S(1)}, bf16[128,3072]{1,0:T(8,128)(2,1)S(1)}, u32[]{:S(2)}, u32[]{:S(2)}) collective-permute-start(bf16[128,3072]{1,0:T(8,128)(2,1)S(1)} %get-tuple-element.52), channel_id=1, source_target_pairs={{0,6},{1,3},{2,0},{3,5},{4,2},{5,7},{6,4},{7,1},{8,14},{9,11},{10,... | collective-permute-start | bytes 2359304 | tf_op jit(solution)/shard_map/ppermute | solution.py:47
  86.4 19.8 %collective-permute-start.24 = (bf16[128,3072]{1,0:T(8,128)(2,1)S(1)}, bf16[128,3072]{1,0:T(8,128)(2,1)S(1)}, u32[]{:S(2)}, u32[]{:S(2)}) collective-permute-start(bf16[128,3072]{1,0:T(8,128)(2,1)S(1)} %get-tuple-element.50), channel_id=1, source_target_pairs={{0,2},{1,7},{2,4},{3,1},{4,6},{5,3},{6,0},{7,5},{8,10},{9,15},{10,... | collective-permute-start | bytes 2359304 | tf_op jit(solution)/shard_map/ppermute | solution.py:47
  89.4 7.1 %copy-start.16 = (bf16[128,3072]{1,0:T(8,128)(2,1)S(1)}, bf16[128,3072]{1,0:T(8,128)(2,1)}, u32[]{:S(2)}) copy-start(bf16[128,3072]{1,0:T(8,128)(2,1)} %copy-done.15) | copy-start | bytes 2359300
  89.4 7.1 %copy-start.18 = (bf16[128,3072]{1,0:T(8,128)(2,1)S(1)}, bf16[128,3072]{1,0:T(8,128)(2,1)}, u32[]{:S(2)}) copy-start(bf16[128,3072]{1,0:T(8,128)(2,1)} %copy-done.17) | copy-start | bytes 2359300
  89.8 6.7 %copy-start.8 = (f32[6,2,128,128]{3,2,1,0:T(8,128)S(1)}, f32[6,2,128,128]{3,2,1,0:T(8,128)}, u32[]{:S(2)}) copy-start(f32[6,2,128,128]{3,2,1,0:T(8,128)} %copy-done.7) | copy-start | bytes 2359300
  89.8 6.7 %copy-start.10 = (bf16[128,3072]{1,0:T(8,128)(2,1)S(1)}, bf16[128,3072]{1,0:T(8,128)(2,1)}, u32[]{:S(2)}) copy-start(bf16[128,3072]{1,0:T(8,128)(2,1)} %copy-done.9) | copy-start | bytes 2359300
  89.8 6.7 %copy-start.12 = (bf16[128,3072]{1,0:T(8,128)(2,1)S(1)}, bf16[128,3072]{1,0:T(8,128)(2,1)}, u32[]{:S(2)}) copy-start(bf16[128,3072]{1,0:T(8,128)(2,1)} %copy-done.11) | copy-start | bytes 2359300
  89.8 6.7 %copy-start.14 = (bf16[128,3072]{1,0:T(8,128)(2,1)S(1)}, bf16[128,3072]{1,0:T(8,128)(2,1)}, u32[]{:S(2)}) copy-start(bf16[128,3072]{1,0:T(8,128)(2,1)} %copy-done.13) | copy-start | bytes 2359300
  90.6 17.5 %collective-permute-start.23 = (bf16[128,3072]{1,0:T(8,128)(2,1)S(1)}, bf16[128,3072]{1,0:T(8,128)(2,1)S(1)}, u32[]{:S(2)}, u32[]{:S(2)}) collective-permute-start(bf16[128,3072]{1,0:T(8,128)(2,1)S(1)} %convolution_convert_fusion.3), channel_id=1, source_target_pairs={{0,48},{1,17},{2,50},{3,19},{4,52},{5,21},{6,54},{7,23},{8,56},{9,... | collective-permute-start | bytes 2359304 | tf_op jit(solution)/shard_map/ppermute | solution.py:47
  90.7 17.9 %collective-permute-start.26 = (bf16[128,3072]{1,0:T(8,128)(2,1)S(1)}, bf16[128,3072]{1,0:T(8,128)(2,1)S(1)}, u32[]{:S(2)}, u32[]{:S(2)}) collective-permute-start(bf16[128,3072]{1,0:T(8,128)(2,1)S(1)} %convolution_convert_fusion.2), channel_id=1, source_target_pairs={{0,64},{1,65},{2,66},{3,67},{4,68},{5,69},{6,70},{7,71},{8,72},{9,... | collective-permute-start | bytes 2359304 | tf_op jit(solution)/shard_map/ppermute | solution.py:47
  93.9 18.0 %collective-permute-start.28 = (bf16[128,3072]{1,0:T(8,128)(2,1)S(1)}, bf16[128,3072]{1,0:T(8,128)(2,1)S(1)}, u32[]{:S(2)}, u32[]{:S(2)}) collective-permute-start(bf16[128,3072]{1,0:T(8,128)(2,1)S(1)} %convolution_convert_fusion.1), channel_id=1, source_target_pairs={{0,16},{1,49},{2,18},{3,51},{4,20},{5,53},{6,22},{7,55},{8,24},{9,... | collective-permute-start | bytes 2359304 | tf_op jit(solution)/shard_map/ppermute | solution.py:47
  96.6 9.6 %copy-start.4 = (bf16[512,3072]{1,0:T(8,128)(2,1)S(1)}, bf16[512,3072]{1,0:T(8,128)(2,1)}, u32[]{:S(2)}) copy-start(bf16[512,3072]{1,0:T(8,128)(2,1)} %copy-done.1) | copy-start | bytes 9437188
  111.9 12.5 %collective-permute-start.29 = (bf16[4,128,3072]{2,1,0:T(8,128)(2,1)S(1)}, bf16[4,128,3072]{2,1,0:T(8,128)(2,1)S(1)}, u32[]{:S(2)}, u32[]{:S(2)}) collective-permute-start(bf16[4,128,3072]{2,1,0:T(8,128)(2,1)S(1)} %shard_map.80), channel_id=1, source_target_pairs={{0,1},{1,0},{2,3},{3,2},{4,5},{5,4},{6,7},{7,6},{8,9},{9,8},{10,11... | collective-permute-start | bytes 9437192 | tf_op jit(solution)/shard_map/ppermute | solution.py:47
  112.8 11.6 %collective-permute-start.27 = (bf16[128,3072]{1,0:T(8,128)(2,1)S(1)}, bf16[128,3072]{1,0:T(8,128)(2,1)S(1)}, u32[]{:S(2)}, u32[]{:S(2)}) collective-permute-start(bf16[128,3072]{1,0:T(8,128)(2,1)S(1)} %add_convert_fusion.1), channel_id=1, source_target_pairs={{0,16},{1,49},{2,18},{3,51},{4,20},{5,53},{6,22},{7,55},{8,24},{9,... | collective-permute-start | bytes 2359304 | tf_op jit(solution)/shard_map/ppermute | solution.py:47
  115.5 18.9 %collective-permute-start.31 = (bf16[128,3072]{1,0:T(8,128)(2,1)S(1)}, bf16[128,3072]{1,0:T(8,128)(2,1)S(1)}, u32[]{:S(2)}, u32[]{:S(2)}) collective-permute-start(bf16[128,3072]{1,0:T(8,128)(2,1)S(1)} %get-tuple-element.54), channel_id=1, source_target_pairs={{0,2},{1,7},{2,4},{3,1},{4,6},{5,3},{6,0},{7,5},{8,10},{9,15},{10,... | collective-permute-start | bytes 2359304 | tf_op jit(solution)/shard_map/ppermute | solution.py:47
  116.7 17.7 %collective-permute-start.32 = (bf16[128,3072]{1,0:T(8,128)(2,1)S(1)}, bf16[128,3072]{1,0:T(8,128)(2,1)S(1)}, u32[]{:S(2)}, u32[]{:S(2)}) collective-permute-start(bf16[128,3072]{1,0:T(8,128)(2,1)S(1)} %get-tuple-element.60), channel_id=1, source_target_pairs={{0,6},{1,3},{2,0},{3,5},{4,2},{5,7},{6,4},{7,1},{8,14},{9,11},{10,... | collective-permute-start | bytes 2359304 | tf_op jit(solution)/shard_map/ppermute | solution.py:47
  117.0 12.4 %copy-start.31 = (bf16[128,3072]{1,0:T(8,128)(2,1)S(1)}, bf16[128,3072]{1,0:T(8,128)(2,1)}, u32[]{:S(2)}) copy-start(bf16[128,3072]{1,0:T(8,128)(2,1)} %copy-done.30) | copy-start | bytes 2359300
  117.0 12.4 %copy-start.33 = (bf16[128,3072]{1,0:T(8,128)(2,1)S(1)}, bf16[128,3072]{1,0:T(8,128)(2,1)}, u32[]{:S(2)}) copy-start(bf16[128,3072]{1,0:T(8,128)(2,1)} %copy-done.32) | copy-start | bytes 2359300
  117.0 12.4 %copy-start.35 = (bf16[128,3072]{1,0:T(8,128)(2,1)S(1)}, bf16[128,3072]{1,0:T(8,128)(2,1)}, u32[]{:S(2)}) copy-start(bf16[128,3072]{1,0:T(8,128)(2,1)} %copy-done.34) | copy-start | bytes 2359300
  117.5 23.2 %collective-permute-start.34 = (bf16[128,3072]{1,0:T(8,128)(2,1)S(1)}, bf16[128,3072]{1,0:T(8,128)(2,1)S(1)}, u32[]{:S(2)}, u32[]{:S(2)}) collective-permute-start(bf16[128,3072]{1,0:T(8,128)(2,1)S(1)} %add_convert_fusion), channel_id=1, source_target_pairs={{0,64},{1,65},{2,66},{3,67},{4,68},{5,69},{6,70},{7,71},{8,72},{9,... | collective-permute-start | bytes 2359304 | tf_op jit(solution)/shard_map/ppermute | solution.py:47
  124.4 4.9 %copy-start.27 = (bf16[128,3072]{1,0:T(8,128)(2,1)S(1)}, bf16[128,3072]{1,0:T(8,128)(2,1)}, u32[]{:S(2)}) copy-start(bf16[128,3072]{1,0:T(8,128)(2,1)} %copy-done.26) | copy-start | bytes 2359300
  124.4 4.9 %copy-start.29 = (bf16[128,3072]{1,0:T(8,128)(2,1)S(1)}, bf16[128,3072]{1,0:T(8,128)(2,1)}, u32[]{:S(2)}) copy-start(bf16[128,3072]{1,0:T(8,128)(2,1)} %copy-done.28) | copy-start | bytes 2359300
  124.8 4.5 %copy-start.21 = (bf16[128,3072]{1,0:T(8,128)(2,1)S(1)}, bf16[128,3072]{1,0:T(8,128)(2,1)}, u32[]{:S(2)}) copy-start(bf16[128,3072]{1,0:T(8,128)(2,1)} %refs_4_.1) | copy-start | bytes 2359300
  124.8 4.5 %copy-start.23 = (bf16[128,3072]{1,0:T(8,128)(2,1)S(1)}, bf16[128,3072]{1,0:T(8,128)(2,1)}, u32[]{:S(2)}) copy-start(bf16[128,3072]{1,0:T(8,128)(2,1)} %copy-done.22) | copy-start | bytes 2359300
  124.9 4.5 %copy-start.25 = (bf16[128,3072]{1,0:T(8,128)(2,1)S(1)}, bf16[128,3072]{1,0:T(8,128)(2,1)}, u32[]{:S(2)}) copy-start(bf16[128,3072]{1,0:T(8,128)(2,1)} %copy-done.24) | copy-start | bytes 2359300
  124.9 17.5 %collective-permute-start.30 = (bf16[128,3072]{1,0:T(8,128)(2,1)S(1)}, bf16[128,3072]{1,0:T(8,128)(2,1)S(1)}, u32[]{:S(2)}, u32[]{:S(2)}) collective-permute-start(bf16[128,3072]{1,0:T(8,128)(2,1)S(1)} %convolution_convert_fusion), channel_id=1, source_target_pairs={{0,48},{1,17},{2,50},{3,19},{4,52},{5,21},{6,54},{7,23},{8,56},{9,... | collective-permute-start | bytes 2359304 | tf_op jit(solution)/shard_map/ppermute | solution.py:47
  125.3 23.1 %collective-permute-start.37 = (bf16[128,3072]{1,0:T(8,128)(2,1)S(1)}, bf16[128,3072]{1,0:T(8,128)(2,1)S(1)}, u32[]{:S(2)}, u32[]{:S(2)}) collective-permute-start(bf16[128,3072]{1,0:T(8,128)(2,1)S(1)} %fusion), channel_id=1, source_target_pairs={{0,16},{1,49},{2,18},{3,51},{4,20},{5,53},{6,22},{7,55},{8,24},{9,... | collective-permute-start | bytes 2359304 | tf_op jit(solution)/shard_map/ppermute | solution.py:47
  137.0 18.5 %collective-permute-start.33 = (bf16[128,3072]{1,0:T(8,128)(2,1)S(1)}, bf16[128,3072]{1,0:T(8,128)(2,1)S(1)}, u32[]{:S(2)}, u32[]{:S(2)}) collective-permute-start(bf16[128,3072]{1,0:T(8,128)(2,1)S(1)} %get-tuple-element.62), channel_id=1, source_target_pairs={{0,2},{1,7},{2,4},{3,1},{4,6},{5,3},{6,0},{7,5},{8,10},{9,15},{10,... | collective-permute-start | bytes 2359304 | tf_op jit(solution)/shard_map/ppermute | solution.py:47
  140.0 16.7 %collective-permute-start.36 = (bf16[128,3072]{1,0:T(8,128)(2,1)S(1)}, bf16[128,3072]{1,0:T(8,128)(2,1)S(1)}, u32[]{:S(2)}, u32[]{:S(2)}) collective-permute-start(bf16[128,3072]{1,0:T(8,128)(2,1)S(1)} %get-tuple-element.65), channel_id=1, source_target_pairs={{0,8},{1,9},{2,10},{3,11},{4,12},{5,13},{6,14},{7,15},{8,0},{9,1},... | collective-permute-start | bytes 2359304 | tf_op jit(solution)/shard_map/ppermute | solution.py:47
  140.6 17.7 %collective-permute-start.35 = (bf16[128,3072]{1,0:T(8,128)(2,1)S(1)}, bf16[128,3072]{1,0:T(8,128)(2,1)S(1)}, u32[]{:S(2)}, u32[]{:S(2)}) collective-permute-start(bf16[128,3072]{1,0:T(8,128)(2,1)S(1)} %get-tuple-element.64), channel_id=1, source_target_pairs={{0,6},{1,3},{2,0},{3,5},{4,2},{5,7},{6,4},{7,1},{8,14},{9,11},{10,... | collective-permute-start | bytes 2359304 | tf_op jit(solution)/shard_map/ppermute | solution.py:47
  (12 other events, 16.8 us)
